TPU v7x, 32 devices: a whole 2x2x4 slice. The times are simulated.
32 devices in a mesh: groups: 2 (over x), docs: 8 (over z, y), tensor: 2 (over core).
Axes of the slice: x: 2, y: 2, z: 4, core: 2. Of those that a mesh axis runs over, the one named last changes fastest.
Arguments:
- sample_act: bfloat16 [128, 32, 11008], P(('groups', 'docs'), None, 'tensor'), parts along dimension 0, may hold values from -6 to 6
- sample_grad: bfloat16 [128, 32, 4096], P(('groups', 'docs'), None, 'tensor'), parts along dimension 0, may hold values from -6 to 6
- doc_act: bfloat16 [16, 768, 11008], P(('groups', 'docs'), None, 'tensor'), parts along dimension 0, may hold values from -6 to 6
- doc_grad: bfloat16 [16, 768, 4096], P(('groups', 'docs'), None, 'tensor'), parts along dimension 0, may hold values from -6 to 6
- pair_doc: int32 [256, 1], P(('groups', 'docs')), parts along dimension 0, may hold values from 0 to 7; in each aligned block of 16 rows (0 to 15, 16 to 31, ...) at most 2 rows name the same one
- pair_sample: int32 [256], P(('groups', 'docs')), parts along dimension 0, may hold values from 0 to 7
Outputs:
- influence: float32 [256], P(('groups', 'docs')), parts along dimension 0
There are 2 independent parts, one for each index of `groups`. A program takes and returns all parts, laid end to end along the dimension named above; each array names one. Nothing has to cross between parts.
Inputs may be any that keep to these rules, and one draw needn't show every extreme that they name: `pair_doc`: among the 16 pairs listed by one index of docs, no document is named more than 2 times, a bound that some block reaches; document d is owned by index d of docs. The sample of pair p is sample (p // 16) * 8 + pair_sample[p].
All inputs are finite; a program needn't handle non-finite values.
Results may differ from a plain program's by a relative error of at most 0.0003.
Values may be sent and summed in bfloat16 or wider, within the bound.
No kernel may reach another device: no remote copies, remote signals or barrier semaphores. Data moves between devices by JAX's collectives and lax.ppermute only.
A program may use at most 128 MiB of HBM per device.

v0:
```python
import jax
import jax.numpy as jnp
from jax import lax
from jax.sharding import PartitionSpec as P

FF = 11008
D = 4096
SEQ_S = 32
SEQ_D = 768
CAP = 2


def per_device(sample_act, sample_grad, doc_act, doc_grad, pair_doc, pair_sample):
    owners = lax.axis_size("docs")
    pair_count = pair_doc.shape[0]
    slot_count = owners * CAP
    factor = 1.0 / jnp.sqrt(
        jnp.float32(FF) * jnp.float32(D) * jnp.float32(SEQ_S) * jnp.float32(SEQ_D)
    )
    target = pair_doc[:, 0]
    order = jnp.arange(pair_count, dtype=jnp.int32)
    earlier = (target[:, None] == target[None, :]) & (order[None, :] < order[:, None])
    rank = jnp.sum(earlier.astype(jnp.int32), axis=1)
    slot_of_pair = target * CAP + rank
    chosen = (jnp.arange(slot_count, dtype=jnp.int32)[:, None] == slot_of_pair[None, :]).astype(
        jnp.int32
    )
    slot_sample = jnp.sum(chosen * pair_sample[None, :], axis=1)
    live = jnp.sum(chosen, axis=1) > 0
    send_act = jnp.where(live[:, None, None], sample_act[slot_sample], jnp.zeros((), jnp.bfloat16))
    send_grad = jnp.where(
        live[:, None, None], sample_grad[slot_sample], jnp.zeros((), jnp.bfloat16)
    )
    send_act = send_act.reshape(owners, CAP, send_act.shape[1], send_act.shape[2])
    send_grad = send_grad.reshape(owners, CAP, send_grad.shape[1], send_grad.shape[2])
    doc_rows = doc_act[0]
    doc_grows = doc_grad[0]
    act_in = lax.all_to_all(send_act, "docs", split_axis=0, concat_axis=0, tiled=True)
    grad_in = lax.all_to_all(send_grad, "docs", split_axis=0, concat_axis=0, tiled=True)
    act_gram = jnp.einsum("nmsf,tf->nmst", act_in, doc_rows, preferred_element_type=jnp.float32)
    grad_gram = jnp.einsum("nmsf,tf->nmst", grad_in, doc_grows, preferred_element_type=jnp.float32)
    act_sum, grad_sum = lax.psum((act_gram, grad_gram), "tensor")
    scores = jnp.sum(act_sum * grad_sum, axis=(2, 3)) * factor
    returned = lax.all_to_all(scores, "docs", split_axis=0, concat_axis=0, tiled=True)
    flat_scores = returned.reshape(slot_count)
    return jnp.sum(chosen.astype(jnp.float32) * flat_scores[:, None], axis=0)


def solution(mesh):
    in_specs = (
        P(("groups", "docs"), None, "tensor"),
        P(("groups", "docs"), None, "tensor"),
        P(("groups", "docs"), None, "tensor"),
        P(("groups", "docs"), None, "tensor"),
        P(("groups", "docs"), None),
        P(("groups", "docs")),
    )
    out_specs = P(("groups", "docs"))
    return jax.shard_map(
        per_device, mesh=mesh, in_specs=in_specs, out_specs=out_specs, check_vma=False
    )
```

profile of v0, /device:TPU:0, one launch (start us, length us, event | category | flops | bytes accessed | tf_op | source)
XLA Modules:
  0.0 255.3 jit_solution(16624626151330442813)
XLA Ops:
  6.5 0.0 copy-start
  6.5 1.0 convert_reduce_fusion.1
  7.5 0.7 multiply_add_fusion
  8.2 0.8 convert_reduce_fusion
  9.0 0.1 gt.11
  9.1 3.3 %gather_fusion.1 = bf16[16,32,2048]{2,1,0:T(8,128)(2,1)} fusion(bf16[8,32,2048]{2,1,0:T(8,128)(2,1)} %param.7, s32[1024]{0:T(1024)S(1)} %pad_clamp_fusion), kind=kCustom, calls=%fused_computation.1 | custom fusion | bytes 4194368 | tf_op jit(solution)/shard_map/gather | solution.py:32
  12.4 3.1 %broadcast_select_fusion.1 = bf16[8,2,32,2048]{3,2,1,0:T(8,128)(2,1)} fusion(bf16[8,2,32,2048]{3,2,1,0:T(8,128)(2,1)} %bitcast.28, pred[8,2]{1,0:T(8,128)(4,1)S(1)} %gt.11), kind=kLoop, calls=%fused_computation.7 | loop fusion | flops 1048576 | bytes 4194320 | tf_op jit(solution)/shard_map/jit(_where)/select_n | solution.py:31
  15.4 7.3 %all-to-all-start.1 = ((bf16[8,2,32,2048]{3,2,1,0:T(8,128)(2,1)}), bf16[8,2,32,2048]{3,2,1,0:T(8,128)(2,1)}, u32[]{:S(2)}, u32[]{:S(2)}) async-start(bf16[8,2,32,2048]{3,2,1,0:T(8,128)(2,1)} %broadcast_select_fusion.1), calls=%async_computation.1 | async-start | bytes 4194304 | tf_op jit(solution)/shard_map/all_to_all | solution.py:39
  22.7 5.4 %gather_fusion = bf16[16,32,5504]{2,1,0:T(8,128)(2,1)} fusion(bf16[8,32,5504]{2,1,0:T(8,128)(2,1)} %param.6, s32[1024]{0:T(1024)S(1)} %pad_clamp_fusion), kind=kCustom, calls=%fused_computation | custom fusion | bytes 11272256 | tf_op jit(solution)/shard_map/gather | solution.py:30
  28.1 5.6 %broadcast_select_fusion = bf16[8,2,32,5504]{3,2,1,0:T(8,128)(2,1)} fusion(bf16[8,2,32,5504]{3,2,1,0:T(8,128)(2,1)} %bitcast.27, pred[8,2]{1,0:T(8,128)(4,1)S(1)} %gt.11), kind=kLoop, calls=%fused_computation.4 | loop fusion | flops 2818048 | bytes 11272208 | tf_op jit(solution)/shard_map/jit(_where)/select_n | solution.py:30
  33.7 37.4 %all-to-all-done.1 = bf16[8,2,32,2048]{3,2,1,0:T(8,128)(2,1)} async-done(((bf16[8,2,32,2048]{3,2,1,0:T(8,128)(2,1)}), bf16[8,2,32,2048]{3,2,1,0:T(8,128)(2,1)}, u32[]{:S(2)}, u32[]{:S(2)}) %all-to-all-start.1) | async-done | bytes 2097184 | tf_op jit(solution)/shard_map/all_to_all | solution.py:39
  71.1 4.7 %all-to-all-start = ((bf16[8,2,32,5504]{3,2,1,0:T(8,128)(2,1)}), bf16[8,2,32,5504]{3,2,1,0:T(8,128)(2,1)}, u32[]{:S(2)}, u32[]{:S(2)}) async-start(bf16[8,2,32,5504]{3,2,1,0:T(8,128)(2,1)} %broadcast_select_fusion), calls=%async_computation | async-start | bytes 11272192 | tf_op jit(solution)/shard_map/all_to_all | solution.py:38
  75.8 0.0 all-reduce.3.cloned.1.call-start
  75.8 0.0 copy-done
  75.8 4.6 %fusion.2 = f32[8,2,32,768]{3,2,1,0:T(8,128)} fusion(bf16[8,2,32,2048]{3,2,1,0:T(8,128)(2,1)} %all-to-all-done.1, bf16[1,768,2048]{2,1,0:T(8,128)(2,1)S(1)} %copy-done), kind=kOutput, calls=%fused_computation.5 | convolution fusion | flops 1610612736 | bytes 6815744 | tf_op jit(solution)/shard_map/nmsf,tf->nmst/dot_general | solution.py:41
  80.4 118.7 %all-to-all-done = bf16[8,2,32,5504]{3,2,1,0:T(8,128)(2,1)} async-done(((bf16[8,2,32,5504]{3,2,1,0:T(8,128)(2,1)}), bf16[8,2,32,5504]{3,2,1,0:T(8,128)(2,1)}, u32[]{:S(2)}, u32[]{:S(2)}) %all-to-all-start) | async-done | bytes 5636128 | tf_op jit(solution)/shard_map/all_to_all | solution.py:38
  199.1 10.9 %fusion = f32[8,2,32,768]{3,2,1,0:T(8,128)} fusion(bf16[8,2,32,5504]{3,2,1,0:T(8,128)(2,1)} %all-to-all-done, bf16[1,768,5504]{2,1,0:T(8,128)(2,1)} %param.8), kind=kOutput, calls=%fused_computation.2 | convolution fusion | flops 4328521728 | bytes 15663104 | tf_op jit(solution)/shard_map/nmsf,tf->nmst/dot_general | solution.py:40
  210.0 0.0 all-reduce.3.cloned.1.call-update
  210.0 22.5 %all-reduce.3.cloned.1.call-done = (f32[8,2,32,768]{3,2,1,0:T(8,128)}, f32[8,2,32,768]{3,2,1,0:T(8,128)}) async-done(((f32[8,2,32,768]{3,2,1,0:T(8,128)}, f32[8,2,32,768]{3,2,1,0:T(8,128)}), (f32[8,2,32,768]{3,2,1,0:T(8,128)}, f32[8,2,32,768]{3,2,1,0:T(8,128)})) %all-reduce.3.cloned.1.call-update) | async-done | bytes 3145744 | tf_op jit(solution)/shard_map/psum | solution.py:42
  232.4 2.1 multiply_reduce_fusion
  234.6 12.0 %all_to_all.16 = f32[8,1,2]{2,1,0:T(1,128)S(1)} all-to-all(f32[8,1,2]{2,1,0:T(1,128)S(1)} %bitcast.29), channel_id=1, replica_groups=mesh['groups'=2,'docs'=8,'tensor'=2] {'docs'}, dimensions={0} | all-to-all | bytes 128 | tf_op jit(solution)/shard_map/all_to_all | solution.py:44
  246.6 0.5 broadcast.76
  247.1 0.7 reduce.3
  247.8 0.1 mul.47
  247.9 0.6 fusion.5
  (4 shorter events, 0.0 us)
Async XLA Ops:
  6.5 69.3 %copy-start = (bf16[1,768,2048]{2,1,0:T(8,128)(2,1)S(1)}, bf16[1,768,2048]{2,1,0:T(8,128)(2,1)}, u32[]{:S(2)}) copy-start(bf16[1,768,2048]{2,1,0:T(8,128)(2,1)} %param.9) | copy-start | bytes 9437188
  15.4 55.6 %all-to-all-start.1 = ((bf16[8,2,32,2048]{3,2,1,0:T(8,128)(2,1)}), bf16[8,2,32,2048]{3,2,1,0:T(8,128)(2,1)}, u32[]{:S(2)}, u32[]{:S(2)}) async-start(bf16[8,2,32,2048]{3,2,1,0:T(8,128)(2,1)} %broadcast_select_fusion.1), calls=%async_computation.1 | async-start | bytes 4194304 | tf_op jit(solution)/shard_map/all_to_all | solution.py:39
  71.1 128.0 %all-to-all-start = ((bf16[8,2,32,5504]{3,2,1,0:T(8,128)(2,1)}), bf16[8,2,32,5504]{3,2,1,0:T(8,128)(2,1)}, u32[]{:S(2)}, u32[]{:S(2)}) async-start(bf16[8,2,32,5504]{3,2,1,0:T(8,128)(2,1)} %broadcast_select_fusion), calls=%async_computation | async-start | bytes 11272192 | tf_op jit(solution)/shard_map/all_to_all | solution.py:38
  75.8 156.7 %all-reduce.3.cloned.1.call-start = ((), (), s32[]{:S(2)}) async-start(), calls=%async_computation.3 | async-start | bytes 6291456 | tf_op jit(solution)/shard_map/psum | solution.py:42
Sparse Core Ops, SparseCore 0:
  210.1 22.2 all-reduce.2
where the time goes:
time: 256 us; the launch traced here: 255 us
  waiting for transfers between devices  179 us (70%)
  matrix products  15.4 us (6%)
  other arithmetic  14.5 us (6%)
  between operations  13.4 us (5%)
  starting transfers between devices  12 us (5%)
  blocking collectives  12 us (5%)
  local copies, waits for them, and re-layouts  9.32 us (4%)
    all_to_all x1, waiting for transfers between devices, per_device(): lax.all_to_all(send_act, 'docs', split_axis=0, concat_axis=0, tiled=True)  119 us
    all_to_all x1, waiting for transfers between devices, per_device(): lax.all_to_all(send_grad, 'docs', split_axis=0, concat_axis=0, tiled=True)  37.4 us
    psum x1, waiting for transfers between devices, per_device(): act_sum, grad_sum = lax.psum((act_gram, grad_gram), 'tensor')  22.5 us
    all_to_all x1, blocking collectives, per_device(): lax.all_to_all(scores, 'docs', split_axis=0, concat_axis=0, tiled=True)  12 us
    dot_general x1, matrix products, per_device(): jnp.einsum('nmsf,tf->nmst', act_in, doc_rows, preferred_element_type=jnp....  10.9 us
    all_to_all x1, starting transfers between devices, per_device(): lax.all_to_all(send_grad, 'docs', split_axis=0, concat_axis=0, tiled=True)  7.28 us
    select_n x1, other arithmetic, per_device(): jnp.where(live[:, None, None], sample_act[slot_sample], jnp.zeros((), jnp...  5.58 us
    gather x1, local copies, waits for them, and re-layouts, per_device(): sample_act[slot_sample]  5.38 us
  transfers between devices with their start and end apart: 3, of which 3 were waited for; matrix products, arithmetic and copies ran while one was open for 6% of the time, Pallas kernels for 0%

commit v1 on v0

v1 whole, which is shorter than its diff:
```python
import functools

import jax
import jax.numpy as jnp
from jax import lax
from jax.experimental import pallas as pl
from jax.experimental.pallas import tpu as pltpu
from jax.sharding import PartitionSpec as P

FF = 11008
D = 4096
SEQ_S = 32
SEQ_D = 768
CAP = 2

ANY = pl.BlockSpec(memory_space=pl.ANY)
SMEM = pl.BlockSpec(memory_space=pltpu.SMEM)
VMEM = pl.BlockSpec(memory_space=pltpu.VMEM)

OUTER = (0, 1, 6, 7)
INNER = (2, 3, 4, 5)
TO_INNER = [(i, i ^ 2) for i in OUTER]
ACROSS = [(i, i ^ 6) for i in INNER]
TO_OUTER = [(i, i ^ 2) for i in INNER]
TO_DIAG = [(i, i ^ 3) for i in INNER]
OVER_Y = [(i, i ^ 1) for i in range(8)]
OVER_Y_INNER = [(i, i ^ 1) for i in INNER]

OWN = 4
COUNTS = (12, 13, 14, 16)

LIST, STRAIGHT, DIAG, SIDE, SLOTS, BRANCH, CODES = 0, 16, 20, 24, 32, 48, 64


def is_inner(me):
    return ((me >> 1) ^ (me >> 2)) & 1


def bits(mask):
    total = mask & 1
    for i in range(1, 8):
        total = total + ((mask >> i) & 1)
    return total


def cost(nbytes, flops=0):
    return pl.CostEstimate(flops=flops, bytes_accessed=nbytes, transcendentals=0)


def start_kernel(me_ref, doc_ref, sample_ref, grad_ref, tab_ref, place_ref, across_ref, straight_ref,
                 diag_ref, side_ref, next_ref, seen, own, sems, *, off):
    me = me_ref[0]
    owners = 8
    for d in range(owners):
        seen[d] = 0
    for i in range(owners * CAP):
        tab_ref[i] = 0
    mask = jnp.int32(0)
    half = me >> 2
    for p in range(owners * CAP):
        doc = doc_ref[p, 0]
        slot = doc * CAP + jnp.minimum(seen[doc], CAP - 1)
        seen[doc] = seen[doc] + 1
        place_ref[p] = slot
        tab_ref[slot] = sample_ref[p]
        bit = jnp.left_shift(1, sample_ref[p])
        mask = jnp.where((doc >> 2) != half, mask | bit, mask)
    for k in range(8):
        own[k] = 0
    count = jnp.int32(0)
    for s in range(8):
        hit = (mask >> s) & 1
        own[jnp.where(hit == 1, count, 8)] = s
        count = count + hit
    width = next_ref.shape[2]
    copies = []

    def go(src, dst):
        c = pltpu.make_async_copy(src, dst, sems.at[len(copies)])
        c.start()
        copies.append(c)

    for k in range(OWN):
        go(grad_ref.at[own[k]], across_ref.at[k])
    for r in range(CAP):
        go(grad_ref.at[tab_ref[(me ^ 2) * CAP + r]], straight_ref.at[r])
        go(grad_ref.at[tab_ref[(me ^ 3) * CAP + r]], diag_ref.at[r])
        go(grad_ref.at[tab_ref[(me ^ 1) * CAP + r]], side_ref.at[r])
    for s in range(8):
        go(grad_ref.at[s, :, pl.ds(off, width)], next_ref.at[s])
    for c in copies:
        c.wait()


def start_call(me, pair_doc, pair_sample, grad, off):
    n, rows, width = grad.shape
    def buf(k, w):
        return jax.ShapeDtypeStruct((k, rows, w), grad.dtype)
    table = jax.ShapeDtypeStruct((8 * CAP,), jnp.int32)
    return pl.pallas_call(
        functools.partial(start_kernel, off=off),
        out_shape=(table, table, buf(OWN, width), buf(CAP, width), buf(CAP, width), buf(CAP, width),
                   buf(n, width - off)),
        in_specs=[SMEM, SMEM, SMEM, ANY],
        out_specs=(SMEM, SMEM, ANY, ANY, ANY, ANY, ANY),
        scratch_shapes=[pltpu.SMEM((8,), jnp.int32), pltpu.SMEM((16,), jnp.int32),
                        pltpu.SemaphoreType.DMA((OWN + 3 * CAP + n,))],
        cost_estimate=cost(6_000_000),
    )(me, pair_doc, pair_sample, grad)


def own_kernel(me_ref, tab_ref, act_ref, token_ref, straight_ref, diag_ref, side_ref, sems):
    me = me_ref[0]
    copies = []
    for r in range(CAP):
        for turn, dst in ((2, straight_ref), (3, diag_ref), (1, side_ref)):
            c = pltpu.make_async_copy(
                act_ref.at[tab_ref[(me ^ turn) * CAP + r]], dst.at[r], sems.at[len(copies)]
            )
            c.start()
            copies.append(c)
    for c in copies:
        c.wait()


def own_call(me, tab, act, token):
    buf = jax.ShapeDtypeStruct((CAP,) + act.shape[1:], act.dtype)
    return pl.pallas_call(
        own_kernel,
        out_shape=(buf,) * 3,
        in_specs=[SMEM, SMEM, ANY, ANY],
        out_specs=(ANY,) * 3,
        scratch_shapes=[pltpu.SemaphoreType.DMA((3 * CAP,))],
        cost_estimate=cost(4_000_000),
    )(me, tab, act, token)


def codes_kernel(me_ref, all_ref, out_ref, scratch, masks, *, groups):
    group, me = me_ref[1], me_ref[0]
    base = group * 8

    def owner_mask(row, _):
        first = jnp.where((row & 7) < 4, 8, 0)
        mask = jnp.int32(0)
        for j in range(8):
            mask = mask | jnp.left_shift(1, all_ref[row, first + j])
        masks[row] = mask
        return 0

    lax.fori_loop(0, groups * 8, owner_mask, 0)

    def longest(k, best):
        row = (k >> 2) * 8 + 2 + (k & 3)
        return jnp.maximum(best, jnp.maximum(bits(masks[row]), OWN) + bits(masks[row ^ 2]))

    best = lax.fori_loop(0, groups * 4, longest, jnp.int32(0))
    branch = jnp.int32(0)
    for c in COUNTS[:-1]:
        branch = branch + (best > c).astype(jnp.int32)
    for i in range(CODES):
        out_ref[i] = 0
    for i in range(32):
        scratch[i] = 0
    out_ref[BRANCH] = branch
    inner = is_inner(me)
    mine, partner = masks[base + me], masks[base + (me ^ 2)]
    count = jnp.int32(0)
    for s in range(8):
        hit = (mine >> s) & 1
        scratch[jnp.where(hit == 1, count, 31)] = s
        count = count + hit
    count = jnp.maximum(count, OWN)
    for s in range(8):
        hit = (partner >> s) & 1
        scratch[jnp.where(hit == 1, count, 31)] = 8 + s
        count = count + hit
    for k in range(16):
        out_ref[LIST + k] = scratch[k]
    far, far_outer = masks[base + (me ^ 6)], masks[base + (me ^ 4)]
    after = jnp.maximum(bits(far), OWN)

    def place(near, doc, r):
        owner = base + ((me ^ 6) if near else (me ^ 4))
        sample = all_ref[owner, doc * CAP + r]
        below = jnp.left_shift(1, sample) - 1
        return (bits(far & below) if near else after + bits(far_outer & below)) * inner

    for r in range(CAP):
        out_ref[STRAIGHT + r] = place(True, me ^ 2, r)
        out_ref[STRAIGHT + CAP + r] = place(False, me ^ 2, r)
        out_ref[DIAG + r] = place(True, me ^ 3, r)
        out_ref[DIAG + CAP + r] = place(False, me ^ 3, r)
        out_ref[SIDE + r] = all_ref[base + (me ^ 2), (me ^ 1) * CAP + r]
        out_ref[SIDE + CAP + r] = place(True, me ^ 1, r)
        out_ref[SIDE + 2 * CAP + r] = place(False, me ^ 1, r)
        out_ref[SLOTS + r] = all_ref[base + me, me * CAP + r]
        out_ref[SLOTS + CAP + r] = all_ref[base + (me ^ 2), me * CAP + r]
        out_ref[SLOTS + 2 * CAP + r] = place(True, me, r)
        out_ref[SLOTS + 3 * CAP + r] = place(False, me, r)


def codes_call(me, tables, groups):
    return pl.pallas_call(
        functools.partial(codes_kernel, groups=groups),
        out_shape=jax.ShapeDtypeStruct((CODES,), jnp.int32),
        in_specs=[SMEM, SMEM],
        out_specs=SMEM,
        scratch_shapes=[pltpu.SMEM((32,), jnp.int32), pltpu.SMEM((groups * 8,), jnp.int32)],
        cost_estimate=cost(4096),
    )(me, tables)


def mix_kernel(codes_ref, own_ref, came_ref, *rest, first, off, ahead):
    if ahead is None:
        token_ref, list_ref, sems = rest
    else:
        token_ref, ahead_ref, list_ref, next_ref, sems = rest
    count, _, width = list_ref.shape
    for k in range(count):
        code = codes_ref[LIST + first + k]

        @pl.when(code < 8)
        def _():
            pltpu.make_async_copy(
                own_ref.at[code, :, pl.ds(off, width)], list_ref.at[k], sems.at[k]
            ).start()

        @pl.when(code >= 8)
        def _():
            pltpu.make_async_copy(came_ref.at[code - 8], list_ref.at[k], sems.at[k]).start()

    copies = []
    if ahead is not None:
        for s in range(8):
            c = pltpu.make_async_copy(
                ahead_ref.at[s, :, pl.ds(ahead, next_ref.shape[2])], next_ref.at[s], sems.at[count + s]
            )
            c.start()
            copies.append(c)
    for k in range(count):
        pltpu.make_async_copy(came_ref.at[0], list_ref.at[k], sems.at[k]).wait()
    for c in copies:
        c.wait()


def mix_call(codes, own, came, count, first, off, token, ahead_array, ahead, ahead_width):
    n, rows, width = came.shape
    out = [jax.ShapeDtypeStruct((count, rows, width), own.dtype)]
    args = [codes, own, came, token]
    if ahead is not None:
        out.append(jax.ShapeDtypeStruct((n, rows, ahead_width), own.dtype))
        args.append(ahead_array)
    return pl.pallas_call(
        functools.partial(mix_kernel, first=first, off=off, ahead=ahead),
        out_shape=tuple(out),
        in_specs=[SMEM] + [ANY] * (len(args) - 1),
        out_specs=(ANY,) * len(out),
        scratch_shapes=[pltpu.SemaphoreType.DMA((count + n,))],
        cost_estimate=cost(4_000_000),
    )(*args)


def fetch(code, early_ref, late_ref, off, dst, sem):
    width = dst.shape[1]
    if early_ref is None:
        pltpu.make_async_copy(late_ref.at[code], dst, sem).start()
        return

    @pl.when(code < OWN)
    def _():
        pltpu.make_async_copy(early_ref.at[code, :, pl.ds(off, width)], dst, sem).start()

    @pl.when(code >= OWN)
    def _():
        pltpu.make_async_copy(late_ref.at[code - OWN], dst, sem).start()


def forward_kernel(codes_ref, came_ref, *rest, split, off):
    if split:
        early_ref, late_ref, token_ref, straight_ref, diag_ref, side_ref, sems = rest
    else:
        late_ref, token_ref, straight_ref, diag_ref, side_ref, sems = rest
        early_ref = None
    waits = []
    for k in range(2 * CAP):
        for at, dst in ((STRAIGHT, straight_ref), (DIAG, diag_ref)):
            fetch(codes_ref[at + k], early_ref, late_ref, off, dst.at[k], sems.at[len(waits)])
            waits.append(dst.at[k])
    for k in range(CAP):
        pltpu.make_async_copy(came_ref.at[codes_ref[SIDE + k]], side_ref.at[k], sems.at[len(waits)]).start()
        waits.append(side_ref.at[k])
    for k in range(CAP, 3 * CAP):
        fetch(codes_ref[SIDE + k], early_ref, late_ref, off, side_ref.at[k], sems.at[len(waits)])
        waits.append(side_ref.at[k])
    for i, dst in enumerate(waits):
        pltpu.make_async_copy(came_ref.at[0], dst, sems.at[i]).wait()


def forward_call(codes, came, early, late, off, token):
    n, rows, width = came.shape

    def buf(k):
        return jax.ShapeDtypeStruct((k, rows, width), came.dtype)

    args = [codes, came] + ([] if early is None else [early]) + [late, token]
    return pl.pallas_call(
        functools.partial(forward_kernel, split=early is not None, off=off),
        out_shape=(buf(2 * CAP), buf(2 * CAP), buf(3 * CAP)),
        in_specs=[SMEM] + [ANY] * (len(args) - 1),
        out_specs=(ANY,) * 3,
        scratch_shapes=[pltpu.SemaphoreType.DMA((7 * CAP,))],
        cost_estimate=cost(4_000_000),
    )(*args)


def gram_kernel(me_ref, codes_ref, own_ref, came_ref, *rest, split, off, mode, last):
    rest = list(rest)
    early_ref = rest.pop(0) if split else None
    (late_ref, own_straight_ref, own_diag_ref, own_side_ref, straight_ref, diag_ref, side_ref, doc_ref,
     token_ref) = rest[:9]
    rest = rest[9:]
    held = [rest.pop(0) for _ in range({"first": 0, "next": 1, "score": 2}[mode])]
    out_ref, rows_ref, cols_ref, acc_ref, sems = rest
    me = me_ref[0]
    inner = is_inner(me)
    rows = own_ref.shape[1]
    width = rows_ref.shape[1]
    docs = pltpu.make_async_copy(doc_ref.at[0, :, pl.ds(off, width)], cols_ref, sems.at[8 * CAP])
    docs.start()

    def slot(k):
        return rows_ref.at[pl.ds(k * rows, rows), :]

    def wide(ref, i):
        return ref.at[i, :, pl.ds(off, width)]

    def go(src, k):
        pltpu.make_async_copy(src, slot(k), sems.at[k]).start()

    for r in range(CAP):
        go(wide(own_ref, codes_ref[SLOTS + r]), r)
        go(wide(own_side_ref, r), 4 * CAP + r)

    @pl.when(inner == 1)
    def _():
        for r in range(CAP):
            go(came_ref.at[codes_ref[SLOTS + CAP + r]], CAP + r)
        for k in range(2 * CAP, 4 * CAP):
            fetch(codes_ref[SLOTS + k], early_ref, late_ref, off, slot(k), sems.at[k])
        for k in range(3 * CAP):
            go(side_ref.at[k], 5 * CAP + k)

    @pl.when(inner == 0)
    def _():
        for r in range(CAP):
            go(wide(own_straight_ref, r), CAP + r)
            go(wide(own_diag_ref, r), 5 * CAP + r)
        for k in range(2 * CAP):
            go(straight_ref.at[k], 2 * CAP + k)
            go(diag_ref.at[k], 6 * CAP + k)

    for k in range(8 * CAP):
        pltpu.make_async_copy(came_ref.at[0], slot(k), sems.at[k]).wait()
    docs.wait()
    step = 256
    if mode == "score":
        acc_ref[...] = held[1][...]

    def block(n, _):
        at = pl.ds(pl.multiple_of(n * step, step), step)
        part = lax.dot_general(
            rows_ref[...], cols_ref[at, :], (((1,), (1,)), ((), ())), preferred_element_type=jnp.float32
        )
        if mode == "first":
            out_ref[:, at] = part
        elif mode == "next":
            out_ref[:, at] = held[0][:, at] + part
        else:
            both = part * held[0][:, at]
            acc_ref[...] += jnp.sum(both.reshape(8 * CAP, rows, step), axis=1)
        return 0

    lax.fori_loop(0, SEQ_D // step, block, 0)
    if mode == "score" and not last:
        out_ref[...] = acc_ref[...]
    if last:
        total = jnp.sum(acc_ref[...], axis=1, keepdims=True)
        out_ref[...] = jnp.zeros_like(out_ref)
        near = jnp.where(inner == 1, me ^ 6, me ^ 4)
        far = jnp.where(inner == 1, me ^ 4, me ^ 6)
        for k, owner in enumerate((me, me ^ 2, near, far, me ^ 1, me ^ 3, near ^ 1, far ^ 1)):
            wide_total = jnp.broadcast_to(total[k * CAP : (k + 1) * CAP], (CAP, 128))
            out_ref[owner] = wide_total


def gram_call(me, codes, own, came, early, late, owns, parts, doc, off, token, mode, held, last=False):
    n, rows, width = came.shape
    tokens = doc.shape[1]
    total = 8 * CAP * rows
    args = [me, codes, own, came] + ([] if early is None else [early]) + [late, *owns, *parts, doc, token]
    if last:
        out = jax.ShapeDtypeStruct((8, CAP, 128), jnp.float32)
    elif mode == "score":
        out = jax.ShapeDtypeStruct((8 * CAP, 256), jnp.float32)
    else:
        out = jax.ShapeDtypeStruct((total, tokens), jnp.float32)
    return pl.pallas_call(
        functools.partial(gram_kernel, split=early is not None, off=off, mode=mode, last=last),
        out_shape=out,
        in_specs=[SMEM, SMEM] + [ANY] * (len(args) - 2) + [VMEM] * len(held),
        out_specs=VMEM,
        scratch_shapes=[
            pltpu.VMEM((total, width), doc.dtype),
            pltpu.VMEM((tokens, width), doc.dtype),
            pltpu.VMEM((8 * CAP, 256), jnp.float32),
            pltpu.SemaphoreType.DMA((8 * CAP + 1,)),
        ],
        compiler_params=pltpu.CompilerParams(vmem_limit_bytes=24 * 1024 * 1024),
        cost_estimate=cost(4_000_000, 2 * total * tokens * width),
    )(*args, *held)


def finish_kernel(came_ref, place_ref, out_ref, *, tensor):
    factor = 1.0 / jnp.sqrt(jnp.float32(FF) * jnp.float32(D) * jnp.float32(SEQ_S) * jnp.float32(SEQ_D))
    for p in range(8 * CAP):
        slot = place_ref[p]
        doc, r = slot // CAP, slot % CAP
        total = came_ref[doc * tensor, r]
        for t in range(1, tensor):
            total = total + came_ref[doc * tensor + t, r]
        out_ref[p] = total * factor


def pieces(width, parts):
    lanes = width // 128
    sizes = [(lanes // parts + (1 if i < lanes % parts else 0)) * 128 for i in range(parts)]
    sizes[-1] += width - sum(sizes)
    return sizes


def chain(sample_act, sample_grad, doc_act, doc_grad, pair_doc, pair_sample):
    groups, tensor = lax.axis_size("groups"), lax.axis_size("tensor")
    me = jnp.stack([lax.axis_index("docs"), lax.axis_index("groups")]).astype(jnp.int32)
    chunks = []
    off = 0
    for w in pieces(sample_grad.shape[2], 2):
        chunks.append((True, off, w))
        off += w
    off = 0
    for w in pieces(sample_act.shape[2], 6):
        chunks.append((False, off, w))
        off += w
    send = lambda x, pairs: lax.ppermute(x, "docs", pairs)
    came0 = send(sample_grad[:, :, : chunks[0][2]], TO_INNER)
    tab, place, across, straight, diag, side, out1 = start_call(
        me, pair_doc, pair_sample, sample_grad, chunks[1][1]
    )
    early = send(across, ACROSS)
    own_grads = (send(straight, TO_OUTER), send(diag, TO_DIAG), send(side, OVER_Y))
    tables = lax.all_to_all(
        jnp.broadcast_to(tab[None, :], (groups * 8, 8 * CAP)), ("groups", "docs"), 0, 0, tiled=True
    )
    codes = codes_call(me, tables, groups)

    def pipeline(count, came0, early, own_grads, out1, codes, sample_act, sample_grad, doc_act, doc_grad):
        total = len(chunks)
        sample = lambda i: sample_grad if chunks[i][0] else sample_act
        came = {0: came0, 1: send(out1, TO_INNER)}
        late, parts, token = {}, {}, codes
        state = dict(grads=None, score=None, owns=None)

        def mix(i, token):
            is_grad, off, w = chunks[i]
            ahead = i + 2 if i + 2 < total else None
            first = OWN if is_grad else 0
            out = mix_call(
                codes, sample(i), came[i], count - first, first, off, token,
                None if ahead is None else sample(ahead),
                None if ahead is None else chunks[ahead][1],
                None if ahead is None else chunks[ahead][2],
            )
            late[i] = send(out[0], ACROSS)
            if ahead is not None:
                came[ahead] = send(out[1], TO_INNER)
            return out[0]

        def forward(i, token):
            is_grad, off, w = chunks[i]
            s, d, y = forward_call(codes, came[i], early if is_grad else None, late[i], off, token)
            parts[i] = (send(s, TO_OUTER), send(d, TO_DIAG), send(y, OVER_Y_INNER))
            return s

        def gram(i, token):
            is_grad, off, w = chunks[i]
            if is_grad:
                held = [] if state["grads"] is None else [state["grads"]]
                mode = "next" if held else "first"
                out = gram_call(me, codes, sample_grad, came[i], early, late[i], own_grads, parts[i],
                                doc_grad, off, token, mode, held)
                state["grads"] = out
                if not chunks[i + 1][0]:
                    state["grads"] = lax.psum(out, "tensor") if tensor != 2 else out + lax.ppermute(
                        out, "tensor", [(0, 1), (1, 0)]
                    )
                    state["score"] = jnp.zeros((8 * CAP, 256), jnp.float32)
                return out
            out = gram_call(me, codes, sample_act, came[i], None, late[i], state["owns"], parts[i],
                            doc_act, off, token, "score", [state["grads"], state["score"]],
                            last=i == total - 1)
            state["score"] = out
            return out

        token = mix(0, token)
        s, d, y = own_call(me, tab, sample_act, token)
        state["owns"] = (send(s, TO_OUTER), send(d, TO_DIAG), send(y, OVER_Y))
        token = mix(1, s)
        for i in range(total):
            if i + 2 < total:
                token = mix(i + 2, token)
            token = forward(i, token)
            if i >= 2:
                token = gram(i - 2, token)
        for i in range(total - 2, total):
            token = gram(i, token)
        return state["score"]

    score = lax.switch(
        codes[BRANCH],
        [functools.partial(pipeline, c) for c in COUNTS],
        came0, early, own_grads, out1, codes, sample_act, sample_grad, doc_act, doc_grad,
    )
    give = jnp.broadcast_to(score[:, None, :, 0], (8, tensor, CAP)).reshape(8 * tensor, CAP)
    back = lax.all_to_all(give, ("docs", "tensor"), 0, 0, tiled=True)
    return pl.pallas_call(
        functools.partial(finish_kernel, tensor=tensor),
        out_shape=jax.ShapeDtypeStruct((8 * CAP,), jnp.float32),
        in_specs=[SMEM, SMEM],
        out_specs=SMEM,
    )(back, place)


def direct(sample_act, sample_grad, doc_act, doc_grad, pair_doc, pair_sample):
    owners = lax.axis_size("docs")
    pair_count = pair_doc.shape[0]
    slot_count = owners * CAP
    factor = 1.0 / jnp.sqrt(
        jnp.float32(FF) * jnp.float32(D) * jnp.float32(SEQ_S) * jnp.float32(SEQ_D)
    )
    target = pair_doc[:, 0]
    order = jnp.arange(pair_count, dtype=jnp.int32)
    earlier = (target[:, None] == target[None, :]) & (order[None, :] < order[:, None])
    rank = jnp.sum(earlier.astype(jnp.int32), axis=1)
    slot_of_pair = target * CAP + rank
    chosen = (jnp.arange(slot_count, dtype=jnp.int32)[:, None] == slot_of_pair[None, :]).astype(
        jnp.int32
    )
    slot_sample = jnp.sum(chosen * pair_sample[None, :], axis=1)
    send_act = sample_act[slot_sample]
    send_grad = sample_grad[slot_sample]
    send_act = send_act.reshape(owners, CAP, send_act.shape[1], send_act.shape[2])
    send_grad = send_grad.reshape(owners, CAP, send_grad.shape[1], send_grad.shape[2])
    grad_in = lax.all_to_all(send_grad, "docs", split_axis=0, concat_axis=0, tiled=True)
    act_in = lax.all_to_all(send_act, "docs", split_axis=0, concat_axis=0, tiled=True)
    grad_gram = jnp.einsum("nmsf,tf->nmst", grad_in, doc_grad[0], preferred_element_type=jnp.float32)
    grad_sum = lax.psum(grad_gram, "tensor")
    act_gram = jnp.einsum("nmsf,tf->nmst", act_in, doc_act[0], preferred_element_type=jnp.float32)
    scores = lax.psum(jnp.sum(act_gram * grad_sum, axis=(2, 3)) * factor, "tensor")
    returned = lax.all_to_all(scores, "docs", split_axis=0, concat_axis=0, tiled=True)
    flat_scores = returned.reshape(slot_count)
    return jnp.sum(jnp.where(chosen > 0, flat_scores[:, None], 0.0), axis=0)


def solution(mesh):
    in_specs = (
        P(("groups", "docs"), None, "tensor"),
        P(("groups", "docs"), None, "tensor"),
        P(("groups", "docs"), None, "tensor"),
        P(("groups", "docs"), None, "tensor"),
        P(("groups", "docs"), None),
        P(("groups", "docs")),
    )
    out_specs = P(("groups", "docs"))

    def per_device(sample_act, sample_grad, doc_act, doc_grad, pair_doc, pair_sample):
        fits = mesh.shape["docs"] == 8 and pair_doc.shape[0] == 8 * CAP and sample_act.shape[0] == 8
        run = chain if fits else direct
        return run(sample_act, sample_grad, doc_act, doc_grad, pair_doc, pair_sample)

    return jax.shard_map(
        per_device, mesh=mesh, in_specs=in_specs, out_specs=out_specs, check_vma=False
    )
```

time: 256 us -> 774 us (3.02)
  Pallas kernels: 0 us -> 541 us
  waiting for transfers between devices: 179 us -> 57 us
  starting transfers between devices: 12 us -> 97.4 us
  local copies, waits for them, and re-layouts: 9.32 us -> 31.7 us
  matrix products: 15.4 us -> 0 us
  blocking collectives: 12 us -> 24.6 us
  between operations: 13.4 us -> 1.02 us
  other arithmetic: 14.5 us -> 2.29 us
  loops' own time: 0 us -> 10.9 us
    pallas_call x0 -> x28, Pallas kernels: none -> 541 us  [the longest x8 249 us: mix_call(): pl.pallas_call(functools.partial(mix_kernel, first=first, off=off, ahead=...]
    all_to_all x2 -> x0, waiting for transfers between devices: 156 us -> none  [the longest x1 119 us: per_device(): lax.all_to_all(send_act, 'docs', split_axis=0, concat_axis=0, tiled=True)]
    ppermute x0 -> x48, starting transfers between devices: none -> 97.4 us  [the longest x47 97.4 us: chain(): send = lambda x, pairs: lax.ppermute(x, 'docs', pairs)]
    ppermute x0 -> x48, waiting for transfers between devices: none -> 57 us  [the longest x47 57 us: chain(): send = lambda x, pairs: lax.ppermute(x, 'docs', pairs)]
    cond x0 -> x144, local copies, waits for them, and re-layouts: none -> 28.4 us
    psum x1 -> x0, waiting for transfers between devices: 22.5 us -> none  [per_device(): act_sum, grad_sum = lax.psum((act_gram, grad_gram), 'tensor')]
    dot_general x2 -> x0, matrix products: 15.4 us -> none  [the longest x1 10.9 us: per_device(): jnp.einsum('nmsf,tf->nmst', act_in, doc_rows, preferred_element_type=jnp....]
    all_to_all x1 -> x2, blocking collectives: 12 us -> 24.6 us  [the longest x1 14.5 us: chain(): lax.all_to_all(jnp.broadcast_to(tab[None, :], (groups * 8, 8 * CAP)), ('g...]
  transfers between devices with their start and end apart: 3 -> 48, of which waited for: 3 -> 7; matrix products, arithmetic and copies ran while one was open for 6% -> 1% of each run, Pallas kernels for 0% -> 70%
where the time goes in v1:
time: 774 us; the launch traced here: 766 us
  Pallas kernels  541 us (70%)
  starting transfers between devices  97.4 us (13%)
  waiting for transfers between devices  57 us (7%)
  local copies, waits for them, and re-layouts  31.7 us (4%)
  blocking collectives  24.6 us (3%)
  loops' own time  10.9 us (1%)
    pallas_call x8, Pallas kernels, mix_call(): pl.pallas_call(functools.partial(mix_kernel, first=first, off=off, ahead=...  249 us
    pallas_call x8, Pallas kernels, forward_call(): pl.pallas_call(functools.partial(forward_kernel, split=early is not None,...  191 us
    ppermute x47, starting transfers between devices, chain(): send = lambda x, pairs: lax.ppermute(x, 'docs', pairs)  97.4 us
    pallas_call x1, Pallas kernels, own_call(): pl.pallas_call(own_kernel, out_shape=(buf,) * 3, in_specs=[SMEM, SMEM, AN...  65.7 us
    ppermute x47, waiting for transfers between devices, chain(): send = lambda x, pairs: lax.ppermute(x, 'docs', pairs)  57 us
    pallas_call x8, Pallas kernels, gram_call(): pl.pallas_call(functools.partial(gram_kernel, split=early is not None, of...  28.6 us
    cond x144, local copies, waits for them, and re-layouts  28.4 us
  transfers between devices with their start and end apart: 48, of which 7 were waited for; matrix products, arithmetic and copies ran while one was open for 1% of the time, Pallas kernels for 70%

profile of v1, /device:TPU:0, one launch (start us, length us, event | category | flops | bytes accessed | tf_op | source)
XLA Modules:
  0.0 765.8 jit_solution(13088567399847723407)
XLA Ops:
  1.2 5.0 collective-permute-start.172
  7.6 2.9 shard_map.64
  13.8 1.6 collective-permute-start.176
  15.4 14.5 %all_to_all.19 = s32[16,1,16]{2,1,0:T(1,128)} all-to-all(s32[16,1,16]{2,1,0:T(1,128)S(1)} %broadcast_in_dim.6), channel_id=1, replica_groups=mesh['groups'=2,'docs'=8,'tensor'=2] {'groups','docs'}, dimensions={0} | all-to-all | bytes 2048 | tf_op jit(solution)/shard_map/all_to_all | solution.py:460
  29.9 2.2 shard_map.65
  33.4 720.4 %conditional.1 = (f32[8,2,128]{2,1,0:T(2,128)S(1)}) conditional(s32[]{:T(128)} %bitcast.3, (bf16[8,32,1024]{2,1,0:T(8,128)(2,1)}, s32[64]{0:T(128)S(1)}, bf16[8,32,2048]{2,1,0:T(8,128)(2,1)S(1)}, bf16[8,32,1024]{2,1,0:T(8,128)(2,1)S(1)}, bf16[8,32,5504]{2,1,0:T(8,128)(2,1)}, /*index=5*/s32[2]{0:T(128)S(1)}, ...), branch_computations={%region_0.0_spmd, %region_1.0_spmd, %region_2.0_spmd, %region_3.0_... | conditional | flops 5939527680 | bytes 355020544 | solution.py:527
  33.7 2.5 collective-permute-start.43
  36.2 17.7 %branch_1_fun.25 = (bf16[9,32,1024]{2,1,0:T(8,128)(2,1)}, bf16[8,32,1024]{2,1,0:T(8,128)(2,1)}) custom-call(s32[64]{0:T(128)S(1)} %get-tuple-element.167.codes_ref.rest_0_, bf16[8,32,2048]{2,1,0:T(8,128)(2,1)S(1)} %get-tuple-element.169.own_ref, bf16[8,32,1024]{2,1,0:T(8,128)(2,1)S(1)} %get-tuple-element.172.came_ref, ...), custom_call_target="tpu_custom_call" | custom-call | bytes 4000000 | tf_op jit(solution)/shard_map/cond/branch_1_fun/pallas_call | solution.py:253
  56.0 65.7 %branch_1_fun.26 = (bf16[2,32,5504]{2,1,0:T(8,128)(2,1)}, bf16[2,32,5504]{2,1,0:T(8,128)(2,1)}, bf16[2,32,5504]{2,1,0:T(8,128)(2,1)}) custom-call(s32[2]{0:T(128)S(1)} %get-tuple-element.166.me_ref, s32[16]{0:T(128)S(1)} %get-tuple-element.171.tab_ref, bf16[8,32,5504]{2,1,0:T(8,128)(2,1)} %get-tuple-element.168.rest_1_.act_ref.own_ref, ...), custom_call_target="tpu_custom_call" | custom-call | bytes 4000000 | tf_op jit(solution)/shard_map/cond/branch_1_fun/pallas_call | solution.py:128
  122.5 25.6 %branch_1_fun.27 = (bf16[9,32,1024]{2,1,0:T(8,128)(2,1)}, bf16[8,32,896]{2,1,0:T(8,128)(2,1)}) custom-call(s32[64]{0:T(128)S(1)} %get-tuple-element.167.codes_ref.rest_0_, bf16[8,32,2048]{2,1,0:T(8,128)(2,1)S(1)} %get-tuple-element.169.own_ref, bf16[8,32,1024]{2,1,0:T(8,128)(2,1)} %copy-done.40, bf16[2,32,5504]{2,1,0:T(8,128)(2,1)} %get-tuple-element.174.rest_0_, ...), custom_call_target="tpu_custom_call" | custom-call | bytes 4000000 | tf_op jit(solution)/shard_map/cond/branch_1_fun/pallas_call | solution.py:253
  150.3 41.5 %branch_1_fun.28 = (bf16[13,32,1024]{2,1,0:T(8,128)(2,1)}, bf16[8,32,896]{2,1,0:T(8,128)(2,1)}) custom-call(s32[64]{0:T(128)S(1)} %get-tuple-element.167.codes_ref.rest_0_, bf16[8,32,5504]{2,1,0:T(8,128)(2,1)} %get-tuple-element.168.rest_1_.act_ref.own_ref, bf16[8,32,1024]{2,1,0:T(8,128)(2,1)} %copy-done.34, ...), custom_call_target="tpu_custom_call" | custom-call | bytes 4000000 | tf_op jit(solution)/shard_map/cond/branch_1_fun/pallas_call | solution.py:253
  194.9 1.6 branch_1_fun.29
  199.9 38.3 %branch_1_fun.30 = (bf16[13,32,896]{2,1,0:T(8,128)(2,1)}, bf16[8,32,896]{2,1,0:T(8,128)(2,1)}) custom-call(s32[64]{0:T(128)S(1)} %get-tuple-element.167.codes_ref.rest_0_, bf16[8,32,5504]{2,1,0:T(8,128)(2,1)} %get-tuple-element.168.rest_1_.act_ref.own_ref, bf16[8,32,896]{2,1,0:T(8,128)(2,1)} %copy-done.56, bf16[4,32,1024]{2,1,0:T(8,128)(2,1)} %get-tuple-element.180.rest_0_, ...), custom_call_target="tpu_custom_call" | custom-call | bytes 4000000 | tf_op jit(solution)/shard_map/cond/branch_1_fun/pallas_call | solution.py:253
  240.4 29.6 %collective-permute-start.52 = (bf16[8,32,896]{2,1,0:T(8,128)(2,1)}, bf16[8,32,896]{2,1,0:T(8,128)(2,1)S(1)}, u32[]{:S(2)}, u32[]{:S(2)}) collective-permute-start(bf16[8,32,896]{2,1,0:T(8,128)(2,1)} %get-tuple-element.188), channel_id=1, source_target_pairs={{0,4},{2,6},{12,8},{14,10},{1,5},{3,7},{13,9},{15,11},{16,20},{18,... | collective-permute-start | bytes 1376264 | tf_op jit(solution)/shard_map/cond/branch_1_fun/ppermute | solution.py:453
  271.3 29.6 %branch_1_fun.31 = (bf16[4,32,1024]{2,1,0:T(8,128)(2,1)}, bf16[4,32,1024]{2,1,0:T(8,128)(2,1)}, bf16[6,32,1024]{2,1,0:T(8,128)(2,1)}) custom-call(s32[64]{0:T(128)S(1)} %get-tuple-element.167.codes_ref.rest_0_, bf16[8,32,1024]{2,1,0:T(8,128)(2,1)} %copy-done.40, bf16[4,32,2048]{2,1,0:T(8,128)(2,1)} %copy-done.215, ...), custom_call_target="tpu_custom_call" | custom-call | bytes 4000000 | tf_op jit(solution)/shard_map/cond/branch_1_fun/pallas_call | solution.py:306
  305.7 38.3 %branch_1_fun.32 = (bf16[13,32,896]{2,1,0:T(8,128)(2,1)}, bf16[8,32,896]{2,1,0:T(8,128)(2,1)}) custom-call(s32[64]{0:T(128)S(1)} %get-tuple-element.167.codes_ref.rest_0_, bf16[8,32,5504]{2,1,0:T(8,128)(2,1)} %get-tuple-element.168.rest_1_.act_ref.own_ref, bf16[8,32,896]{2,1,0:T(8,128)(2,1)} %copy-done.60, bf16[4,32,1024]{2,1,0:T(8,128)(2,1)} %get-tuple-element.190.rest_0_, ...), custom_call_target="tpu_custom_call" | custom-call | bytes 4000000 | tf_op jit(solution)/shard_map/cond/branch_1_fun/pallas_call | solution.py:253
  344.1 29.6 %branch_1_fun.33 = (bf16[4,32,1024]{2,1,0:T(8,128)(2,1)}, bf16[4,32,1024]{2,1,0:T(8,128)(2,1)}, bf16[6,32,1024]{2,1,0:T(8,128)(2,1)}) custom-call(s32[64]{0:T(128)S(1)} %get-tuple-element.167.codes_ref.rest_0_, bf16[8,32,1024]{2,1,0:T(8,128)(2,1)} %copy-done.34, bf16[13,32,1024]{2,1,0:T(8,128)(2,1)} %copy-done.86, ...), custom_call_target="tpu_custom_call" | custom-call | bytes 4000000 | tf_op jit(solution)/shard_map/cond/branch_1_fun/pallas_call | solution.py:306
  374.7 3.5 branch_1_fun.34.rest_0_.rest_10_
  380.2 38.3 %branch_1_fun.35 = (bf16[13,32,896]{2,1,0:T(8,128)(2,1)}, bf16[8,32,896]{2,1,0:T(8,128)(2,1)}) custom-call(s32[64]{0:T(128)S(1)} %get-tuple-element.167.codes_ref.rest_0_, bf16[8,32,5504]{2,1,0:T(8,128)(2,1)} %get-tuple-element.168.rest_1_.act_ref.own_ref, bf16[8,32,896]{2,1,0:T(8,128)(2,1)} %copy-done.76, f32[512,768]{1,0:T(8,128)} %copy-done.26, ...), custom_call_target="tpu_custom_call" | custom-call | bytes 4000000 | tf_op jit(solution)/shard_map/cond/branch_1_fun/pallas_call | solution.py:253
  419.5 26.1 %branch_1_fun.36 = (bf16[4,32,896]{2,1,0:T(8,128)(2,1)}, bf16[4,32,896]{2,1,0:T(8,128)(2,1)}, bf16[6,32,896]{2,1,0:T(8,128)(2,1)}) custom-call(s32[64]{0:T(128)S(1)} %get-tuple-element.167.codes_ref.rest_0_, bf16[8,32,896]{2,1,0:T(8,128)(2,1)} %copy-done.56, bf16[13,32,896]{2,1,0:T(8,128)(2,1)} %copy-done.94, bf16[13,32,896]{2,1,0:T(8,128)(2,1)} %get-tuple-element.202.rest_1_), custom_call_target="tpu_custom_call" | custom-call | bytes 4000000 | tf_op jit(solution)/shard_map/cond/branch_1_fun/pallas_call | solution.py:306
  448.1 3.9 branch_1_fun.37.rest_0_
  454.8 6.9 collective-permute-start.62
  461.7 12.4 %collective-permute-done.55.rest_1_ = bf16[2,32,5504]{2,1,0:T(8,128)(2,1)S(1)} collective-permute-done((bf16[2,32,5504]{2,1,0:T(8,128)(2,1)S(1)}, bf16[2,32,5504]{2,1,0:T(8,128)(2,1)S(1)}, u32[]{:S(2)}, u32[]{:S(2)}) %collective-permute-start.55) | collective-permute-done | bytes 704544 | tf_op jit(solution)/shard_map/cond/branch_1_fun/ppermute | solution.py:453
  474.1 1.5 collective-permute-start.61
  475.7 13.6 %collective-permute-done.56.rest_2_ = bf16[2,32,5504]{2,1,0:T(8,128)(2,1)S(1)} collective-permute-done((bf16[2,32,5504]{2,1,0:T(8,128)(2,1)S(1)}, bf16[2,32,5504]{2,1,0:T(8,128)(2,1)S(1)}, u32[]{:S(2)}, u32[]{:S(2)}) %collective-permute-start.56) | collective-permute-done | bytes 704544 | tf_op jit(solution)/shard_map/cond/branch_1_fun/ppermute | solution.py:453
  494.2 6.1 collective-permute-done.58.rest_4_
  501.0 2.2 collective-permute-start.54
  503.2 2.3 collective-permute-done.59.rest_5_
  506.2 1.5 collective-permute-start.76
  507.8 24.4 %branch_1_fun.38.rest_1_ = bf16[13,32,896]{2,1,0:T(8,128)(2,1)} custom-call(s32[64]{0:T(128)S(1)} %get-tuple-element.167.codes_ref.rest_0_, bf16[8,32,5504]{2,1,0:T(8,128)(2,1)} %get-tuple-element.168.rest_1_.act_ref.own_ref, bf16[8,32,896]{2,1,0:T(8,128)(2,1)} %copy-done.64, f32[512,768]{1,0:T(8,128)} %copy-done.21), custom_call_target="tpu_custom_call" | custom-call | bytes 4000000 | tf_op jit(solution)/shard_map/cond/branch_1_fun/pallas_call | solution.py:253
  532.2 1.5 collective-permute-start.72
  535.1 26.1 %branch_1_fun.39 = (bf16[4,32,896]{2,1,0:T(8,128)(2,1)}, bf16[4,32,896]{2,1,0:T(8,128)(2,1)}, bf16[6,32,896]{2,1,0:T(8,128)(2,1)}) custom-call(s32[64]{0:T(128)S(1)} %get-tuple-element.167.codes_ref.rest_0_, bf16[8,32,896]{2,1,0:T(8,128)(2,1)} %copy-done.60, bf16[13,32,896]{2,1,0:T(8,128)(2,1)} %collective-permute-done.61.rest_0_, ...), custom_call_target="tpu_custom_call" | custom-call | bytes 4000000 | tf_op jit(solution)/shard_map/cond/branch_1_fun/pallas_call | solution.py:306
  561.2 2.2 add.9.rest_9_
  563.8 3.6 branch_1_fun.40.rest_0_.rest_10_
  568.0 24.4 %branch_1_fun.41.rest_1_ = bf16[13,32,896]{2,1,0:T(8,128)(2,1)} custom-call(s32[64]{0:T(128)S(1)} %get-tuple-element.167.codes_ref.rest_0_, bf16[8,32,5504]{2,1,0:T(8,128)(2,1)} %get-tuple-element.168.rest_1_.act_ref.own_ref, bf16[8,32,896]{2,1,0:T(8,128)(2,1)} %collective-permute-done.54.came_ref, f32[16,256]{1,0:T(8,128)} %copy-done.181), custom_call_target="tpu_custom_call" | custom-call | bytes 4000000 | tf_op jit(solution)/shard_map/cond/branch_1_fun/pallas_call | solution.py:253
  592.5 1.7 collective-permute-start.68
  596.1 11.1 %collective-permute-done.74.rest_5_ = bf16[4,32,896]{2,1,0:T(8,128)(2,1)S(1)} collective-permute-done((bf16[4,32,896]{2,1,0:T(8,128)(2,1)}, bf16[4,32,896]{2,1,0:T(8,128)(2,1)S(1)}, u32[]{:S(2)}, u32[]{:S(2)}) %collective-permute-start.74) | collective-permute-done | bytes 229408 | tf_op jit(solution)/shard_map/cond/branch_1_fun/ppermute | solution.py:453
  612.6 26.1 %branch_1_fun.42 = (bf16[4,32,896]{2,1,0:T(8,128)(2,1)}, bf16[4,32,896]{2,1,0:T(8,128)(2,1)}, bf16[6,32,896]{2,1,0:T(8,128)(2,1)}) custom-call(s32[64]{0:T(128)S(1)} %get-tuple-element.167.codes_ref.rest_0_, bf16[8,32,896]{2,1,0:T(8,128)(2,1)} %copy-done.76, bf16[13,32,896]{2,1,0:T(8,128)(2,1)} %collective-permute-done.76.rest_0_, ...), custom_call_target="tpu_custom_call" | custom-call | bytes 4000000 | tf_op jit(solution)/shard_map/cond/branch_1_fun/pallas_call | solution.py:306
  643.9 3.5 branch_1_fun.43.rest_1_.rest_10_
  649.4 26.1 %branch_1_fun.44 = (bf16[4,32,896]{2,1,0:T(8,128)(2,1)}, bf16[4,32,896]{2,1,0:T(8,128)(2,1)}, bf16[6,32,896]{2,1,0:T(8,128)(2,1)}) custom-call(s32[64]{0:T(128)S(1)} %get-tuple-element.167.codes_ref.rest_0_, bf16[8,32,896]{2,1,0:T(8,128)(2,1)} %copy-done.64, bf16[13,32,896]{2,1,0:T(8,128)(2,1)} %collective-permute-done.72.rest_0_, f32[16,256]{1,0:T(8,128)} %copy-done.185), custom_call_target="tpu_custom_call" | custom-call | bytes 4000000 | tf_op jit(solution)/shard_map/cond/branch_1_fun/pallas_call | solution.py:306
  684.7 3.6 branch_1_fun.45.rest_1_.rest_10_
  688.9 26.1 %branch_1_fun.46 = (bf16[4,32,896]{2,1,0:T(8,128)(2,1)}, bf16[4,32,896]{2,1,0:T(8,128)(2,1)}, bf16[6,32,896]{2,1,0:T(8,128)(2,1)}) custom-call(s32[64]{0:T(128)S(1)} %get-tuple-element.167.codes_ref.rest_0_, bf16[8,32,896]{2,1,0:T(8,128)(2,1)} %collective-permute-done.54.came_ref, bf16[13,32,896]{2,1,0:T(8,128)(2,1)} %collective-permute-done.68.rest_0_, ...), custom_call_target="tpu_custom_call" | custom-call | bytes 4000000 | tf_op jit(solution)/shard_map/cond/branch_1_fun/pallas_call | solution.py:306
  722.4 3.8 branch_1_fun.47.rest_8_.rest_10_
  726.2 9.2 %collective-permute-done.81.rest_5_ = bf16[4,32,896]{2,1,0:T(8,128)(2,1)S(1)} collective-permute-done((bf16[4,32,896]{2,1,0:T(8,128)(2,1)}, bf16[4,32,896]{2,1,0:T(8,128)(2,1)S(1)}, u32[]{:S(2)}, u32[]{:S(2)}) %collective-permute-start.81) | collective-permute-done | bytes 229408 | tf_op jit(solution)/shard_map/cond/branch_1_fun/ppermute | solution.py:453
  735.5 3.5 branch_1_fun.48.rest_8_.rest_10_
  739.0 2.2 collective-permute-done.78.rest_5_
  741.2 3.1 branch_1_fun.49
  754.0 10.0 %all_to_all.20 = f32[16,1,2]{2,1,0:T(1,128)} all-to-all(f32[16,1,2]{2,1,0:T(1,128)S(1)} %bitcast.19), channel_id=1, replica_groups=mesh['groups'=2,'docs'=8,'tensor'=2] {'docs','tensor'}, dimensions={0} | all-to-all | bytes 256 | tf_op jit(solution)/shard_map/all_to_all | solution.py:533
  (236 shorter events, 76.6 us)
Async XLA Ops:
  1.2 32.2 %collective-permute-start.172 = (bf16[8,32,1024]{2,1,0:T(8,128)(2,1)S(1)}, bf16[8,32,1024]{2,1,0:T(8,128)(2,1)S(1)}, u32[]{:S(2)}, u32[]{:S(2)}) collective-permute-start(bf16[8,32,1024]{2,1,0:T(8,128)(2,1)S(1)} %slice.10), channel_id=1, source_target_pairs={{0,4},{2,6},{12,8},{14,10},{1,5},{3,7},{13,9},{15,11},{16,20},{18,... | collective-permute-start | bytes 1572872 | tf_op jit(solution)/shard_map/ppermute | solution.py:453
  10.5 22.9 %collective-permute-start.173 = (bf16[4,32,2048]{2,1,0:T(8,128)(2,1)}, bf16[4,32,2048]{2,1,0:T(8,128)(2,1)S(1)}, u32[]{:S(2)}, u32[]{:S(2)}) collective-permute-start(bf16[4,32,2048]{2,1,0:T(8,128)(2,1)} %get-tuple-element.331), channel_id=1, source_target_pairs={{4,8},{6,10},{8,4},{10,6},{5,9},{7,11},{9,5},{11,7},{20,24},{22,26... | collective-permute-start | bytes 1572872 | tf_op jit(solution)/shard_map/ppermute | solution.py:453
  11.2 22.2 %collective-permute-start.174 = (bf16[2,32,2048]{2,1,0:T(8,128)(2,1)}, bf16[2,32,2048]{2,1,0:T(8,128)(2,1)}, u32[]{:S(2)}, u32[]{:S(2)}) collective-permute-start(bf16[2,32,2048]{2,1,0:T(8,128)(2,1)} %get-tuple-element.332), channel_id=1, source_target_pairs={{4,0},{6,2},{8,12},{10,14},{5,1},{7,3},{9,13},{11,15},{20,16},{22,... | collective-permute-start | bytes 786440 | tf_op jit(solution)/shard_map/ppermute | solution.py:453
  12.5 20.9 %collective-permute-start.175 = (bf16[2,32,2048]{2,1,0:T(8,128)(2,1)}, bf16[2,32,2048]{2,1,0:T(8,128)(2,1)}, u32[]{:S(2)}, u32[]{:S(2)}) collective-permute-start(bf16[2,32,2048]{2,1,0:T(8,128)(2,1)} %get-tuple-element.333), channel_id=1, source_target_pairs={{4,2},{6,0},{8,14},{10,12},{5,3},{7,1},{9,15},{11,13},{20,18},{22,... | collective-permute-start | bytes 786440 | tf_op jit(solution)/shard_map/ppermute | solution.py:453
  13.8 19.6 %collective-permute-start.176 = (bf16[2,32,2048]{2,1,0:T(8,128)(2,1)}, bf16[2,32,2048]{2,1,0:T(8,128)(2,1)}, u32[]{:S(2)}, u32[]{:S(2)}) collective-permute-start(bf16[2,32,2048]{2,1,0:T(8,128)(2,1)} %get-tuple-element.334), channel_id=1, source_target_pairs={{0,2},{2,0},{4,6},{6,4},{8,10},{10,8},{12,14},{14,12},{1,3},{3,1},... | collective-permute-start | bytes 786440 | tf_op jit(solution)/shard_map/ppermute | solution.py:453
  33.7 88.0 %collective-permute-start.43 = (bf16[8,32,1024]{2,1,0:T(8,128)(2,1)}, bf16[8,32,1024]{2,1,0:T(8,128)(2,1)S(1)}, u32[]{:S(2)}, u32[]{:S(2)}) collective-permute-start(bf16[8,32,1024]{2,1,0:T(8,128)(2,1)} %get-tuple-element.170), channel_id=1, source_target_pairs={{0,4},{2,6},{12,8},{14,10},{1,5},{3,7},{13,9},{15,11},{16,20},{18,... | collective-permute-start | bytes 1572872 | tf_op jit(solution)/shard_map/cond/branch_1_fun/ppermute | solution.py:453
  53.9 95.6 %collective-permute-start.46 = (bf16[8,32,1024]{2,1,0:T(8,128)(2,1)}, bf16[8,32,1024]{2,1,0:T(8,128)(2,1)S(1)}, u32[]{:S(2)}, u32[]{:S(2)}) collective-permute-start(bf16[8,32,1024]{2,1,0:T(8,128)(2,1)} %get-tuple-element.177), channel_id=1, source_target_pairs={{0,4},{2,6},{12,8},{14,10},{1,5},{3,7},{13,9},{15,11},{16,20},{18,... | collective-permute-start | bytes 1572872 | tf_op jit(solution)/shard_map/cond/branch_1_fun/ppermute | solution.py:453
  55.3 138.8 %collective-permute-start.45 = (bf16[9,32,1024]{2,1,0:T(8,128)(2,1)}, bf16[9,32,1024]{2,1,0:T(8,128)(2,1)S(1)}, u32[]{:S(2)}, u32[]{:S(2)}) collective-permute-start(bf16[9,32,1024]{2,1,0:T(8,128)(2,1)} %get-tuple-element.173.token_ref), channel_id=1, source_target_pairs={{4,8},{6,10},{8,4},{10,6},{5,9},{7,11},{9,5},{11,7},{20,24},{22,26... | collective-permute-start | bytes 1769480 | tf_op jit(solution)/shard_map/cond/branch_1_fun/ppermute | solution.py:453
  148.2 50.9 %collective-permute-start.44 = (bf16[8,32,896]{2,1,0:T(8,128)(2,1)}, bf16[8,32,896]{2,1,0:T(8,128)(2,1)S(1)}, u32[]{:S(2)}, u32[]{:S(2)}) collective-permute-start(bf16[8,32,896]{2,1,0:T(8,128)(2,1)} %get-tuple-element.175), channel_id=1, source_target_pairs={{0,4},{2,6},{12,8},{14,10},{1,5},{3,7},{13,9},{15,11},{16,20},{18,... | collective-permute-start | bytes 1376264 | tf_op jit(solution)/shard_map/cond/branch_1_fun/ppermute | solution.py:453
  191.8 112.5 %collective-permute-start.51 = (bf16[13,32,1024]{2,1,0:T(8,128)(2,1)}, bf16[13,32,1024]{2,1,0:T(8,128)(2,1)S(1)}, u32[]{:S(2)}, u32[]{:S(2)}) collective-permute-start(bf16[13,32,1024]{2,1,0:T(8,128)(2,1)} %get-tuple-element.179.rest_2_), channel_id=1, source_target_pairs={{4,8},{6,10},{8,4},{10,6},{5,9},{7,11},{9,5},{11,7},{20,24},{22,26... | collective-permute-start | bytes 2555912 | tf_op jit(solution)/shard_map/cond/branch_1_fun/ppermute | solution.py:453
  192.6 77.4 %collective-permute-start.53 = (bf16[9,32,1024]{2,1,0:T(8,128)(2,1)}, bf16[9,32,1024]{2,1,0:T(8,128)(2,1)}, u32[]{:S(2)}, u32[]{:S(2)}) collective-permute-start(bf16[9,32,1024]{2,1,0:T(8,128)(2,1)} %get-tuple-element.178.rest_0_), channel_id=1, source_target_pairs={{4,8},{6,10},{8,4},{10,6},{5,9},{7,11},{9,5},{11,7},{20,24},{22,26... | collective-permute-start | bytes 1769480 | tf_op jit(solution)/shard_map/cond/branch_1_fun/ppermute | solution.py:453
  196.5 41.7 %collective-permute-start.48 = (bf16[4,32,1024]{2,1,0:T(8,128)(2,1)}, bf16[4,32,1024]{2,1,0:T(8,128)(2,1)S(1)}, u32[]{:S(2)}, u32[]{:S(2)}) collective-permute-start(bf16[4,32,1024]{2,1,0:T(8,128)(2,1)} %get-tuple-element.180.rest_0_), channel_id=1, source_target_pairs={{4,0},{6,2},{8,12},{10,14},{5,1},{7,3},{9,13},{11,15},{20,16},{22,... | collective-permute-start | bytes 786440 | tf_op jit(solution)/shard_map/cond/branch_1_fun/ppermute | solution.py:453
  197.8 41.8 %collective-permute-start.49 = (bf16[4,32,1024]{2,1,0:T(8,128)(2,1)}, bf16[4,32,1024]{2,1,0:T(8,128)(2,1)S(1)}, u32[]{:S(2)}, u32[]{:S(2)}) collective-permute-start(bf16[4,32,1024]{2,1,0:T(8,128)(2,1)} %get-tuple-element.185), channel_id=1, source_target_pairs={{4,2},{6,0},{8,14},{10,12},{5,3},{7,1},{9,15},{11,13},{20,18},{22,... | collective-permute-start | bytes 786440 | tf_op jit(solution)/shard_map/cond/branch_1_fun/ppermute | solution.py:453
  199.1 101.8 %collective-permute-start.50 = (bf16[6,32,1024]{2,1,0:T(8,128)(2,1)}, bf16[6,32,1024]{2,1,0:T(8,128)(2,1)S(1)}, u32[]{:S(2)}, u32[]{:S(2)}) collective-permute-start(bf16[6,32,1024]{2,1,0:T(8,128)(2,1)} %get-tuple-element.186), channel_id=1, source_target_pairs={{4,6},{6,4},{8,10},{10,8},{5,7},{7,5},{9,11},{11,9},{20,22},{22,20... | collective-permute-start | bytes 1179656 | tf_op jit(solution)/shard_map/cond/branch_1_fun/ppermute | solution.py:453
  238.9 179.7 %collective-permute-start.66 = (bf16[13,32,896]{2,1,0:T(8,128)(2,1)}, bf16[13,32,896]{2,1,0:T(8,128)(2,1)S(1)}, u32[]{:S(2)}, u32[]{:S(2)}) collective-permute-start(bf16[13,32,896]{2,1,0:T(8,128)(2,1)} %get-tuple-element.189.rest_2_), channel_id=1, source_target_pairs={{4,8},{6,10},{8,4},{10,6},{5,9},{7,11},{9,5},{11,7},{20,24},{22,26... | collective-permute-start | bytes 2236424 | tf_op jit(solution)/shard_map/cond/branch_1_fun/ppermute | solution.py:453
  240.4 62.7 %collective-permute-start.52 = (bf16[8,32,896]{2,1,0:T(8,128)(2,1)}, bf16[8,32,896]{2,1,0:T(8,128)(2,1)S(1)}, u32[]{:S(2)}, u32[]{:S(2)}) collective-permute-start(bf16[8,32,896]{2,1,0:T(8,128)(2,1)} %get-tuple-element.188), channel_id=1, source_target_pairs={{0,4},{2,6},{12,8},{14,10},{1,5},{3,7},{13,9},{15,11},{16,20},{18,... | collective-permute-start | bytes 1376264 | tf_op jit(solution)/shard_map/cond/branch_1_fun/ppermute | solution.py:453
  270.0 109.4 %collective-permute-start.47 = (bf16[8,32,896]{2,1,0:T(8,128)(2,1)}, bf16[8,32,896]{2,1,0:T(8,128)(2,1)S(1)}, u32[]{:S(2)}, u32[]{:S(2)}) collective-permute-start(bf16[8,32,896]{2,1,0:T(8,128)(2,1)} %get-tuple-element.181), channel_id=1, source_target_pairs={{0,4},{2,6},{12,8},{14,10},{1,5},{3,7},{13,9},{15,11},{16,20},{18,... | collective-permute-start | bytes 1376264 | tf_op jit(solution)/shard_map/cond/branch_1_fun/ppermute | solution.py:453
  301.7 144.0 %collective-permute-start.65 = (bf16[6,32,1024]{2,1,0:T(8,128)(2,1)}, bf16[6,32,1024]{2,1,0:T(8,128)(2,1)}, u32[]{:S(2)}, u32[]{:S(2)}) collective-permute-start(bf16[6,32,1024]{2,1,0:T(8,128)(2,1)} %get-tuple-element.201), channel_id=1, source_target_pairs={{4,6},{6,4},{8,10},{10,8},{5,7},{7,5},{9,11},{11,9},{20,22},{22,20... | collective-permute-start | bytes 1179656 | tf_op jit(solution)/shard_map/cond/branch_1_fun/ppermute | solution.py:453
  303.1 142.5 %collective-permute-start.63 = (bf16[4,32,1024]{2,1,0:T(8,128)(2,1)}, bf16[4,32,1024]{2,1,0:T(8,128)(2,1)}, u32[]{:S(2)}, u32[]{:S(2)}) collective-permute-start(bf16[4,32,1024]{2,1,0:T(8,128)(2,1)} %get-tuple-element.190.rest_0_), channel_id=1, source_target_pairs={{4,0},{6,2},{8,12},{10,14},{5,1},{7,3},{9,13},{11,15},{20,16},{22,... | collective-permute-start | bytes 786440 | tf_op jit(solution)/shard_map/cond/branch_1_fun/ppermute | solution.py:453
  304.4 141.2 %collective-permute-start.64 = (bf16[4,32,1024]{2,1,0:T(8,128)(2,1)}, bf16[4,32,1024]{2,1,0:T(8,128)(2,1)}, u32[]{:S(2)}, u32[]{:S(2)}) collective-permute-start(bf16[4,32,1024]{2,1,0:T(8,128)(2,1)} %get-tuple-element.200), channel_id=1, source_target_pairs={{4,2},{6,0},{8,14},{10,12},{5,3},{7,1},{9,15},{11,13},{20,18},{22,... | collective-permute-start | bytes 786440 | tf_op jit(solution)/shard_map/cond/branch_1_fun/ppermute | solution.py:453
  452.0 81.8 %collective-permute-start.67 = (f32[512,768]{1,0:T(8,128)S(1)}, f32[512,768]{1,0:T(8,128)}, u32[]{:S(2)}, u32[]{:S(2)}) collective-permute-start(f32[512,768]{1,0:T(8,128)S(1)} %branch_1_fun.37.rest_0_), channel_id=1, source_target_pairs={{0,1},{1,0},{2,3},{3,2},{4,5},{5,4},{6,7},{7,6},{8,9},{9,8},{10,11... | collective-permute-start | bytes 4718600 | tf_op jit(solution)/shard_map/cond/branch_1_fun/ppermute | solution.py:502
  452.1 22.0 %collective-permute-start.55 = (bf16[2,32,5504]{2,1,0:T(8,128)(2,1)S(1)}, bf16[2,32,5504]{2,1,0:T(8,128)(2,1)S(1)}, u32[]{:S(2)}, u32[]{:S(2)}) collective-permute-start(bf16[2,32,5504]{2,1,0:T(8,128)(2,1)S(1)} %copy-done.244), channel_id=1, source_target_pairs={{4,0},{6,2},{8,12},{10,14},{5,1},{7,3},{9,13},{11,15},{20,16},{22,... | collective-permute-start | bytes 2113544 | tf_op jit(solution)/shard_map/cond/branch_1_fun/ppermute | solution.py:453
  453.4 35.9 %collective-permute-start.56 = (bf16[2,32,5504]{2,1,0:T(8,128)(2,1)S(1)}, bf16[2,32,5504]{2,1,0:T(8,128)(2,1)S(1)}, u32[]{:S(2)}, u32[]{:S(2)}) collective-permute-start(bf16[2,32,5504]{2,1,0:T(8,128)(2,1)S(1)} %copy-done.253), channel_id=1, source_target_pairs={{4,2},{6,0},{8,14},{10,12},{5,3},{7,1},{9,15},{11,13},{20,18},{22,... | collective-permute-start | bytes 2113544 | tf_op jit(solution)/shard_map/cond/branch_1_fun/ppermute | solution.py:453
  454.7 35.8 %collective-permute-start.57 = (bf16[2,32,5504]{2,1,0:T(8,128)(2,1)S(1)}, bf16[2,32,5504]{2,1,0:T(8,128)(2,1)S(1)}, u32[]{:S(2)}, u32[]{:S(2)}) collective-permute-start(bf16[2,32,5504]{2,1,0:T(8,128)(2,1)S(1)} %copy-done.249), channel_id=1, source_target_pairs={{0,2},{2,0},{4,6},{6,4},{8,10},{10,8},{12,14},{14,12},{1,3},{3,1},... | collective-permute-start | bytes 2113544 | tf_op jit(solution)/shard_map/cond/branch_1_fun/ppermute | solution.py:453
  454.8 37.9 %collective-permute-start.62 = (bf16[8,32,896]{2,1,0:T(8,128)(2,1)S(1)}, bf16[8,32,896]{2,1,0:T(8,128)(2,1)S(1)}, u32[]{:S(2)}, u32[]{:S(2)}) collective-permute-start(bf16[8,32,896]{2,1,0:T(8,128)(2,1)S(1)} %copy-done.257), channel_id=1, source_target_pairs={{0,4},{2,6},{12,8},{14,10},{1,5},{3,7},{13,9},{15,11},{16,20},{18,... | collective-permute-start | bytes 1376264 | tf_op jit(solution)/shard_map/cond/branch_1_fun/ppermute | solution.py:453
  474.1 58.1 %collective-permute-start.61 = (bf16[13,32,896]{2,1,0:T(8,128)(2,1)}, bf16[13,32,896]{2,1,0:T(8,128)(2,1)}, u32[]{:S(2)}, u32[]{:S(2)}) collective-permute-start(bf16[13,32,896]{2,1,0:T(8,128)(2,1)} %get-tuple-element.191.rest_1_), channel_id=1, source_target_pairs={{4,8},{6,10},{8,4},{10,6},{5,9},{7,11},{9,5},{11,7},{20,24},{22,26... | collective-permute-start | bytes 2236424 | tf_op jit(solution)/shard_map/cond/branch_1_fun/ppermute | solution.py:453
  489.2 11.1 %collective-permute-start.58 = (bf16[4,32,1024]{2,1,0:T(8,128)(2,1)S(1)}, bf16[4,32,1024]{2,1,0:T(8,128)(2,1)S(1)}, u32[]{:S(2)}, u32[]{:S(2)}) collective-permute-start(bf16[4,32,1024]{2,1,0:T(8,128)(2,1)S(1)} %copy-done.137), channel_id=1, source_target_pairs={{4,0},{6,2},{8,12},{10,14},{5,1},{7,3},{9,13},{11,15},{20,16},{22,... | collective-permute-start | bytes 786440 | tf_op jit(solution)/shard_map/cond/branch_1_fun/ppermute | solution.py:453
  491.5 14.1 %collective-permute-start.59 = (bf16[4,32,1024]{2,1,0:T(8,128)(2,1)S(1)}, bf16[4,32,1024]{2,1,0:T(8,128)(2,1)S(1)}, u32[]{:S(2)}, u32[]{:S(2)}) collective-permute-start(bf16[4,32,1024]{2,1,0:T(8,128)(2,1)S(1)} %copy-done.261), channel_id=1, source_target_pairs={{4,2},{6,0},{8,14},{10,12},{5,3},{7,1},{9,15},{11,13},{20,18},{22,... | collective-permute-start | bytes 786440 | tf_op jit(solution)/shard_map/cond/branch_1_fun/ppermute | solution.py:453
  492.8 70.7 %collective-permute-start.60 = (bf16[6,32,1024]{2,1,0:T(8,128)(2,1)}, bf16[6,32,1024]{2,1,0:T(8,128)(2,1)}, u32[]{:S(2)}, u32[]{:S(2)}) collective-permute-start(bf16[6,32,1024]{2,1,0:T(8,128)(2,1)} %get-tuple-element.197), channel_id=1, source_target_pairs={{4,6},{6,4},{8,10},{10,8},{5,7},{7,5},{9,11},{11,9},{20,22},{22,20... | collective-permute-start | bytes 1179656 | tf_op jit(solution)/shard_map/cond/branch_1_fun/ppermute | solution.py:453
  501.0 67.0 %collective-permute-start.54 = (bf16[8,32,896]{2,1,0:T(8,128)(2,1)}, bf16[8,32,896]{2,1,0:T(8,128)(2,1)}, u32[]{:S(2)}, u32[]{:S(2)}) collective-permute-start(bf16[8,32,896]{2,1,0:T(8,128)(2,1)} %get-tuple-element.193), channel_id=1, source_target_pairs={{0,4},{2,6},{12,8},{14,10},{1,5},{3,7},{13,9},{15,11},{16,20},{18,... | collective-permute-start | bytes 1376264 | tf_op jit(solution)/shard_map/cond/branch_1_fun/ppermute | solution.py:453
  506.2 105.1 %collective-permute-start.76 = (bf16[13,32,896]{2,1,0:T(8,128)(2,1)}, bf16[13,32,896]{2,1,0:T(8,128)(2,1)}, u32[]{:S(2)}, u32[]{:S(2)}) collective-permute-start(bf16[13,32,896]{2,1,0:T(8,128)(2,1)} %get-tuple-element.202.rest_1_), channel_id=1, source_target_pairs={{4,8},{6,10},{8,4},{10,6},{5,9},{7,11},{9,5},{11,7},{20,24},{22,26... | collective-permute-start | bytes 2236424 | tf_op jit(solution)/shard_map/cond/branch_1_fun/ppermute | solution.py:453
  532.2 115.8 %collective-permute-start.72 = (bf16[13,32,896]{2,1,0:T(8,128)(2,1)}, bf16[13,32,896]{2,1,0:T(8,128)(2,1)}, u32[]{:S(2)}, u32[]{:S(2)}) collective-permute-start(bf16[13,32,896]{2,1,0:T(8,128)(2,1)} %branch_1_fun.38.rest_1_), channel_id=1, source_target_pairs={{4,8},{6,10},{8,4},{10,6},{5,9},{7,11},{9,5},{11,7},{20,24},{22,26... | collective-permute-start | bytes 2236424 | tf_op jit(solution)/shard_map/cond/branch_1_fun/ppermute | solution.py:453
  533.8 61.1 %collective-permute-start.73 = (bf16[4,32,896]{2,1,0:T(8,128)(2,1)}, bf16[4,32,896]{2,1,0:T(8,128)(2,1)}, u32[]{:S(2)}, u32[]{:S(2)}) collective-permute-start(bf16[4,32,896]{2,1,0:T(8,128)(2,1)} %get-tuple-element.203.rest_9_), channel_id=1, source_target_pairs={{4,0},{6,2},{8,12},{10,14},{5,1},{7,3},{9,13},{11,15},{20,16},{22,... | collective-permute-start | bytes 688136 | tf_op jit(solution)/shard_map/cond/branch_1_fun/ppermute | solution.py:453
  592.5 87.0 %collective-permute-start.68 = (bf16[13,32,896]{2,1,0:T(8,128)(2,1)}, bf16[13,32,896]{2,1,0:T(8,128)(2,1)}, u32[]{:S(2)}, u32[]{:S(2)}) collective-permute-start(bf16[13,32,896]{2,1,0:T(8,128)(2,1)} %branch_1_fun.41.rest_1_), channel_id=1, source_target_pairs={{4,8},{6,10},{8,4},{10,6},{5,9},{7,11},{9,5},{11,7},{20,24},{22,26... | collective-permute-start | bytes 2236424 | tf_op jit(solution)/shard_map/cond/branch_1_fun/ppermute | solution.py:453
  594.2 15.1 %collective-permute-start.75 = (bf16[6,32,896]{2,1,0:T(8,128)(2,1)}, bf16[6,32,896]{2,1,0:T(8,128)(2,1)S(1)}, u32[]{:S(2)}, u32[]{:S(2)}) collective-permute-start(bf16[6,32,896]{2,1,0:T(8,128)(2,1)} %get-tuple-element.208), channel_id=1, source_target_pairs={{4,6},{6,4},{8,10},{10,8},{5,7},{7,5},{9,11},{11,9},{20,22},{22,20... | collective-permute-start | bytes 1032200 | tf_op jit(solution)/shard_map/cond/branch_1_fun/ppermute | solution.py:453
  594.8 12.4 %collective-permute-start.74 = (bf16[4,32,896]{2,1,0:T(8,128)(2,1)}, bf16[4,32,896]{2,1,0:T(8,128)(2,1)S(1)}, u32[]{:S(2)}, u32[]{:S(2)}) collective-permute-start(bf16[4,32,896]{2,1,0:T(8,128)(2,1)} %get-tuple-element.207), channel_id=1, source_target_pairs={{4,2},{6,0},{8,14},{10,12},{5,3},{7,1},{9,15},{11,13},{20,18},{22,... | collective-permute-start | bytes 688136 | tf_op jit(solution)/shard_map/cond/branch_1_fun/ppermute | solution.py:453
  607.9 70.3 %collective-permute-start.71 = (bf16[6,32,896]{2,1,0:T(8,128)(2,1)}, bf16[6,32,896]{2,1,0:T(8,128)(2,1)}, u32[]{:S(2)}, u32[]{:S(2)}) collective-permute-start(bf16[6,32,896]{2,1,0:T(8,128)(2,1)} %get-tuple-element.206), channel_id=1, source_target_pairs={{4,6},{6,4},{8,10},{10,8},{5,7},{7,5},{9,11},{11,9},{20,22},{22,20... | collective-permute-start | bytes 1032200 | tf_op jit(solution)/shard_map/cond/branch_1_fun/ppermute | solution.py:453
  610.0 65.5 %collective-permute-start.69 = (bf16[4,32,896]{2,1,0:T(8,128)(2,1)}, bf16[4,32,896]{2,1,0:T(8,128)(2,1)}, u32[]{:S(2)}, u32[]{:S(2)}) collective-permute-start(bf16[4,32,896]{2,1,0:T(8,128)(2,1)} %get-tuple-element.204.rest_8_), channel_id=1, source_target_pairs={{4,0},{6,2},{8,12},{10,14},{5,1},{7,3},{9,13},{11,15},{20,16},{22,... | collective-permute-start | bytes 688136 | tf_op jit(solution)/shard_map/cond/branch_1_fun/ppermute | solution.py:453
  611.3 65.5 %collective-permute-start.70 = (bf16[4,32,896]{2,1,0:T(8,128)(2,1)}, bf16[4,32,896]{2,1,0:T(8,128)(2,1)}, u32[]{:S(2)}, u32[]{:S(2)}) collective-permute-start(bf16[4,32,896]{2,1,0:T(8,128)(2,1)} %get-tuple-element.205), channel_id=1, source_target_pairs={{4,2},{6,0},{8,14},{10,12},{5,3},{7,1},{9,15},{11,13},{20,18},{22,... | collective-permute-start | bytes 688136 | tf_op jit(solution)/shard_map/cond/branch_1_fun/ppermute | solution.py:453
  648.0 70.3 %collective-permute-start.85 = (bf16[6,32,896]{2,1,0:T(8,128)(2,1)}, bf16[6,32,896]{2,1,0:T(8,128)(2,1)}, u32[]{:S(2)}, u32[]{:S(2)}) collective-permute-start(bf16[6,32,896]{2,1,0:T(8,128)(2,1)} %get-tuple-element.217), channel_id=1, source_target_pairs={{4,6},{6,4},{8,10},{10,8},{5,7},{7,5},{9,11},{11,9},{20,22},{22,20... | collective-permute-start | bytes 1032200 | tf_op jit(solution)/shard_map/cond/branch_1_fun/ppermute | solution.py:453
  675.5 39.4 %collective-permute-start.80 = (bf16[4,32,896]{2,1,0:T(8,128)(2,1)}, bf16[4,32,896]{2,1,0:T(8,128)(2,1)}, u32[]{:S(2)}, u32[]{:S(2)}) collective-permute-start(bf16[4,32,896]{2,1,0:T(8,128)(2,1)} %get-tuple-element.210.rest_8_), channel_id=1, source_target_pairs={{4,0},{6,2},{8,12},{10,14},{5,1},{7,3},{9,13},{11,15},{20,16},{22,... | collective-permute-start | bytes 688136 | tf_op jit(solution)/shard_map/cond/branch_1_fun/ppermute | solution.py:453
  676.9 38.8 %collective-permute-start.83 = (bf16[4,32,896]{2,1,0:T(8,128)(2,1)}, bf16[4,32,896]{2,1,0:T(8,128)(2,1)}, u32[]{:S(2)}, u32[]{:S(2)}) collective-permute-start(bf16[4,32,896]{2,1,0:T(8,128)(2,1)} %get-tuple-element.209.rest_8_), channel_id=1, source_target_pairs={{4,0},{6,2},{8,12},{10,14},{5,1},{7,3},{9,13},{11,15},{20,16},{22,... | collective-permute-start | bytes 688136 | tf_op jit(solution)/shard_map/cond/branch_1_fun/ppermute | solution.py:453
  678.2 38.8 %collective-permute-start.84 = (bf16[4,32,896]{2,1,0:T(8,128)(2,1)}, bf16[4,32,896]{2,1,0:T(8,128)(2,1)}, u32[]{:S(2)}, u32[]{:S(2)}) collective-permute-start(bf16[4,32,896]{2,1,0:T(8,128)(2,1)} %get-tuple-element.216), channel_id=1, source_target_pairs={{4,2},{6,0},{8,14},{10,12},{5,3},{7,1},{9,15},{11,13},{20,18},{22,... | collective-permute-start | bytes 688136 | tf_op jit(solution)/shard_map/cond/branch_1_fun/ppermute | solution.py:453
  679.5 56.0 %collective-permute-start.82 = (bf16[6,32,896]{2,1,0:T(8,128)(2,1)}, bf16[6,32,896]{2,1,0:T(8,128)(2,1)}, u32[]{:S(2)}, u32[]{:S(2)}) collective-permute-start(bf16[6,32,896]{2,1,0:T(8,128)(2,1)} %get-tuple-element.215), channel_id=1, source_target_pairs={{4,6},{6,4},{8,10},{10,8},{5,7},{7,5},{9,11},{11,9},{20,22},{22,20... | collective-permute-start | bytes 1032200 | tf_op jit(solution)/shard_map/cond/branch_1_fun/ppermute | solution.py:453
  715.0 26.2 %collective-permute-start.79 = (bf16[6,32,896]{2,1,0:T(8,128)(2,1)}, bf16[6,32,896]{2,1,0:T(8,128)(2,1)S(1)}, u32[]{:S(2)}, u32[]{:S(2)}) collective-permute-start(bf16[6,32,896]{2,1,0:T(8,128)(2,1)} %get-tuple-element.213), channel_id=1, source_target_pairs={{4,6},{6,4},{8,10},{10,8},{5,7},{7,5},{9,11},{11,9},{20,22},{22,20... | collective-permute-start | bytes 1032200 | tf_op jit(solution)/shard_map/cond/branch_1_fun/ppermute | solution.py:453
  715.7 19.8 %collective-permute-start.81 = (bf16[4,32,896]{2,1,0:T(8,128)(2,1)}, bf16[4,32,896]{2,1,0:T(8,128)(2,1)S(1)}, u32[]{:S(2)}, u32[]{:S(2)}) collective-permute-start(bf16[4,32,896]{2,1,0:T(8,128)(2,1)} %get-tuple-element.214), channel_id=1, source_target_pairs={{4,2},{6,0},{8,14},{10,12},{5,3},{7,1},{9,15},{11,13},{20,18},{22,... | collective-permute-start | bytes 688136 | tf_op jit(solution)/shard_map/cond/branch_1_fun/ppermute | solution.py:453
  717.0 22.0 %collective-permute-start.77 = (bf16[4,32,896]{2,1,0:T(8,128)(2,1)}, bf16[4,32,896]{2,1,0:T(8,128)(2,1)S(1)}, u32[]{:S(2)}, u32[]{:S(2)}) collective-permute-start(bf16[4,32,896]{2,1,0:T(8,128)(2,1)} %get-tuple-element.211.rest_8_), channel_id=1, source_target_pairs={{4,0},{6,2},{8,12},{10,14},{5,1},{7,3},{9,13},{11,15},{20,16},{22,... | collective-permute-start | bytes 688136 | tf_op jit(solution)/shard_map/cond/branch_1_fun/ppermute | solution.py:453
  718.3 22.9 %collective-permute-start.78 = (bf16[4,32,896]{2,1,0:T(8,128)(2,1)}, bf16[4,32,896]{2,1,0:T(8,128)(2,1)S(1)}, u32[]{:S(2)}, u32[]{:S(2)}) collective-permute-start(bf16[4,32,896]{2,1,0:T(8,128)(2,1)} %get-tuple-element.212), channel_id=1, source_target_pairs={{4,2},{6,0},{8,14},{10,12},{5,3},{7,1},{9,15},{11,13},{20,18},{22,... | collective-permute-start | bytes 688136 | tf_op jit(solution)/shard_map/cond/branch_1_fun/ppermute | solution.py:453
  (73 other events, 979.3 us)

commit v2 on v0

v2 whole, which is shorter than its diff:
```python
import functools

import jax
import jax.numpy as jnp
from jax import lax
from jax.experimental import pallas as pl
from jax.experimental.pallas import tpu as pltpu
from jax.sharding import PartitionSpec as P

FF = 11008
D = 4096
SEQ_S = 32
SEQ_D = 768
CAP = 2

ANY = pl.BlockSpec(memory_space=pl.ANY)
SMEM = pl.BlockSpec(memory_space=pltpu.SMEM)
VMEM = pl.BlockSpec(memory_space=pltpu.VMEM)

INNER = (2, 3, 4, 5)
ACROSS = [(i, i ^ 6) for i in INNER]
OVER_Z = [(i, i ^ 2) for i in range(8)]
OVER_Y = [(i, i ^ 1) for i in range(8)]

OWN = 4
MAIN = 12
EXTRAS = (0, 1, 2, 4)

LIST, STRAIGHT, DIAG, SIDE, SLOTS, BRANCH, CODES = 0, 16, 20, 24, 32, 48, 64
SENT = 16


def is_inner(me):
    return ((me >> 1) ^ (me >> 2)) & 1


def bits(mask):
    total = mask & 1
    for i in range(1, 8):
        total = total + ((mask >> i) & 1)
    return total


SMALL = pltpu.CompilerParams(vmem_limit_bytes=6 * 1024 * 1024)
CHEAP = pl.CostEstimate(flops=0, bytes_accessed=1024, transcendentals=0)
CHUNK = 1024
LEAD = 4


class Copies:
    def __init__(self, sems):
        self.sems, self.used, self.held = sems, 0, []

    def start(self, src, dst):
        copy = pltpu.make_async_copy(src, dst, self.sems.at[self.used])
        copy.start()
        self.used += 1
        self.held.append(copy)

    def either(self, first, src, other, dst):
        sem = self.sems.at[self.used]

        @pl.when(first)
        def _():
            pltpu.make_async_copy(src, dst, sem).start()

        @pl.when(jnp.logical_not(first))
        def _():
            pltpu.make_async_copy(other, dst, sem).start()

        self.used += 1
        self.held.append(pltpu.make_async_copy(src, dst, sem))

    def wait(self):
        for copy in self.held:
            copy.wait()
        self.held = []


def cut(ref, i, off, width):
    return ref.at[i, :, pl.ds(off, width)]


def own_slots(copies, inner, me, tab_ref, here, ahead, dst):
    @pl.when(inner == 1)
    def _():
        c = Copies(copies.sems)
        for part, (ref, off, width) in enumerate(here):
            for k in range(2 * CAP):
                sample = tab_ref[(me ^ (2 + k // CAP)) * CAP + k % CAP]
                c.start(cut(ref, sample, off, width), cut(dst, part * 2 * CAP + k, 0, width))
        c.wait()

    @pl.when(inner == 0)
    def _():
        c = Copies(copies.sems)
        ref, off, width = ahead
        for s in range(8):
            c.start(cut(ref, s, off, width), cut(dst, s, 0, width))
        c.wait()


def start_kernel(me_ref, doc_ref, sample_ref, grad_ref, act_ref, tab_ref, place_ref, own_ref, z_ref, across_ref,
                 seen, sems, out_sems):
    me = me_ref[0]
    inner = is_inner(me)
    for d in range(8):
        seen[d] = 0
    for i in range(8 * CAP):
        tab_ref[i] = 0
    for i in range(16):
        own_ref[i] = 0
    mask = jnp.int32(0)
    half = me >> 2
    for p in range(8 * CAP):
        doc = doc_ref[p, 0]
        slot = doc * CAP + jnp.minimum(seen[doc], CAP - 1)
        seen[doc] = seen[doc] + 1
        place_ref[p] = slot
        tab_ref[slot] = sample_ref[p]
        bit = jnp.left_shift(1, sample_ref[p])
        mask = jnp.where((doc >> 2) != half, mask | bit, mask)
    count = jnp.int32(0)
    for s in range(8):
        hit = (mask >> s) & 1
        own_ref[jnp.where(hit == 1, count, 8)] = s
        count = count + hit
    width = grad_ref.shape[2] // 2
    lists = Copies(sems)
    for k in range(OWN):
        lists.start(cut(grad_ref, own_ref[k], 0, 2 * width), across_ref.at[k])
    own_slots(Copies(out_sems), inner, me, tab_ref,
              ((grad_ref, 0, width), (grad_ref, width, width)), (grad_ref, 0, width), z_ref)
    lists.wait()


def start_call(me, pair_doc, pair_sample, grad, act):
    rows, width = grad.shape[1:]
    table = jax.ShapeDtypeStruct((16,), jnp.int32)
    return pl.pallas_call(
        start_kernel,
        out_shape=(table, table, table, jax.ShapeDtypeStruct((8, rows, CHUNK), grad.dtype),
                   jax.ShapeDtypeStruct((OWN, rows, width), grad.dtype)),
        in_specs=[SMEM, SMEM, SMEM, ANY, ANY],
        out_specs=(SMEM, SMEM, SMEM, VMEM, VMEM),
        scratch_shapes=[pltpu.SMEM((8,), jnp.int32), pltpu.SemaphoreType.DMA((OWN,)),
                        pltpu.SemaphoreType.DMA((8,))],
        compiler_params=SMALL,
        cost_estimate=CHEAP,
    )(me, pair_doc, pair_sample, grad, act)


def second_kernel(me_ref, tab_ref, own_ref, grad_ref, act_ref, token_ref, z_ref, across_ref, sems, out_sems):
    me = me_ref[0]
    inner = is_inner(me)
    lists = Copies(sems)
    for k in range(OWN):
        lists.start(cut(act_ref, own_ref[k], 0, 2 * CHUNK), across_ref.at[k])
    own_slots(Copies(out_sems), inner, me, tab_ref,
              ((act_ref, 0, CHUNK), (act_ref, CHUNK, CHUNK)), (grad_ref, CHUNK, CHUNK), z_ref)
    lists.wait()


def second_call(me, tab, own, grad, act, token):
    rows = grad.shape[1]

    def buf(k, w):
        return jax.ShapeDtypeStruct((k, rows, w), grad.dtype)

    return pl.pallas_call(
        second_kernel,
        out_shape=(buf(8, CHUNK), buf(OWN, 2 * CHUNK)),
        in_specs=[SMEM, SMEM, SMEM, ANY, ANY, ANY],
        out_specs=(VMEM,) * 2,
        scratch_shapes=[pltpu.SemaphoreType.DMA((OWN,)), pltpu.SemaphoreType.DMA((8,))],
        compiler_params=SMALL,
        cost_estimate=CHEAP,
    )(me, tab, own, grad, act, token)


def third_kernel(me_ref, tab_ref, act_ref, token_ref, z2_ref, z3_ref, out_sems, *, rest):
    me = me_ref[0]
    inner = is_inner(me)
    own_slots(Copies(out_sems), inner, me, tab_ref,
              ((act_ref, 2 * CHUNK, CHUNK), (act_ref, 3 * CHUNK, CHUNK)), (act_ref, 0, CHUNK), z2_ref)
    own_slots(Copies(out_sems), inner, me, tab_ref,
              ((act_ref, 4 * CHUNK, CHUNK), (act_ref, 5 * CHUNK, rest)), (act_ref, CHUNK, CHUNK), z3_ref)


def third_call(me, tab, act, token):
    rows, width = act.shape[1:]
    buf = jax.ShapeDtypeStruct((8, rows, CHUNK), act.dtype)
    return pl.pallas_call(
        functools.partial(third_kernel, rest=width - 5 * CHUNK),
        out_shape=(buf, buf),
        in_specs=[SMEM, SMEM, ANY, ANY],
        out_specs=(VMEM,) * 2,
        scratch_shapes=[pltpu.SemaphoreType.DMA((8,))],
        compiler_params=SMALL,
        cost_estimate=CHEAP,
    )(me, tab, act, token)


def mix_kernel(me_ref, codes_ref, own_ref, came_ref, token_ref, list_ref, sems, *, first, off):
    count, _, width = list_ref.shape

    @pl.when(is_inner(me_ref[0]) == 1)
    def _():
        copies = Copies(sems)
        for k in range(count):
            code = codes_ref[LIST + first + k]
            mine = code < 8
            copies.either(mine, cut(own_ref, jnp.minimum(code, 7), off, width),
                          cut(came_ref, jnp.maximum(code - 8, 0), 0, width), list_ref.at[k])
        copies.wait()


def mix_call(me, codes, own, came, count, first, off, width, token):
    rows = own.shape[1]
    return pl.pallas_call(
        functools.partial(mix_kernel, first=first, off=off),
        out_shape=jax.ShapeDtypeStruct((count, rows, width), own.dtype),
        in_specs=[SMEM, SMEM, ANY, ANY, ANY],
        out_specs=VMEM,
        scratch_shapes=[pltpu.SemaphoreType.DMA((count,))],
        compiler_params=SMALL,
        cost_estimate=CHEAP,
    )(me, codes, own, came, token)


def entry(copies, code, came_over, width, dst):
    early, late_ref, (extra_ref, extra_off) = came_over
    sem = copies.sems.at[copies.used]
    copies.used += 1
    skip = 0 if early is None else OWN

    @pl.when(code >= SENT)
    def _():
        pltpu.make_async_copy(cut(extra_ref, jnp.maximum(code - SENT, 0), extra_off, width), dst, sem).start()

    @pl.when((code >= skip) & (code < SENT))
    def _():
        at = jnp.clip(code - skip, 0, late_ref.shape[0] - 1)
        pltpu.make_async_copy(cut(late_ref, at, 0, width), dst, sem).start()

    if early is not None:
        @pl.when(code < OWN)
        def _():
            pltpu.make_async_copy(cut(early[0], jnp.minimum(code, OWN - 1), early[1], width), dst, sem).start()

    copies.held.append(pltpu.make_async_copy(cut(late_ref, 0, 0, width), dst, sem))


def over(rest, early_off, extra_off):
    early = None if early_off is None else (rest.pop(0), early_off)
    return early, rest.pop(0), (rest.pop(0), extra_off)


def ahead_kernel(own_ref, grad_ref, act_ref, grad_out, act_out, sems):
    copies = Copies(sems)
    for k in range(grad_out.shape[0]):
        copies.start(grad_ref.at[own_ref[OWN + k]], grad_out.at[k])
        copies.start(act_ref.at[own_ref[OWN + k]], act_out.at[k])
    copies.wait()


def ahead_call(count, own, grad, act):
    return pl.pallas_call(
        ahead_kernel,
        out_shape=tuple(jax.ShapeDtypeStruct((count,) + x.shape[1:], x.dtype) for x in (grad, act)),
        in_specs=[SMEM, ANY, ANY],
        out_specs=(VMEM, VMEM),
        scratch_shapes=[pltpu.SemaphoreType.DMA((2 * count,))],
        compiler_params=SMALL,
        cost_estimate=CHEAP,
    )(own, grad, act)


def forward_kernel(me_ref, codes_ref, *rest, offs, ahead):
    rest = list(rest)
    came_over = over(rest, *offs)
    ahead_ref, token_ref, z_ref, sems = rest
    inner = is_inner(me_ref[0])
    width = came_over[1].shape[2]

    @pl.when(inner == 1)
    def _():
        copies = Copies(sems)
        for k in range(2 * CAP):
            entry(copies, codes_ref[STRAIGHT + k], came_over, width, cut(z_ref, k, 0, width))
            entry(copies, codes_ref[DIAG + k], came_over, width, cut(z_ref, 2 * CAP + k, 0, width))
        copies.wait()

    if ahead is not None:
        @pl.when(inner == 0)
        def _():
            copies = Copies(sems)
            off, some = ahead
            for s in range(8):
                copies.start(cut(ahead_ref, s, off, some), cut(z_ref, s, 0, some))
            copies.wait()


def forward_call(me, codes, arrays, offs, ahead_array, ahead, token):
    late = arrays[-2]
    rows, width = late.shape[1:]
    args = [me, codes, *arrays, ahead_array, token]
    return pl.pallas_call(
        functools.partial(forward_kernel, offs=offs, ahead=ahead),
        out_shape=jax.ShapeDtypeStruct((8, rows, width), late.dtype),
        in_specs=[SMEM, SMEM] + [ANY] * (len(args) - 2),
        out_specs=VMEM,
        scratch_shapes=[pltpu.SemaphoreType.DMA((8,))],
        compiler_params=SMALL,
        cost_estimate=CHEAP,
    )(*args)


def side_kernel(me_ref, codes_ref, tab_ref, sample_ref, came_ref, *rest, offs, off, part):
    rest = list(rest)
    came_over = over(rest, *offs)
    own_ref, far_ref, token_ref, side_ref, sems, role_sems = rest
    me = me_ref[0]
    inner = is_inner(me)
    width = side_ref.shape[2]
    mine = Copies(sems)
    for r in range(CAP):
        mine.start(cut(sample_ref, tab_ref[(me ^ 1) * CAP + r], off, width), side_ref.at[r])

    @pl.when(inner == 1)
    def _():
        copies = Copies(role_sems)
        for k in range(CAP):
            copies.start(cut(came_ref, codes_ref[SIDE + k], 0, width), side_ref.at[CAP + k])
        for k in range(CAP, 3 * CAP):
            entry(copies, codes_ref[SIDE + k], came_over, width, side_ref.at[CAP + k])
        copies.wait()

    @pl.when(inner == 0)
    def _():
        copies = Copies(role_sems)
        for k in range(CAP):
            copies.start(cut(own_ref, part * 2 * CAP + CAP + k, 0, width), side_ref.at[CAP + k])
        for k in range(2 * CAP):
            copies.start(cut(far_ref, 2 * CAP + k, 0, width), side_ref.at[2 * CAP + k])
        copies.wait()

    mine.wait()


def side_call(me, codes, tab, sample, came, arrays, offs, own, far, off, part, token):
    late = arrays[-2]
    rows, width = late.shape[1:]
    args = [me, codes, tab, sample, came, *arrays, own, far, token]
    return pl.pallas_call(
        functools.partial(side_kernel, offs=offs, off=off, part=part),
        out_shape=jax.ShapeDtypeStruct((4 * CAP, rows, width), late.dtype),
        in_specs=[SMEM, SMEM, SMEM] + [ANY] * (len(args) - 3),
        out_specs=VMEM,
        scratch_shapes=[pltpu.SemaphoreType.DMA((CAP,)), pltpu.SemaphoreType.DMA((3 * CAP,))],
        compiler_params=SMALL,
        cost_estimate=CHEAP,
    )(*args)


def gram_kernel(me_ref, codes_ref, own_ref, came_ref, *rest, offs, off, part, mode, last, tensor):
    rest = list(rest)
    came_over = over(rest, *offs)
    partner_ref, far_ref, side_ref, doc_ref, token_ref = rest[:5]
    rest = rest[5:]
    held = [rest.pop(0) for _ in range({"first": 0, "next": 1, "score": 3}[mode])]
    out_ref, rows_ref, cols_ref, acc_ref, doc_sem, sems, role_sems = rest
    me = me_ref[0]
    inner = is_inner(me)
    rows = own_ref.shape[1]
    width = rows_ref.shape[1]
    docs = pltpu.make_async_copy(doc_ref.at[0, :, pl.ds(off, width)], cols_ref, doc_sem.at[0])
    docs.start()

    def slot(k):
        return rows_ref.at[pl.ds(k * rows, rows), :]

    copies = Copies(sems)
    for r in range(CAP):
        copies.start(cut(own_ref, codes_ref[SLOTS + r], off, width), slot(r))
    for k in range(4 * CAP):
        copies.start(side_ref.at[k], slot(4 * CAP + k))

    @pl.when(inner == 1)
    def _():
        more = Copies(role_sems)
        for r in range(CAP):
            more.start(cut(came_ref, codes_ref[SLOTS + CAP + r], 0, width), slot(CAP + r))
        for k in range(2 * CAP, 4 * CAP):
            entry(more, codes_ref[SLOTS + k], came_over, width, slot(k))
        more.wait()

    @pl.when(inner == 0)
    def _():
        more = Copies(role_sems)
        for r in range(CAP):
            more.start(cut(partner_ref, part * 2 * CAP + r, 0, width), slot(CAP + r))
        for k in range(2 * CAP):
            more.start(cut(far_ref, k, 0, width), slot(2 * CAP + k))
        more.wait()

    copies.wait()
    docs.wait()
    step = 256
    if mode == "score":
        acc_ref[...] = held[2][...]

    def block(n, _):
        at = pl.ds(pl.multiple_of(n * step, step), step)
        part = lax.dot_general(
            rows_ref[...], cols_ref[at, :], (((1,), (1,)), ((), ())), preferred_element_type=jnp.float32
        )
        if mode == "first":
            out_ref[:, at] = part
        elif mode == "next":
            out_ref[:, at] = held[0][:, at] + part
        else:
            both = part * (held[0][:, at] + held[1][:, at])
            acc_ref[...] += jnp.sum(both.reshape(8 * CAP, rows, step), axis=1)
        return 0

    lax.fori_loop(0, SEQ_D // step, block, 0)
    if mode == "score" and not last:
        out_ref[...] = acc_ref[...]
    if last:
        total = jnp.sum(acc_ref[...], axis=1, keepdims=True)
        near = jnp.where(inner == 1, me ^ 6, me ^ 4)
        far = jnp.where(inner == 1, me ^ 4, me ^ 6)
        for k, owner in enumerate((me, me ^ 2, near, far, me ^ 1, me ^ 3, near ^ 1, far ^ 1)):
            for t in range(tensor):
                out_ref[owner * tensor + t] = jnp.broadcast_to(total[k * CAP : (k + 1) * CAP], (CAP, 128))


def gram_call(me, codes, own, came, arrays, offs, partner, far, side, doc, off, part, token, mode, held,
              last, tensor):
    late = arrays[-2]
    rows, width = late.shape[1:]
    tokens = doc.shape[1]
    total = 8 * CAP * rows
    args = [me, codes, own, came, *arrays, partner, far, side, doc, token]
    if last:
        out = jax.ShapeDtypeStruct((8 * tensor, CAP, 128), jnp.float32)
    elif mode == "score":
        out = jax.ShapeDtypeStruct((8 * CAP, 256), jnp.float32)
    else:
        out = jax.ShapeDtypeStruct((total, tokens), jnp.float32)
    return pl.pallas_call(
        functools.partial(gram_kernel, offs=offs, off=off, part=part, mode=mode, last=last, tensor=tensor),
        out_shape=out,
        in_specs=[SMEM, SMEM] + [ANY] * (len(args) - 2) + [VMEM] * len(held),
        out_specs=VMEM,
        scratch_shapes=[
            pltpu.VMEM((total, width), doc.dtype),
            pltpu.VMEM((tokens, width), doc.dtype),
            pltpu.VMEM((8 * CAP, 256), jnp.float32),
            pltpu.SemaphoreType.DMA((1,)),
            pltpu.SemaphoreType.DMA((5 * CAP,)),
            pltpu.SemaphoreType.DMA((3 * CAP,)),
        ],
        compiler_params=pltpu.CompilerParams(vmem_limit_bytes=16 * 1024 * 1024),
        cost_estimate=CHEAP,
    )(*args, *held)


def finish_kernel(came_ref, place_ref, out_ref, *, tensor):
    factor = 1.0 / jnp.sqrt(jnp.float32(FF) * jnp.float32(D) * jnp.float32(SEQ_S) * jnp.float32(SEQ_D))
    for p in range(8 * CAP):
        slot = place_ref[p]
        doc, r = slot // CAP, slot % CAP
        total = came_ref[doc * tensor, r, 0]
        for t in range(1, tensor):
            total = total + came_ref[doc * tensor + t, r, 0]
        out_ref[p] = total * factor


def chain(sample_act, sample_grad, doc_act, doc_grad, pair_doc, pair_sample):
    groups, tensor = lax.axis_size("groups"), lax.axis_size("tensor")
    me = jnp.stack([lax.axis_index("docs"), lax.axis_index("groups")]).astype(jnp.int32)
    chunks = [(True, 0, CHUNK), (True, CHUNK, CHUNK)] + [(False, i * CHUNK, CHUNK) for i in range(5)]
    chunks.append((False, 5 * CHUNK, sample_act.shape[2] - 5 * CHUNK))
    total = len(chunks)
    send = lambda x, pairs: lax.ppermute(x, "docs", pairs)
    tab, place, own, z, across = start_call(me, pair_doc, pair_sample, sample_grad, sample_act)
    z0 = send(z, OVER_Z)
    early_grad = send(across, ACROSS)
    z, across = second_call(me, tab, own, sample_grad, sample_act, z)
    z1 = send(z, OVER_Z)
    early_act = send(across, ACROSS)
    tables = lax.all_to_all(
        jnp.broadcast_to(tab[None, :], (groups * 8, 8 * CAP)), ("groups", "docs"), 0, 0, tiled=True
    )
    codes = codes_call(me, tables, groups)

    def send_extras(count):
        if count == 0:
            return tuple(jnp.zeros((EXTRAS[-1],) + x.shape[1:], x.dtype) for x in (sample_grad, sample_act))
        sent = [send(x, ACROSS) for x in ahead_call(count, own, sample_grad, sample_act)]
        return tuple(jnp.pad(x, ((0, EXTRAS[-1] - count), (0, 0), (0, 0))) for x in sent)

    extras = lax.switch(codes[BRANCH], [functools.partial(send_extras, c) for c in EXTRAS])

    ahead_of = [z0, z1]
    main, late, sides = {}, {}, {}
    state = dict(grads=None, score=None)

    def came(i):
        return ahead_of[i] if i < LEAD else main[i - LEAD]

    def sample(i):
        return sample_grad if chunks[i][0] else sample_act

    def over_arrays(i):
        is_grad, off, _ = chunks[i]
        extra = extras[0 if is_grad else 1]
        if i >= LEAD:
            return [late[i], extra], (None, off)
        return [early_grad if is_grad else early_act, late[i], extra], (off, off)

    def mix(i, token):
        _, off, w = chunks[i]
        first = OWN if i < LEAD else 0
        out = mix_call(me, codes, sample(i), came(i), MAIN - first, first, off, w, token)
        late[i] = send(out, ACROSS)
        return out

    def forward(i, token):
        ahead = chunks[i + LEAD][1:] if i + LEAD < total else None
        out = forward_call(me, codes, *over_arrays(i), sample_act, ahead, token)
        main[i] = send(out, OVER_Z)
        return out

    def side(i, token):
        out = side_call(me, codes, tab, sample(i), came(i), *over_arrays(i), ahead_of[i // 2], main[i],
                        chunks[i][1], i % 2, token)
        sides[i] = send(out, OVER_Y)
        return out

    def gram(i, token):
        is_grad, off, w = chunks[i]
        last = i == total - 1
        if is_grad:
            held = [] if i == 0 else [state["grads"]]
            mode = "next" if held else "first"
        else:
            held, mode = [*state["grads"], state["score"]], "score"
        out = gram_call(
            me, codes, sample(i), came(i), *over_arrays(i), ahead_of[i // 2], main[i],
            sides[i], doc_grad if is_grad else doc_act, off, i % 2, token, mode, held, last, tensor,
        )
        if not is_grad:
            state["score"] = out
        elif chunks[i + 1][0]:
            state["grads"] = out
        else:
            state["grads"] = (out, lax.psum(out, "tensor") - out if tensor != 2 else lax.ppermute(
                out, "tensor", [(0, 1), (1, 0)]
            ))
            state["score"] = jnp.zeros((8 * CAP, 256), jnp.float32)
        return out

    token = mix(0, codes)
    z2, z3 = third_call(me, tab, sample_act, token)
    ahead_of.append(send(z2, OVER_Z))
    ahead_of.append(send(z3, OVER_Z))
    token = z2
    for i in range(total + 2):
        if i + 1 < total:
            token = mix(i + 1, token)
        if i < total:
            token = forward(i, token)
        if i >= 2:
            token = gram(i - 2, token)
        if 1 <= i < total + 1:
            token = side(i - 1, token)
    back = lax.all_to_all(state["score"], ("docs", "tensor"), 0, 0, tiled=True)
    return pl.pallas_call(
        functools.partial(finish_kernel, tensor=tensor),
        out_shape=jax.ShapeDtypeStruct((8 * CAP,), jnp.float32),
        in_specs=[SMEM, SMEM],
        out_specs=SMEM,
        compiler_params=SMALL,
        cost_estimate=CHEAP,
    )(back, place)


def codes_kernel(me_ref, all_ref, out_ref, scratch, masks, *, groups):
    group, me = me_ref[1], me_ref[0]
    base = group * 8

    def owner_mask(row, _):
        first = jnp.where((row & 7) < 4, 8, 0)
        mask = jnp.int32(0)
        for j in range(8):
            mask = mask | jnp.left_shift(1, all_ref[row, first + j])
        masks[row] = mask
        return 0

    lax.fori_loop(0, groups * 8, owner_mask, 0)

    def longest(k, best):
        row = (k >> 2) * 8 + 2 + (k & 3)
        return jnp.maximum(best, jnp.maximum(bits(masks[row]), OWN) + bits(masks[row ^ 2]))

    best = lax.fori_loop(0, groups * 4, longest, jnp.int32(0))
    branch = jnp.int32(0)
    for c in EXTRAS[:-1]:
        branch = branch + (best > MAIN + c).astype(jnp.int32)
    for i in range(CODES):
        out_ref[i] = 0
    for i in range(32):
        scratch[i] = 0
    out_ref[BRANCH] = branch
    inner = is_inner(me)
    mine, partner = masks[base + me], masks[base + (me ^ 2)]
    count = jnp.int32(0)
    for s in range(8):
        hit = (mine >> s) & 1
        scratch[jnp.where(hit == 1, count, 31)] = s
        count = count + hit
    count = jnp.maximum(count, OWN)
    for s in range(8):
        hit = (partner >> s) & 1
        scratch[jnp.where(hit == 1, count, 31)] = 8 + s
        count = count + hit
    need = jnp.maximum(count - MAIN, 0)
    for k in range(MAIN):
        out_ref[LIST + k] = scratch[k if k < OWN else k + need]
    far, far_outer = masks[base + (me ^ 6)], masks[base + (me ^ 4)]
    after = jnp.maximum(bits(far), OWN)
    extra = jnp.maximum(after + bits(far_outer) - MAIN, 0)

    def place(near, doc, r):
        owner = base + ((me ^ 6) if near else (me ^ 4))
        sample = all_ref[owner, doc * CAP + r]
        below = jnp.left_shift(1, sample) - 1
        if near:
            at = bits(far & below)
            at = jnp.where(at < OWN, at, jnp.where(at < OWN + extra, at - OWN + SENT, at - extra))
        else:
            at = after + bits(far_outer & below) - extra
        return at * inner

    for r in range(CAP):
        out_ref[STRAIGHT + r] = place(True, me ^ 2, r)
        out_ref[STRAIGHT + CAP + r] = place(False, me ^ 2, r)
        out_ref[DIAG + r] = place(True, me ^ 3, r)
        out_ref[DIAG + CAP + r] = place(False, me ^ 3, r)
        out_ref[SIDE + r] = all_ref[base + (me ^ 2), (me ^ 1) * CAP + r]
        out_ref[SIDE + CAP + r] = place(True, me ^ 1, r)
        out_ref[SIDE + 2 * CAP + r] = place(False, me ^ 1, r)
        out_ref[SLOTS + r] = all_ref[base + me, me * CAP + r]
        out_ref[SLOTS + CAP + r] = all_ref[base + (me ^ 2), me * CAP + r]
        out_ref[SLOTS + 2 * CAP + r] = place(True, me, r)
        out_ref[SLOTS + 3 * CAP + r] = place(False, me, r)


def codes_call(me, tables, groups):
    return pl.pallas_call(
        functools.partial(codes_kernel, groups=groups),
        out_shape=jax.ShapeDtypeStruct((CODES,), jnp.int32),
        in_specs=[SMEM, SMEM],
        out_specs=SMEM,
        scratch_shapes=[pltpu.SMEM((32,), jnp.int32), pltpu.SMEM((groups * 8,), jnp.int32)],
        compiler_params=SMALL,
        cost_estimate=CHEAP,
    )(me, tables)


def direct(sample_act, sample_grad, doc_act, doc_grad, pair_doc, pair_sample):
    owners = lax.axis_size("docs")
    pair_count = pair_doc.shape[0]
    slot_count = owners * CAP
    factor = 1.0 / jnp.sqrt(
        jnp.float32(FF) * jnp.float32(D) * jnp.float32(SEQ_S) * jnp.float32(SEQ_D)
    )
    target = pair_doc[:, 0]
    order = jnp.arange(pair_count, dtype=jnp.int32)
    earlier = (target[:, None] == target[None, :]) & (order[None, :] < order[:, None])
    rank = jnp.sum(earlier.astype(jnp.int32), axis=1)
    slot_of_pair = target * CAP + rank
    chosen = (jnp.arange(slot_count, dtype=jnp.int32)[:, None] == slot_of_pair[None, :]).astype(
        jnp.int32
    )
    slot_sample = jnp.sum(chosen * pair_sample[None, :], axis=1)
    send_act = sample_act[slot_sample]
    send_grad = sample_grad[slot_sample]
    send_act = send_act.reshape(owners, CAP, send_act.shape[1], send_act.shape[2])
    send_grad = send_grad.reshape(owners, CAP, send_grad.shape[1], send_grad.shape[2])
    grad_in = lax.all_to_all(send_grad, "docs", split_axis=0, concat_axis=0, tiled=True)
    act_in = lax.all_to_all(send_act, "docs", split_axis=0, concat_axis=0, tiled=True)
    grad_gram = jnp.einsum("nmsf,tf->nmst", grad_in, doc_grad[0], preferred_element_type=jnp.float32)
    grad_sum = lax.psum(grad_gram, "tensor")
    act_gram = jnp.einsum("nmsf,tf->nmst", act_in, doc_act[0], preferred_element_type=jnp.float32)
    scores = lax.psum(jnp.sum(act_gram * grad_sum, axis=(2, 3)) * factor, "tensor")
    returned = lax.all_to_all(scores, "docs", split_axis=0, concat_axis=0, tiled=True)
    flat_scores = returned.reshape(slot_count)
    return jnp.sum(jnp.where(chosen > 0, flat_scores[:, None], 0.0), axis=0)


def solution(mesh):
    in_specs = (
        P(("groups", "docs"), None, "tensor"),
        P(("groups", "docs"), None, "tensor"),
        P(("groups", "docs"), None, "tensor"),
        P(("groups", "docs"), None, "tensor"),
        P(("groups", "docs"), None),
        P(("groups", "docs")),
    )
    out_specs = P(("groups", "docs"))

    def per_device(sample_act, sample_grad, doc_act, doc_grad, pair_doc, pair_sample):
        fits = (
            mesh.shape["docs"] == 8
            and mesh.shape["tensor"] == 2
            and pair_doc.shape[0] == 8 * CAP
            and sample_act.shape[0] == 8
            and sample_grad.shape[2] == 2 * CHUNK
            and 5 * CHUNK < sample_act.shape[2] <= 6 * CHUNK
        )
        run = chain if fits else direct
        return run(sample_act, sample_grad, doc_act, doc_grad, pair_doc, pair_sample)

    return jax.shard_map(
        per_device, mesh=mesh, in_specs=in_specs, out_specs=out_specs, check_vma=False
    )
```

time: 256 us -> 217 us (0.85)
  waiting for transfers between devices: 179 us -> 89.7 us
  Pallas kernels: 0 us -> 60.3 us
  starting transfers between devices: 12 us -> 48.6 us
  matrix products: 15.4 us -> 0 us
  other arithmetic: 14.5 us -> 0.08 us
  between operations: 13.4 us -> 1.42 us
  local copies, waits for them, and re-layouts: 9.32 us -> 5.73 us
    all_to_all x2 -> x1, waiting for transfers between devices: 156 us -> 1.6 us  [chain(): lax.all_to_all(jnp.broadcast_to(tab[None, :], (groups * 8, 8 * CAP)), ('g...]
    ppermute x0 -> x31, waiting for transfers between devices: none -> 88.1 us  [the longest x30 88.1 us: chain(): send = lambda x, pairs: lax.ppermute(x, 'docs', pairs)]
    pallas_call x0 -> x37, Pallas kernels: none -> 60.3 us  [the longest x8 27.7 us: gram_call(): pl.pallas_call(functools.partial(gram_kernel, offs=offs, off=off, part=pa...]
    ppermute x0 -> x31, starting transfers between devices: none -> 42.8 us  [the longest x30 42.7 us: chain(): send = lambda x, pairs: lax.ppermute(x, 'docs', pairs)]
    psum x1 -> x0, waiting for transfers between devices: 22.5 us -> none  [per_device(): act_sum, grad_sum = lax.psum((act_gram, grad_gram), 'tensor')]
    dot_general x2 -> x0, matrix products: 15.4 us -> none  [the longest x1 10.9 us: per_device(): jnp.einsum('nmsf,tf->nmst', act_in, doc_rows, preferred_element_type=jnp....]
    select_n x3 -> x0, other arithmetic: 8.68 us -> none  [the longest x1 5.58 us: per_device(): jnp.where(live[:, None, None], sample_act[slot_sample], jnp.zeros((), jnp...]
    gather x2 -> x0, local copies, waits for them, and re-layouts: 8.64 us -> none  [the longest x1 5.38 us: per_device(): sample_act[slot_sample]]
  transfers between devices with their start and end apart: 3 -> 32, of which waited for: 3 -> 13; matrix products, arithmetic and copies ran while one was open for 6% -> 2% of each run, Pallas kernels for 0% -> 22%
where the time goes in v2:
time: 217 us; the launch traced here: 216 us
  waiting for transfers between devices  89.7 us (41%)
  Pallas kernels  60.3 us (28%)
  starting transfers between devices  48.6 us (22%)
  blocking collectives  10.1 us (5%)
  local copies, waits for them, and re-layouts  5.73 us (3%)
    ppermute x30, waiting for transfers between devices, chain(): send = lambda x, pairs: lax.ppermute(x, 'docs', pairs)  88.1 us
    ppermute x30, starting transfers between devices, chain(): send = lambda x, pairs: lax.ppermute(x, 'docs', pairs)  42.7 us
    pallas_call x8, Pallas kernels, gram_call(): pl.pallas_call(functools.partial(gram_kernel, offs=offs, off=off, part=pa...  27.7 us
    all_to_all x1, blocking collectives, chain(): back = lax.all_to_all(state['score'], ('docs', 'tensor'), 0, 0, tiled=True)  10.1 us
    pallas_call x8, Pallas kernels, side_call(): pl.pallas_call(functools.partial(side_kernel, offs=offs, off=off, part=pa...  9.27 us
    all_to_all x1, starting transfers between devices, chain(): lax.all_to_all(jnp.broadcast_to(tab[None, :], (groups * 8, 8 * CAP)), ('g...  5.85 us
    pallas_call x8, Pallas kernels, forward_call(): pl.pallas_call(functools.partial(forward_kernel, offs=offs, ahead=ahead),...  5.8 us
    pallas_call x8, Pallas kernels, mix_call(): pl.pallas_call(functools.partial(mix_kernel, first=first, off=off), out_s...  5.14 us
  transfers between devices with their start and end apart: 32, of which 13 were waited for; matrix products, arithmetic and copies ran while one was open for 2% of the time, Pallas kernels for 22%

profile of v2, /device:TPU:0, one launch (start us, length us, event | category | flops | bytes accessed | tf_op | source)
XLA Modules:
  0.0 216.0 jit_solution(2086143457298346699)
XLA Ops:
  1.5 3.0 %shard_map.64 = (s32[16]{0:T(128)S(1)}, s32[16]{0:T(128)S(1)}, s32[16]{0:T(128)S(1)}, bf16[8,32,1024]{2,1,0:T(8,128)(2,1)S(1)}, bf16[4,32,2048]{2,1,0:T(8,128)(2,1)}) custom-call(s32[2]{0:T(128)S(1)} %pad_add_fusion.me_ref, s32[16,1]{1,0:T(8,128)S(1)} %copy.8.doc_ref, s32[16]{0:T(128)S(1)} %copy-done.1, bf16[8,32,2048]{2,1,0:T(8,128)(2,1)} %own_ref.22, ...), custom_call_target="tpu_custom_call" | custom-call | bytes 1024 | tf_op jit(solution)/shard_map/pallas_call | solution.py:140
  4.5 3.1 %collective-permute-start.7 = (bf16[8,32,1024]{2,1,0:T(8,128)(2,1)S(1)}, bf16[8,32,1024]{2,1,0:T(8,128)(2,1)S(1)}, u32[]{:S(2)}, u32[]{:S(2)}) collective-permute-start(bf16[8,32,1024]{2,1,0:T(8,128)(2,1)S(1)} %get-tuple-element.51.token_ref), channel_id=1, source_target_pairs={{0,4},{2,6},{4,0},{6,2},{8,12},{10,14},{12,8},{14,10},{1,5},{3,7},... | collective-permute-start | bytes 1572872 | tf_op jit(solution)/shard_map/ppermute | solution.py:487
  8.2 5.8 %all-to-all-start = ((s32[16,1,16]{2,1,0:T(1,128)}), s32[16,1,16]{2,1,0:T(1,128)S(1)}, u32[]{:S(2)}, u32[]{:S(2)}) async-start(s32[16,1,16]{2,1,0:T(1,128)} %broadcast_in_dim.4), calls=%async_computation | async-start | bytes 16384 | tf_op jit(solution)/shard_map/all_to_all | solution.py:494
  14.7 2.7 %shard_map.66 = (bf16[8,32,1024]{2,1,0:T(8,128)(2,1)}, bf16[4,32,2048]{2,1,0:T(8,128)(2,1)S(1)}) custom-call(s32[2]{0:T(128)S(1)} %pad_add_fusion.me_ref, s32[16]{0:T(128)S(1)} %get-tuple-element.49.tab_ref, s32[16]{0:T(128)S(1)} %get-tuple-element.50.own_ref, bf16[8,32,2048]{2,1,0:T(8,128)(2,1)} %own_ref.22, bf16[8,32,5504]{2,1,0:T(8,128)(2,1)} %own_ref.31, ...), custom_call_target="tpu_custom_call" | custom-call | bytes 1024 | tf_op jit(solution)/shard_map/pallas_call | solution.py:170
  17.4 4.7 %collective-permute-start.11 = (bf16[8,32,1024]{2,1,0:T(8,128)(2,1)}, bf16[8,32,1024]{2,1,0:T(8,128)(2,1)S(1)}, u32[]{:S(2)}, u32[]{:S(2)}) collective-permute-start(bf16[8,32,1024]{2,1,0:T(8,128)(2,1)} %get-tuple-element.56), channel_id=1, source_target_pairs={{0,4},{2,6},{4,0},{6,2},{8,12},{10,14},{12,8},{14,10},{1,5},{3,7},... | collective-permute-start | bytes 1572872 | tf_op jit(solution)/shard_map/ppermute | solution.py:487
  22.1 1.6 all-to-all-done
  23.7 2.1 shard_map.65.codes_ref.token_ref
  28.4 2.1 conditional.1
  29.3 1.2 broadcast.8
  30.5 3.0 %shard_map.68 = (bf16[8,32,1024]{2,1,0:T(8,128)(2,1)S(1)}, bf16[8,32,1024]{2,1,0:T(8,128)(2,1)S(1)}) custom-call(s32[2]{0:T(128)S(1)} %pad_add_fusion.me_ref, s32[16]{0:T(128)S(1)} %get-tuple-element.49.tab_ref, bf16[8,32,5504]{2,1,0:T(8,128)(2,1)} %own_ref.31, bf16[8,32,1024]{2,1,0:T(8,128)(2,1)S(1)} %shard_map.67.token_ref), custom_call_target="tpu_custom_call" | custom-call | bytes 1024 | tf_op jit(solution)/shard_map/pallas_call | solution.py:193
  33.6 3.6 %collective-permute-start.14 = (bf16[8,32,1024]{2,1,0:T(8,128)(2,1)S(1)}, bf16[8,32,1024]{2,1,0:T(8,128)(2,1)S(1)}, u32[]{:S(2)}, u32[]{:S(2)}) collective-permute-start(bf16[8,32,1024]{2,1,0:T(8,128)(2,1)S(1)} %get-tuple-element.57.token_ref), channel_id=1, source_target_pairs={{0,4},{2,6},{4,0},{6,2},{8,12},{10,14},{12,8},{14,10},{1,5},{3,7},... | collective-permute-start | bytes 1572872 | tf_op jit(solution)/shard_map/ppermute | solution.py:487
  39.4 4.7 %collective-permute-start.12 = (bf16[8,32,1024]{2,1,0:T(8,128)(2,1)S(1)}, bf16[8,32,1024]{2,1,0:T(8,128)(2,1)S(1)}, u32[]{:S(2)}, u32[]{:S(2)}) collective-permute-start(bf16[8,32,1024]{2,1,0:T(8,128)(2,1)S(1)} %shard_map.70.token_ref), channel_id=1, source_target_pairs={{0,4},{2,6},{4,0},{6,2},{8,12},{10,14},{12,8},{14,10},{1,5},{3,7},... | collective-permute-start | bytes 1572872 | tf_op jit(solution)/shard_map/ppermute | solution.py:487
  44.8 2.8 %collective-permute-start.8 = (bf16[8,32,1024]{2,1,0:T(8,128)(2,1)S(1)}, bf16[8,32,1024]{2,1,0:T(8,128)(2,1)S(1)}, u32[]{:S(2)}, u32[]{:S(2)}) collective-permute-start(bf16[8,32,1024]{2,1,0:T(8,128)(2,1)S(1)} %get-tuple-element.53), channel_id=1, source_target_pairs={{0,4},{2,6},{4,0},{6,2},{8,12},{10,14},{12,8},{14,10},{1,5},{3,7},... | collective-permute-start | bytes 1572872 | tf_op jit(solution)/shard_map/ppermute | solution.py:487
  47.6 2.5 %collective-permute-done.14.came_ref.rest_2_ = bf16[8,32,1024]{2,1,0:T(8,128)(2,1)S(1)} collective-permute-done((bf16[8,32,1024]{2,1,0:T(8,128)(2,1)S(1)}, bf16[8,32,1024]{2,1,0:T(8,128)(2,1)S(1)}, u32[]{:S(2)}, u32[]{:S(2)}) %collective-permute-start.14) | collective-permute-done | bytes 524320 | tf_op jit(solution)/shard_map/ppermute | solution.py:487
  52.3 8.9 %collective-permute-done.12.rest_4_.came_ref = bf16[8,32,1024]{2,1,0:T(8,128)(2,1)S(1)} collective-permute-done((bf16[8,32,1024]{2,1,0:T(8,128)(2,1)S(1)}, bf16[8,32,1024]{2,1,0:T(8,128)(2,1)S(1)}, u32[]{:S(2)}, u32[]{:S(2)}) %collective-permute-start.12) | collective-permute-done | bytes 524320 | tf_op jit(solution)/shard_map/ppermute | solution.py:487
  61.3 1.2 shard_map.73.token_ref
  63.0 1.9 collective-permute-start.16
  65.0 7.5 %collective-permute-done.8.came_ref.rest_2_ = bf16[8,32,1024]{2,1,0:T(8,128)(2,1)S(1)} collective-permute-done((bf16[8,32,1024]{2,1,0:T(8,128)(2,1)S(1)}, bf16[8,32,1024]{2,1,0:T(8,128)(2,1)S(1)}, u32[]{:S(2)}, u32[]{:S(2)}) %collective-permute-start.8) | collective-permute-done | bytes 524320 | tf_op jit(solution)/shard_map/ppermute | solution.py:487
  75.8 3.6 %shard_map.76.rest_5_.rest_8_ = f32[512,768]{1,0:T(8,128)S(1)} custom-call(s32[2]{0:T(128)S(1)} %pad_add_fusion.me_ref, s32[64]{0:T(128)S(1)} %shard_map.65.codes_ref.token_ref, bf16[8,32,2048]{2,1,0:T(8,128)(2,1)S(1)} %copy-done.4, bf16[8,32,1024]{2,1,0:T(8,128)(2,1)S(1)} %collective-permute-done.7.came_ref.rest_3_, ...), custom_call_target="tpu_custom_call" | custom-call | bytes 1024 | tf_op jit(solution)/shard_map/pallas_call | solution.py:452
  79.4 2.0 collective-permute-done.16.rest_4_.came_ref
  84.5 9.7 %collective-permute-done.22.rest_5_ = bf16[8,32,1024]{2,1,0:T(8,128)(2,1)S(1)} collective-permute-done((bf16[8,32,1024]{2,1,0:T(8,128)(2,1)S(1)}, bf16[8,32,1024]{2,1,0:T(8,128)(2,1)S(1)}, u32[]{:S(2)}, u32[]{:S(2)}) %collective-permute-start.22) | collective-permute-done | bytes 524320 | tf_op jit(solution)/shard_map/ppermute | solution.py:487
  94.2 3.6 %shard_map.80.rest_5_.rest_8_.rest_7_ = f32[512,768]{1,0:T(8,128)S(1)} custom-call(s32[2]{0:T(128)S(1)} %pad_add_fusion.me_ref, s32[64]{0:T(128)S(1)} %shard_map.65.codes_ref.token_ref, bf16[8,32,2048]{2,1,0:T(8,128)(2,1)S(1)} %copy-done.4, bf16[8,32,1024]{2,1,0:T(8,128)(2,1)S(1)} %collective-permute-done.11.came_ref.rest_3_, ...), custom_call_target="tpu_custom_call" | custom-call | bytes 1024 | tf_op jit(solution)/shard_map/pallas_call | solution.py:452
  97.9 1.5 collective-permute-start.21
  100.1 12.1 %collective-permute-done.21.rest_4_.came_ref = bf16[8,32,1024]{2,1,0:T(8,128)(2,1)S(1)} collective-permute-done((bf16[8,32,1024]{2,1,0:T(8,128)(2,1)S(1)}, bf16[8,32,1024]{2,1,0:T(8,128)(2,1)S(1)}, u32[]{:S(2)}, u32[]{:S(2)}) %collective-permute-start.21) | collective-permute-done | bytes 524320 | tf_op jit(solution)/shard_map/ppermute | solution.py:487
  112.2 1.2 shard_map.81.token_ref
  114.0 1.7 collective-permute-start.19
  117.7 9.3 %collective-permute-done.24.rest_5_ = bf16[8,32,1024]{2,1,0:T(8,128)(2,1)S(1)} collective-permute-done((bf16[8,32,1024]{2,1,0:T(8,128)(2,1)S(1)}, bf16[8,32,1024]{2,1,0:T(8,128)(2,1)S(1)}, u32[]{:S(2)}, u32[]{:S(2)}) %collective-permute-start.24) | collective-permute-done | bytes 524320 | tf_op jit(solution)/shard_map/ppermute | solution.py:487
  127.1 3.6 %shard_map.84.rest_5_.rest_10_ = f32[16,256]{1,0:T(8,128)S(1)} custom-call(s32[2]{0:T(128)S(1)} %pad_add_fusion.me_ref, s32[64]{0:T(128)S(1)} %shard_map.65.codes_ref.token_ref, bf16[8,32,5504]{2,1,0:T(8,128)(2,1)S(1)} %copy-done.2, bf16[8,32,1024]{2,1,0:T(8,128)(2,1)S(1)} %collective-permute-done.14.came_ref.rest_2_, ...), custom_call_target="tpu_custom_call" | custom-call | bytes 1024 | tf_op jit(solution)/shard_map/pallas_call | solution.py:452
  130.7 1.2 shard_map.85.token_ref
  132.4 1.6 collective-permute-start.23
  136.1 8.5 %collective-permute-done.26.rest_5_ = bf16[8,32,1024]{2,1,0:T(8,128)(2,1)S(1)} collective-permute-done((bf16[8,32,1024]{2,1,0:T(8,128)(2,1)S(1)}, bf16[8,32,1024]{2,1,0:T(8,128)(2,1)S(1)}, u32[]{:S(2)}, u32[]{:S(2)}) %collective-permute-start.26) | collective-permute-done | bytes 524320 | tf_op jit(solution)/shard_map/ppermute | solution.py:487
  144.6 3.6 %shard_map.88.rest_4_.rest_9_ = f32[16,256]{1,0:T(8,128)S(1)} custom-call(s32[2]{0:T(128)S(1)} %pad_add_fusion.me_ref, s32[64]{0:T(128)S(1)} %shard_map.65.codes_ref.token_ref, bf16[8,32,5504]{2,1,0:T(8,128)(2,1)S(1)} %copy-done.2, bf16[8,32,1024]{2,1,0:T(8,128)(2,1)S(1)} %collective-permute-done.8.came_ref.rest_2_, ...), custom_call_target="tpu_custom_call" | custom-call | bytes 1024 | tf_op jit(solution)/shard_map/pallas_call | solution.py:452
  148.3 1.2 shard_map.89.token_ref
  149.9 1.7 collective-permute-start.29
  153.1 8.1 %collective-permute-done.30.rest_4_ = bf16[8,32,1024]{2,1,0:T(8,128)(2,1)S(1)} collective-permute-done((bf16[8,32,1024]{2,1,0:T(8,128)(2,1)S(1)}, bf16[8,32,1024]{2,1,0:T(8,128)(2,1)S(1)}, u32[]{:S(2)}, u32[]{:S(2)}) %collective-permute-start.30) | collective-permute-done | bytes 524320 | tf_op jit(solution)/shard_map/ppermute | solution.py:487
  161.2 3.6 %shard_map.92.rest_4_.rest_9_ = f32[16,256]{1,0:T(8,128)S(1)} custom-call(s32[2]{0:T(128)S(1)} %pad_add_fusion.me_ref, s32[64]{0:T(128)S(1)} %shard_map.65.codes_ref.token_ref, bf16[8,32,5504]{2,1,0:T(8,128)(2,1)S(1)} %copy-done.2, bf16[8,32,1024]{2,1,0:T(8,128)(2,1)S(1)} %collective-permute-done.12.rest_4_.came_ref, ...), custom_call_target="tpu_custom_call" | custom-call | bytes 1024 | tf_op jit(solution)/shard_map/pallas_call | solution.py:452
  164.9 1.2 shard_map.93.rest_3_
  166.6 1.7 collective-permute-start.33
  169.6 7.3 %collective-permute-done.34.rest_4_ = bf16[8,32,1024]{2,1,0:T(8,128)(2,1)S(1)} collective-permute-done((bf16[8,32,1024]{2,1,0:T(8,128)(2,1)S(1)}, bf16[8,32,1024]{2,1,0:T(8,128)(2,1)S(1)}, u32[]{:S(2)}, u32[]{:S(2)}) %collective-permute-start.34) | collective-permute-done | bytes 524320 | tf_op jit(solution)/shard_map/ppermute | solution.py:487
  176.9 3.6 %shard_map.95.rest_4_.rest_9_ = f32[16,256]{1,0:T(8,128)S(1)} custom-call(s32[2]{0:T(128)S(1)} %pad_add_fusion.me_ref, s32[64]{0:T(128)S(1)} %shard_map.65.codes_ref.token_ref, bf16[8,32,5504]{2,1,0:T(8,128)(2,1)S(1)} %copy-done.2, bf16[8,32,1024]{2,1,0:T(8,128)(2,1)S(1)} %collective-permute-done.16.rest_4_.came_ref, ...), custom_call_target="tpu_custom_call" | custom-call | bytes 1024 | tf_op jit(solution)/shard_map/pallas_call | solution.py:452
  180.6 1.2 shard_map.96.rest_6_
  182.3 2.6 %collective-permute-start.32 = (bf16[8,32,384]{2,1,0:T(8,128)(2,1)S(1)}, bf16[8,32,384]{2,1,0:T(8,128)(2,1)S(1)}, u32[]{:S(2)}, u32[]{:S(2)}) collective-permute-start(bf16[8,32,384]{2,1,0:T(8,128)(2,1)S(1)} %shard_map.94.rest_6_), channel_id=1, source_target_pairs={{0,4},{2,6},{4,0},{6,2},{8,12},{10,14},{12,8},{14,10},{1,5},{3,7},... | collective-permute-start | bytes 589832 | tf_op jit(solution)/shard_map/ppermute | solution.py:487
  184.9 6.8 %collective-permute-done.35.rest_4_ = bf16[8,32,1024]{2,1,0:T(8,128)(2,1)S(1)} collective-permute-done((bf16[8,32,1024]{2,1,0:T(8,128)(2,1)S(1)}, bf16[8,32,1024]{2,1,0:T(8,128)(2,1)S(1)}, u32[]{:S(2)}, u32[]{:S(2)}) %collective-permute-start.35) | collective-permute-done | bytes 524320 | tf_op jit(solution)/shard_map/ppermute | solution.py:487
  191.7 3.6 %shard_map.97.rest_4_.rest_9_ = f32[16,256]{1,0:T(8,128)S(1)} custom-call(s32[2]{0:T(128)S(1)} %pad_add_fusion.me_ref, s32[64]{0:T(128)S(1)} %shard_map.65.codes_ref.token_ref, bf16[8,32,5504]{2,1,0:T(8,128)(2,1)S(1)} %copy-done.2, bf16[8,32,1024]{2,1,0:T(8,128)(2,1)S(1)} %collective-permute-done.21.rest_4_.came_ref, ...), custom_call_target="tpu_custom_call" | custom-call | bytes 1024 | tf_op jit(solution)/shard_map/pallas_call | solution.py:452
  196.7 5.2 %collective-permute-done.36.rest_4_ = bf16[8,32,384]{2,1,0:T(8,128)(2,1)S(1)} collective-permute-done((bf16[8,32,384]{2,1,0:T(8,128)(2,1)S(1)}, bf16[8,32,384]{2,1,0:T(8,128)(2,1)S(1)}, u32[]{:S(2)}, u32[]{:S(2)}) %collective-permute-start.36) | collective-permute-done | bytes 196640 | tf_op jit(solution)/shard_map/ppermute | solution.py:487
  201.9 2.3 %shard_map.99 = f32[16,2,128]{2,1,0:T(2,128)S(1)} custom-call(s32[2]{0:T(128)S(1)} %pad_add_fusion.me_ref, s32[64]{0:T(128)S(1)} %shard_map.65.codes_ref.token_ref, bf16[8,32,5504]{2,1,0:T(8,128)(2,1)S(1)} %copy-done.2, bf16[8,32,1024]{2,1,0:T(8,128)(2,1)S(1)} %collective-permute-done.19.rest_4_.came_ref, ...), custom_call_target="tpu_custom_call" | custom-call | bytes 1024 | tf_op jit(solution)/shard_map/pallas_call | solution.py:452
  204.2 10.1 %all_to_all.13.came_ref = f32[16,2,128]{2,1,0:T(2,128)S(1)} all-to-all(f32[16,2,128]{2,1,0:T(2,128)S(1)} %shard_map.99), channel_id=1, replica_groups=mesh['groups'=2,'docs'=8,'tensor'=2] {'docs','tensor'}, dimensions={0} | all-to-all | bytes 32768 | tf_op jit(solution)/shard_map/all_to_all | solution.py:580
  214.3 1.5 shard_map.100
  (79 shorter events, 28.7 us)
Async XLA Ops:
  0.8 0.7 copy-start.1
  4.5 21.4 %collective-permute-start.7 = (bf16[8,32,1024]{2,1,0:T(8,128)(2,1)S(1)}, bf16[8,32,1024]{2,1,0:T(8,128)(2,1)S(1)}, u32[]{:S(2)}, u32[]{:S(2)}) collective-permute-start(bf16[8,32,1024]{2,1,0:T(8,128)(2,1)S(1)} %get-tuple-element.51.token_ref), channel_id=1, source_target_pairs={{0,4},{2,6},{4,0},{6,2},{8,12},{10,14},{12,8},{14,10},{1,5},{3,7},... | collective-permute-start | bytes 1572872 | tf_op jit(solution)/shard_map/ppermute | solution.py:487
  8.2 15.6 %all-to-all-start = ((s32[16,1,16]{2,1,0:T(1,128)}), s32[16,1,16]{2,1,0:T(1,128)S(1)}, u32[]{:S(2)}, u32[]{:S(2)}) async-start(s32[16,1,16]{2,1,0:T(1,128)} %broadcast_in_dim.4), calls=%async_computation | async-start | bytes 16384 | tf_op jit(solution)/shard_map/all_to_all | solution.py:494
  14.0 24.5 %collective-permute-start.9 = (bf16[4,32,2048]{2,1,0:T(8,128)(2,1)}, bf16[4,32,2048]{2,1,0:T(8,128)(2,1)S(1)}, u32[]{:S(2)}, u32[]{:S(2)}) collective-permute-start(bf16[4,32,2048]{2,1,0:T(8,128)(2,1)} %get-tuple-element.54), channel_id=1, source_target_pairs={{4,8},{6,10},{8,4},{10,6},{5,9},{7,11},{9,5},{11,7},{20,24},{22,26... | collective-permute-start | bytes 1572872 | tf_op jit(solution)/shard_map/ppermute | solution.py:487
  17.4 19.8 %collective-permute-start.11 = (bf16[8,32,1024]{2,1,0:T(8,128)(2,1)}, bf16[8,32,1024]{2,1,0:T(8,128)(2,1)S(1)}, u32[]{:S(2)}, u32[]{:S(2)}) collective-permute-start(bf16[8,32,1024]{2,1,0:T(8,128)(2,1)} %get-tuple-element.56), channel_id=1, source_target_pairs={{0,4},{2,6},{4,0},{6,2},{8,12},{10,14},{12,8},{14,10},{1,5},{3,7},... | collective-permute-start | bytes 1572872 | tf_op jit(solution)/shard_map/ppermute | solution.py:487
  23.7 4.7 %copy-start.3 = (bf16[8,32,2048]{2,1,0:T(8,128)(2,1)S(1)}, bf16[8,32,2048]{2,1,0:T(8,128)(2,1)}, u32[]{:S(2)}) copy-start(bf16[8,32,2048]{2,1,0:T(8,128)(2,1)} %own_ref.22) | copy-start | bytes 3145732
  26.5 12.1 %collective-permute-start.10 = (bf16[8,32,1024]{2,1,0:T(8,128)(2,1)S(1)}, bf16[8,32,1024]{2,1,0:T(8,128)(2,1)S(1)}, u32[]{:S(2)}, u32[]{:S(2)}) collective-permute-start(bf16[8,32,1024]{2,1,0:T(8,128)(2,1)S(1)} %shard_map.67.token_ref), channel_id=1, source_target_pairs={{4,8},{6,10},{8,4},{10,6},{5,9},{7,11},{9,5},{11,7},{20,24},{22,26... | collective-permute-start | bytes 1572872 | tf_op jit(solution)/shard_map/ppermute | solution.py:487
  30.5 8.0 %copy-start.2 = (bf16[8,32,5504]{2,1,0:T(8,128)(2,1)S(1)}, bf16[8,32,5504]{2,1,0:T(8,128)(2,1)}, u32[]{:S(2)}) copy-start(bf16[8,32,5504]{2,1,0:T(8,128)(2,1)} %own_ref.31) | copy-start | bytes 8454148
  33.6 16.5 %collective-permute-start.14 = (bf16[8,32,1024]{2,1,0:T(8,128)(2,1)S(1)}, bf16[8,32,1024]{2,1,0:T(8,128)(2,1)S(1)}, u32[]{:S(2)}, u32[]{:S(2)}) collective-permute-start(bf16[8,32,1024]{2,1,0:T(8,128)(2,1)S(1)} %get-tuple-element.57.token_ref), channel_id=1, source_target_pairs={{0,4},{2,6},{4,0},{6,2},{8,12},{10,14},{12,8},{14,10},{1,5},{3,7},... | collective-permute-start | bytes 1572872 | tf_op jit(solution)/shard_map/ppermute | solution.py:487
  37.8 13.7 %collective-permute-start.13 = (bf16[8,32,1024]{2,1,0:T(8,128)(2,1)S(1)}, bf16[8,32,1024]{2,1,0:T(8,128)(2,1)S(1)}, u32[]{:S(2)}, u32[]{:S(2)}) collective-permute-start(bf16[8,32,1024]{2,1,0:T(8,128)(2,1)S(1)} %shard_map.69.rest_4_), channel_id=1, source_target_pairs={{4,8},{6,10},{8,4},{10,6},{5,9},{7,11},{9,5},{11,7},{20,24},{22,26... | collective-permute-start | bytes 1572872 | tf_op jit(solution)/shard_map/ppermute | solution.py:487
  39.4 21.9 %collective-permute-start.12 = (bf16[8,32,1024]{2,1,0:T(8,128)(2,1)S(1)}, bf16[8,32,1024]{2,1,0:T(8,128)(2,1)S(1)}, u32[]{:S(2)}, u32[]{:S(2)}) collective-permute-start(bf16[8,32,1024]{2,1,0:T(8,128)(2,1)S(1)} %shard_map.70.token_ref), channel_id=1, source_target_pairs={{0,4},{2,6},{4,0},{6,2},{8,12},{10,14},{12,8},{14,10},{1,5},{3,7},... | collective-permute-start | bytes 1572872 | tf_op jit(solution)/shard_map/ppermute | solution.py:487
  44.1 29.8 %collective-permute-start.6 = (bf16[4,32,2048]{2,1,0:T(8,128)(2,1)S(1)}, bf16[4,32,2048]{2,1,0:T(8,128)(2,1)S(1)}, u32[]{:S(2)}, u32[]{:S(2)}) collective-permute-start(bf16[4,32,2048]{2,1,0:T(8,128)(2,1)S(1)} %get-tuple-element.52), channel_id=1, source_target_pairs={{4,8},{6,10},{8,4},{10,6},{5,9},{7,11},{9,5},{11,7},{20,24},{22,26... | collective-permute-start | bytes 1572872 | tf_op jit(solution)/shard_map/ppermute | solution.py:487
  44.8 27.7 %collective-permute-start.8 = (bf16[8,32,1024]{2,1,0:T(8,128)(2,1)S(1)}, bf16[8,32,1024]{2,1,0:T(8,128)(2,1)S(1)}, u32[]{:S(2)}, u32[]{:S(2)}) collective-permute-start(bf16[8,32,1024]{2,1,0:T(8,128)(2,1)S(1)} %get-tuple-element.53), channel_id=1, source_target_pairs={{0,4},{2,6},{4,0},{6,2},{8,12},{10,14},{12,8},{14,10},{1,5},{3,7},... | collective-permute-start | bytes 1572872 | tf_op jit(solution)/shard_map/ppermute | solution.py:487
  50.7 10.6 %copy-start.4 = (bf16[8,32,2048]{2,1,0:T(8,128)(2,1)S(1)}, bf16[8,32,2048]{2,1,0:T(8,128)(2,1)}, u32[]{:S(2)}) copy-start(bf16[8,32,2048]{2,1,0:T(8,128)(2,1)} %own_ref.22) | copy-start | bytes 3145732
  50.7 23.2 %collective-permute-start.18 = (bf16[8,32,1024]{2,1,0:T(8,128)(2,1)S(1)}, bf16[8,32,1024]{2,1,0:T(8,128)(2,1)S(1)}, u32[]{:S(2)}, u32[]{:S(2)}) collective-permute-start(bf16[8,32,1024]{2,1,0:T(8,128)(2,1)S(1)} %shard_map.71.rest_4_), channel_id=1, source_target_pairs={{4,8},{6,10},{8,4},{10,6},{5,9},{7,11},{9,5},{11,7},{20,24},{22,26... | collective-permute-start | bytes 1572872 | tf_op jit(solution)/shard_map/ppermute | solution.py:487
  62.5 12.2 %collective-permute-start.17 = (bf16[8,32,1024]{2,1,0:T(8,128)(2,1)S(1)}, bf16[8,32,1024]{2,1,0:T(8,128)(2,1)S(1)}, u32[]{:S(2)}, u32[]{:S(2)}) collective-permute-start(bf16[8,32,1024]{2,1,0:T(8,128)(2,1)S(1)} %shard_map.73.token_ref), channel_id=1, source_target_pairs={{0,2},{2,0},{4,6},{6,4},{8,10},{10,8},{12,14},{14,12},{1,3},{3,1},... | collective-permute-start | bytes 1572872 | tf_op jit(solution)/shard_map/ppermute | solution.py:487
  63.0 18.3 %collective-permute-start.16 = (bf16[8,32,1024]{2,1,0:T(8,128)(2,1)S(1)}, bf16[8,32,1024]{2,1,0:T(8,128)(2,1)S(1)}, u32[]{:S(2)}, u32[]{:S(2)}) collective-permute-start(bf16[8,32,1024]{2,1,0:T(8,128)(2,1)S(1)} %shard_map.72.rest_5_), channel_id=1, source_target_pairs={{0,4},{2,6},{4,0},{6,2},{8,12},{10,14},{12,8},{14,10},{1,5},{3,7},... | collective-permute-start | bytes 1572872 | tf_op jit(solution)/shard_map/ppermute | solution.py:487
  73.1 10.6 %collective-permute-start.15 = (bf16[8,32,1024]{2,1,0:T(8,128)(2,1)S(1)}, bf16[8,32,1024]{2,1,0:T(8,128)(2,1)S(1)}, u32[]{:S(2)}, u32[]{:S(2)}) collective-permute-start(bf16[8,32,1024]{2,1,0:T(8,128)(2,1)S(1)} %shard_map.74.rest_4_), channel_id=1, source_target_pairs={{4,8},{6,10},{8,4},{10,6},{5,9},{7,11},{9,5},{11,7},{20,24},{22,26... | collective-permute-start | bytes 1572872 | tf_op jit(solution)/shard_map/ppermute | solution.py:487
  73.9 1.9 copy-start
  82.6 11.6 %collective-permute-start.22 = (bf16[8,32,1024]{2,1,0:T(8,128)(2,1)S(1)}, bf16[8,32,1024]{2,1,0:T(8,128)(2,1)S(1)}, u32[]{:S(2)}, u32[]{:S(2)}) collective-permute-start(bf16[8,32,1024]{2,1,0:T(8,128)(2,1)S(1)} %shard_map.77.token_ref), channel_id=1, source_target_pairs={{0,2},{2,0},{4,6},{6,4},{8,10},{10,8},{12,14},{14,12},{1,3},{3,1},... | collective-permute-start | bytes 1572872 | tf_op jit(solution)/shard_map/ppermute | solution.py:487
  97.8 29.2 %collective-permute-start.25 = (f32[512,768]{1,0:T(8,128)S(1)}, f32[512,768]{1,0:T(8,128)S(1)}, u32[]{:S(2)}, u32[]{:S(2)}) collective-permute-start(f32[512,768]{1,0:T(8,128)S(1)} %shard_map.80.rest_5_.rest_8_.rest_7_), channel_id=1, source_target_pairs={{0,1},{1,0},{2,3},{3,2},{4,5},{5,4},{6,7},{7,6},{8,9},{9,8},{10,11... | collective-permute-start | bytes 4718600 | tf_op jit(solution)/shard_map/ppermute | solution.py:560
  97.9 14.3 %collective-permute-start.21 = (bf16[8,32,1024]{2,1,0:T(8,128)(2,1)S(1)}, bf16[8,32,1024]{2,1,0:T(8,128)(2,1)S(1)}, u32[]{:S(2)}, u32[]{:S(2)}) collective-permute-start(bf16[8,32,1024]{2,1,0:T(8,128)(2,1)S(1)} %shard_map.75.rest_7_), channel_id=1, source_target_pairs={{0,4},{2,6},{4,0},{6,2},{8,12},{10,14},{12,8},{14,10},{1,5},{3,7},... | collective-permute-start | bytes 1572872 | tf_op jit(solution)/shard_map/ppermute | solution.py:487
  99.4 17.6 %collective-permute-start.20 = (bf16[12,32,1024]{2,1,0:T(8,128)(2,1)S(1)}, bf16[12,32,1024]{2,1,0:T(8,128)(2,1)S(1)}, u32[]{:S(2)}, u32[]{:S(2)}) collective-permute-start(bf16[12,32,1024]{2,1,0:T(8,128)(2,1)S(1)} %shard_map.78.rest_4_), channel_id=1, source_target_pairs={{4,8},{6,10},{8,4},{10,6},{5,9},{7,11},{9,5},{11,7},{20,24},{22,26... | collective-permute-start | bytes 2359304 | tf_op jit(solution)/shard_map/ppermute | solution.py:487
  112.2 14.8 %slice-start = ((s8[8454144]{0:T(1024)(128)(4,1)}), s8[4194304]{0:T(1024)(128)(4,1)S(1)}, s32[]{:S(2)}) async-start(s8[8454144]{0:T(1024)(128)(4,1)} %bitcast.4), calls=%async_computation.2 | async-start | bytes 8388608
  112.2 14.8 %slice-start.1 = ((s8[8454144]{0:T(1024)(128)(4,1)}), s8[4194304]{0:T(1024)(128)(4,1)S(1)}, s32[]{:S(2)}) async-start(s8[8454144]{0:T(1024)(128)(4,1)} %bitcast.4), calls=%async_computation.3 | async-start | bytes 8388608
  113.4 13.6 %slice-start.2 = ((s8[8454144]{0:T(1024)(128)(4,1)}), s8[65536]{0:T(1024)(128)(4,1)S(1)}, s32[]{:S(2)}) async-start(s8[8454144]{0:T(1024)(128)(4,1)} %bitcast.4), calls=%async_computation.4 | async-start | bytes 131072
  113.5 13.6 %collective-permute-start.24 = (bf16[8,32,1024]{2,1,0:T(8,128)(2,1)S(1)}, bf16[8,32,1024]{2,1,0:T(8,128)(2,1)S(1)}, u32[]{:S(2)}, u32[]{:S(2)}) collective-permute-start(bf16[8,32,1024]{2,1,0:T(8,128)(2,1)S(1)} %shard_map.81.token_ref), channel_id=1, source_target_pairs={{0,2},{2,0},{4,6},{6,4},{8,10},{10,8},{12,14},{14,12},{1,3},{3,1},... | collective-permute-start | bytes 1572872 | tf_op jit(solution)/shard_map/ppermute | solution.py:487
  114.0 16.8 %collective-permute-start.19 = (bf16[8,32,1024]{2,1,0:T(8,128)(2,1)S(1)}, bf16[8,32,1024]{2,1,0:T(8,128)(2,1)S(1)}, u32[]{:S(2)}, u32[]{:S(2)}) collective-permute-start(bf16[8,32,1024]{2,1,0:T(8,128)(2,1)S(1)} %shard_map.79.rest_7_), channel_id=1, source_target_pairs={{0,4},{2,6},{4,0},{6,2},{8,12},{10,14},{12,8},{14,10},{1,5},{3,7},... | collective-permute-start | bytes 1572872 | tf_op jit(solution)/shard_map/ppermute | solution.py:487
  116.3 19.1 %collective-permute-start.27 = (bf16[12,32,1024]{2,1,0:T(8,128)(2,1)S(1)}, bf16[12,32,1024]{2,1,0:T(8,128)(2,1)S(1)}, u32[]{:S(2)}, u32[]{:S(2)}) collective-permute-start(bf16[12,32,1024]{2,1,0:T(8,128)(2,1)S(1)} %shard_map.82.rest_3_), channel_id=1, source_target_pairs={{4,8},{6,10},{8,4},{10,6},{5,9},{7,11},{9,5},{11,7},{20,24},{22,26... | collective-permute-start | bytes 2359304 | tf_op jit(solution)/shard_map/ppermute | solution.py:487
  131.9 12.7 %collective-permute-start.26 = (bf16[8,32,1024]{2,1,0:T(8,128)(2,1)S(1)}, bf16[8,32,1024]{2,1,0:T(8,128)(2,1)S(1)}, u32[]{:S(2)}, u32[]{:S(2)}) collective-permute-start(bf16[8,32,1024]{2,1,0:T(8,128)(2,1)S(1)} %shard_map.85.token_ref), channel_id=1, source_target_pairs={{0,2},{2,0},{4,6},{6,4},{8,10},{10,8},{12,14},{14,12},{1,3},{3,1},... | collective-permute-start | bytes 1572872 | tf_op jit(solution)/shard_map/ppermute | solution.py:487
  132.4 15.8 %collective-permute-start.23 = (bf16[8,32,1024]{2,1,0:T(8,128)(2,1)S(1)}, bf16[8,32,1024]{2,1,0:T(8,128)(2,1)S(1)}, u32[]{:S(2)}, u32[]{:S(2)}) collective-permute-start(bf16[8,32,1024]{2,1,0:T(8,128)(2,1)S(1)} %shard_map.83.rest_7_), channel_id=1, source_target_pairs={{0,4},{2,6},{4,0},{6,2},{8,12},{10,14},{12,8},{14,10},{1,5},{3,7},... | collective-permute-start | bytes 1572872 | tf_op jit(solution)/shard_map/ppermute | solution.py:487
  134.7 17.6 %collective-permute-start.31 = (bf16[12,32,1024]{2,1,0:T(8,128)(2,1)S(1)}, bf16[12,32,1024]{2,1,0:T(8,128)(2,1)S(1)}, u32[]{:S(2)}, u32[]{:S(2)}) collective-permute-start(bf16[12,32,1024]{2,1,0:T(8,128)(2,1)S(1)} %shard_map.86.rest_3_), channel_id=1, source_target_pairs={{4,8},{6,10},{8,4},{10,6},{5,9},{7,11},{9,5},{11,7},{20,24},{22,26... | collective-permute-start | bytes 2359304 | tf_op jit(solution)/shard_map/ppermute | solution.py:487
  149.5 11.7 %collective-permute-start.30 = (bf16[8,32,1024]{2,1,0:T(8,128)(2,1)S(1)}, bf16[8,32,1024]{2,1,0:T(8,128)(2,1)S(1)}, u32[]{:S(2)}, u32[]{:S(2)}) collective-permute-start(bf16[8,32,1024]{2,1,0:T(8,128)(2,1)S(1)} %shard_map.89.token_ref), channel_id=1, source_target_pairs={{0,2},{2,0},{4,6},{6,4},{8,10},{10,8},{12,14},{14,12},{1,3},{3,1},... | collective-permute-start | bytes 1572872 | tf_op jit(solution)/shard_map/ppermute | solution.py:487
  149.9 14.9 %collective-permute-start.29 = (bf16[8,32,1024]{2,1,0:T(8,128)(2,1)S(1)}, bf16[8,32,1024]{2,1,0:T(8,128)(2,1)S(1)}, u32[]{:S(2)}, u32[]{:S(2)}) collective-permute-start(bf16[8,32,1024]{2,1,0:T(8,128)(2,1)S(1)} %shard_map.87.rest_7_), channel_id=1, source_target_pairs={{0,4},{2,6},{4,0},{6,2},{8,12},{10,14},{12,8},{14,10},{1,5},{3,7},... | collective-permute-start | bytes 1572872 | tf_op jit(solution)/shard_map/ppermute | solution.py:487
  166.1 10.8 %collective-permute-start.34 = (bf16[8,32,1024]{2,1,0:T(8,128)(2,1)S(1)}, bf16[8,32,1024]{2,1,0:T(8,128)(2,1)S(1)}, u32[]{:S(2)}, u32[]{:S(2)}) collective-permute-start(bf16[8,32,1024]{2,1,0:T(8,128)(2,1)S(1)} %shard_map.93.rest_3_), channel_id=1, source_target_pairs={{0,2},{2,0},{4,6},{6,4},{8,10},{10,8},{12,14},{14,12},{1,3},{3,1},... | collective-permute-start | bytes 1572872 | tf_op jit(solution)/shard_map/ppermute | solution.py:487
  166.6 14.0 %collective-permute-start.33 = (bf16[8,32,1024]{2,1,0:T(8,128)(2,1)S(1)}, bf16[8,32,1024]{2,1,0:T(8,128)(2,1)S(1)}, u32[]{:S(2)}, u32[]{:S(2)}) collective-permute-start(bf16[8,32,1024]{2,1,0:T(8,128)(2,1)S(1)} %shard_map.91.rest_6_), channel_id=1, source_target_pairs={{0,4},{2,6},{4,0},{6,2},{8,12},{10,14},{12,8},{14,10},{1,5},{3,7},... | collective-permute-start | bytes 1572872 | tf_op jit(solution)/shard_map/ppermute | solution.py:487
  168.3 0.7 collective-permute-start.28
  181.8 9.9 %collective-permute-start.35 = (bf16[8,32,1024]{2,1,0:T(8,128)(2,1)S(1)}, bf16[8,32,1024]{2,1,0:T(8,128)(2,1)S(1)}, u32[]{:S(2)}, u32[]{:S(2)}) collective-permute-start(bf16[8,32,1024]{2,1,0:T(8,128)(2,1)S(1)} %shard_map.96.rest_6_), channel_id=1, source_target_pairs={{0,2},{2,0},{4,6},{6,4},{8,10},{10,8},{12,14},{14,12},{1,3},{3,1},... | collective-permute-start | bytes 1572872 | tf_op jit(solution)/shard_map/ppermute | solution.py:487
  182.3 13.1 %collective-permute-start.32 = (bf16[8,32,384]{2,1,0:T(8,128)(2,1)S(1)}, bf16[8,32,384]{2,1,0:T(8,128)(2,1)S(1)}, u32[]{:S(2)}, u32[]{:S(2)}) collective-permute-start(bf16[8,32,384]{2,1,0:T(8,128)(2,1)S(1)} %shard_map.94.rest_6_), channel_id=1, source_target_pairs={{0,4},{2,6},{4,0},{6,2},{8,12},{10,14},{12,8},{14,10},{1,5},{3,7},... | collective-permute-start | bytes 589832 | tf_op jit(solution)/shard_map/ppermute | solution.py:487
  196.2 5.7 %collective-permute-start.36 = (bf16[8,32,384]{2,1,0:T(8,128)(2,1)S(1)}, bf16[8,32,384]{2,1,0:T(8,128)(2,1)S(1)}, u32[]{:S(2)}, u32[]{:S(2)}) collective-permute-start(bf16[8,32,384]{2,1,0:T(8,128)(2,1)S(1)} %shard_map.98.rest_6_), channel_id=1, source_target_pairs={{0,2},{2,0},{4,6},{6,4},{8,10},{10,8},{12,14},{14,12},{1,3},{3,1},... | collective-permute-start | bytes 589832 | tf_op jit(solution)/shard_map/ppermute | solution.py:487

commit v3 on v2

--- a/solution.py
+++ b/solution.py
@@ -44,6 +44,7 @@
 SMALL = pltpu.CompilerParams(vmem_limit_bytes=6 * 1024 * 1024)
 CHEAP = pl.CostEstimate(flops=0, bytes_accessed=1024, transcendentals=0)
 CHUNK = 1024
+WIDTHS = (1024, 1024, 1024, 1024, 768)
 LEAD = 4
 
 
@@ -81,22 +82,22 @@
     return ref.at[i, :, pl.ds(off, width)]
 
 
-def own_slots(copies, inner, me, tab_ref, here, ahead, dst):
+def own_slots(sems, inner, me, tab_ref, here, ahead, dst, first):
     @pl.when(inner == 1)
     def _():
-        c = Copies(copies.sems)
+        c = Copies(sems)
         for part, (ref, off, width) in enumerate(here):
             for k in range(2 * CAP):
                 sample = tab_ref[(me ^ (2 + k // CAP)) * CAP + k % CAP]
-                c.start(cut(ref, sample, off, width), cut(dst, part * 2 * CAP + k, 0, width))
+                c.start(cut(ref, sample, off, width), cut(dst, first + part * 2 * CAP + k, 0, width))
         c.wait()
 
     @pl.when(inner == 0)
     def _():
-        c = Copies(copies.sems)
+        c = Copies(sems)
         ref, off, width = ahead
         for s in range(8):
-            c.start(cut(ref, s, off, width), cut(dst, s, 0, width))
+            c.start(cut(ref, s, off, width), cut(dst, first + s, 0, width))
         c.wait()
 
 
@@ -129,8 +130,8 @@
     lists = Copies(sems)
     for k in range(OWN):
         lists.start(cut(grad_ref, own_ref[k], 0, 2 * width), across_ref.at[k])
-    own_slots(Copies(out_sems), inner, me, tab_ref,
-              ((grad_ref, 0, width), (grad_ref, width, width)), (grad_ref, 0, width), z_ref)
+    own_slots(out_sems, inner, me, tab_ref,
+              ((grad_ref, 0, width), (grad_ref, width, width)), (grad_ref, 0, width), z_ref, 0)
     lists.wait()
 
 
@@ -150,58 +151,24 @@
     )(me, pair_doc, pair_sample, grad, act)
 
 
-def second_kernel(me_ref, tab_ref, own_ref, grad_ref, act_ref, token_ref, z_ref, across_ref, sems, out_sems):
+def ahead_block_kernel(me_ref, tab_ref, act_ref, far_ref, token_ref, z_ref, sems, *, here, ahead):
     me = me_ref[0]
-    inner = is_inner(me)
-    lists = Copies(sems)
-    for k in range(OWN):
-        lists.start(cut(act_ref, own_ref[k], 0, 2 * CHUNK), across_ref.at[k])
-    own_slots(Copies(out_sems), inner, me, tab_ref,
-              ((act_ref, 0, CHUNK), (act_ref, CHUNK, CHUNK)), (grad_ref, CHUNK, CHUNK), z_ref)
-    lists.wait()
-
-
-def second_call(me, tab, own, grad, act, token):
-    rows = grad.shape[1]
-
-    def buf(k, w):
-        return jax.ShapeDtypeStruct((k, rows, w), grad.dtype)
-
-    return pl.pallas_call(
-        second_kernel,
-        out_shape=(buf(8, CHUNK), buf(OWN, 2 * CHUNK)),
-        in_specs=[SMEM, SMEM, SMEM, ANY, ANY, ANY],
-        out_specs=(VMEM,) * 2,
-        scratch_shapes=[pltpu.SemaphoreType.DMA((OWN,)), pltpu.SemaphoreType.DMA((8,))],
-        compiler_params=SMALL,
-        cost_estimate=CHEAP,
-    )(me, tab, own, grad, act, token)
-
-
-def third_kernel(me_ref, tab_ref, act_ref, token_ref, z2_ref, z3_ref, out_sems, *, rest):
-    me = me_ref[0]
-    inner = is_inner(me)
-    own_slots(Copies(out_sems), inner, me, tab_ref,
-              ((act_ref, 2 * CHUNK, CHUNK), (act_ref, 3 * CHUNK, CHUNK)), (act_ref, 0, CHUNK), z2_ref)
-    own_slots(Copies(out_sems), inner, me, tab_ref,
-              ((act_ref, 4 * CHUNK, CHUNK), (act_ref, 5 * CHUNK, rest)), (act_ref, CHUNK, CHUNK), z3_ref)
-
-
-def third_call(me, tab, act, token):
-    rows, width = act.shape[1:]
-    buf = jax.ShapeDtypeStruct((8, rows, CHUNK), act.dtype)
-    return pl.pallas_call(
-        functools.partial(third_kernel, rest=width - 5 * CHUNK),
-        out_shape=(buf, buf),
-        in_specs=[SMEM, SMEM, ANY, ANY],
-        out_specs=(VMEM,) * 2,
+    own_slots(sems, is_inner(me), me, tab_ref, [(act_ref, *span) for span in here], (far_ref, *ahead), z_ref, 0)
+
+
+def ahead_block_call(me, tab, act, far, token, here, ahead):
+    return pl.pallas_call(
+        functools.partial(ahead_block_kernel, here=here, ahead=ahead),
+        out_shape=jax.ShapeDtypeStruct((8, act.shape[1], CHUNK), act.dtype),
+        in_specs=[SMEM, SMEM, ANY, ANY, ANY],
+        out_specs=VMEM,
         scratch_shapes=[pltpu.SemaphoreType.DMA((8,))],
         compiler_params=SMALL,
         cost_estimate=CHEAP,
-    )(me, tab, act, token)
-
-
-def mix_kernel(me_ref, codes_ref, own_ref, came_ref, token_ref, list_ref, sems, *, first, off):
+    )(me, tab, act, far, token)
+
+
+def mix_kernel(me_ref, codes_ref, own_ref, came_ref, token_ref, list_ref, sems, *, first, off, at):
     count, _, width = list_ref.shape
 
     @pl.when(is_inner(me_ref[0]) == 1)
@@ -211,14 +178,14 @@
             code = codes_ref[LIST + first + k]
             mine = code < 8
             copies.either(mine, cut(own_ref, jnp.minimum(code, 7), off, width),
-                          cut(came_ref, jnp.maximum(code - 8, 0), 0, width), list_ref.at[k])
+                          cut(came_ref, at + jnp.maximum(code - 8, 0), 0, width), list_ref.at[k])
         copies.wait()
 
 
-def mix_call(me, codes, own, came, count, first, off, width, token):
+def mix_call(me, codes, own, came, at, count, first, off, width, token):
     rows = own.shape[1]
     return pl.pallas_call(
-        functools.partial(mix_kernel, first=first, off=off),
+        functools.partial(mix_kernel, first=first, off=off, at=at),
         out_shape=jax.ShapeDtypeStruct((count, rows, width), own.dtype),
         in_specs=[SMEM, SMEM, ANY, ANY, ANY],
         out_specs=VMEM,
@@ -254,6 +221,21 @@
 def over(rest, early_off, extra_off):
     early = None if early_off is None else (rest.pop(0), early_off)
     return early, rest.pop(0), (rest.pop(0), extra_off)
+
+
+def blank_kernel(token_ref, *refs):
+    pass
+
+
+def blank_call(shapes, token):
+    return tuple(pl.pallas_call(
+        blank_kernel,
+        out_shape=[jax.ShapeDtypeStruct(x, jnp.bfloat16) for x in shapes],
+        in_specs=[SMEM],
+        out_specs=[ANY] * len(shapes),
+        compiler_params=SMALL,
+        cost_estimate=CHEAP,
+    )(token))
 
 
 def ahead_kernel(own_ref, grad_ref, act_ref, grad_out, act_out, sems):
@@ -316,7 +298,7 @@
     )(*args)
 
 
-def side_kernel(me_ref, codes_ref, tab_ref, sample_ref, came_ref, *rest, offs, off, part):
+def side_kernel(me_ref, codes_ref, tab_ref, sample_ref, came_ref, *rest, offs, off, at, part):
     rest = list(rest)
     came_over = over(rest, *offs)
     own_ref, far_ref, token_ref, side_ref, sems, role_sems = rest
@@ -331,7 +313,7 @@
     def _():
         copies = Copies(role_sems)
         for k in range(CAP):
-            copies.start(cut(came_ref, codes_ref[SIDE + k], 0, width), side_ref.at[CAP + k])
+            copies.start(cut(came_ref, at + codes_ref[SIDE + k], 0, width), side_ref.at[CAP + k])
         for k in range(CAP, 3 * CAP):
             entry(copies, codes_ref[SIDE + k], came_over, width, side_ref.at[CAP + k])
         copies.wait()
@@ -340,7 +322,7 @@
     def _():
         copies = Copies(role_sems)
         for k in range(CAP):
-            copies.start(cut(own_ref, part * 2 * CAP + CAP + k, 0, width), side_ref.at[CAP + k])
+            copies.start(cut(own_ref, part + CAP + k, 0, width), side_ref.at[CAP + k])
         for k in range(2 * CAP):
             copies.start(cut(far_ref, 2 * CAP + k, 0, width), side_ref.at[2 * CAP + k])
         copies.wait()
@@ -348,12 +330,12 @@
     mine.wait()
 
 
-def side_call(me, codes, tab, sample, came, arrays, offs, own, far, off, part, token):
+def side_call(me, codes, tab, sample, came, at, arrays, offs, own, part, far, off, token):
     late = arrays[-2]
     rows, width = late.shape[1:]
     args = [me, codes, tab, sample, came, *arrays, own, far, token]
     return pl.pallas_call(
-        functools.partial(side_kernel, offs=offs, off=off, part=part),
+        functools.partial(side_kernel, offs=offs, off=off, at=at, part=part),
         out_shape=jax.ShapeDtypeStruct((4 * CAP, rows, width), late.dtype),
         in_specs=[SMEM, SMEM, SMEM] + [ANY] * (len(args) - 3),
         out_specs=VMEM,
@@ -363,7 +345,7 @@
     )(*args)
 
 
-def gram_kernel(me_ref, codes_ref, own_ref, came_ref, *rest, offs, off, part, mode, last, tensor):
+def gram_kernel(me_ref, codes_ref, own_ref, came_ref, *rest, offs, off, at, part, mode, last, tensor):
     rest = list(rest)
     came_over = over(rest, *offs)
     partner_ref, far_ref, side_ref, doc_ref, token_ref = rest[:5]
@@ -390,7 +372,7 @@
     def _():
         more = Copies(role_sems)
         for r in range(CAP):
-            more.start(cut(came_ref, codes_ref[SLOTS + CAP + r], 0, width), slot(CAP + r))
+            more.start(cut(came_ref, at + codes_ref[SLOTS + CAP + r], 0, width), slot(CAP + r))
         for k in range(2 * CAP, 4 * CAP):
             entry(more, codes_ref[SLOTS + k], came_over, width, slot(k))
         more.wait()
@@ -399,7 +381,7 @@
     def _():
         more = Copies(role_sems)
         for r in range(CAP):
-            more.start(cut(partner_ref, part * 2 * CAP + r, 0, width), slot(CAP + r))
+            more.start(cut(partner_ref, part + r, 0, width), slot(CAP + r))
         for k in range(2 * CAP):
             more.start(cut(far_ref, k, 0, width), slot(2 * CAP + k))
         more.wait()
@@ -411,16 +393,16 @@
         acc_ref[...] = held[2][...]
 
     def block(n, _):
-        at = pl.ds(pl.multiple_of(n * step, step), step)
-        part = lax.dot_general(
-            rows_ref[...], cols_ref[at, :], (((1,), (1,)), ((), ())), preferred_element_type=jnp.float32
+        cols = pl.ds(pl.multiple_of(n * step, step), step)
+        gram = lax.dot_general(
+            rows_ref[...], cols_ref[cols, :], (((1,), (1,)), ((), ())), preferred_element_type=jnp.float32
         )
         if mode == "first":
-            out_ref[:, at] = part
+            out_ref[:, cols] = gram
         elif mode == "next":
-            out_ref[:, at] = held[0][:, at] + part
+            out_ref[:, cols] = held[0][:, cols] + gram
         else:
-            both = part * (held[0][:, at] + held[1][:, at])
+            both = gram * (held[0][:, cols] + held[1][:, cols])
             acc_ref[...] += jnp.sum(both.reshape(8 * CAP, rows, step), axis=1)
         return 0
 
@@ -436,7 +418,7 @@
                 out_ref[owner * tensor + t] = jnp.broadcast_to(total[k * CAP : (k + 1) * CAP], (CAP, 128))
 
 
-def gram_call(me, codes, own, came, arrays, offs, partner, far, side, doc, off, part, token, mode, held,
+def gram_call(me, codes, own, came, at, arrays, offs, partner, part, far, side, doc, off, token, mode, held,
               last, tensor):
     late = arrays[-2]
     rows, width = late.shape[1:]
@@ -450,7 +432,7 @@
     else:
         out = jax.ShapeDtypeStruct((total, tokens), jnp.float32)
     return pl.pallas_call(
-        functools.partial(gram_kernel, offs=offs, off=off, part=part, mode=mode, last=last, tensor=tensor),
+        functools.partial(gram_kernel, offs=offs, off=off, at=at, part=part, mode=mode, last=last, tensor=tensor),
         out_shape=out,
         in_specs=[SMEM, SMEM] + [ANY] * (len(args) - 2) + [VMEM] * len(held),
         out_specs=VMEM,
@@ -481,35 +463,41 @@
 def chain(sample_act, sample_grad, doc_act, doc_grad, pair_doc, pair_sample):
     groups, tensor = lax.axis_size("groups"), lax.axis_size("tensor")
     me = jnp.stack([lax.axis_index("docs"), lax.axis_index("groups")]).astype(jnp.int32)
-    chunks = [(True, 0, CHUNK), (True, CHUNK, CHUNK)] + [(False, i * CHUNK, CHUNK) for i in range(5)]
-    chunks.append((False, 5 * CHUNK, sample_act.shape[2] - 5 * CHUNK))
+    chunks = [(True, 0, CHUNK), (True, CHUNK, CHUNK)]
+    off = 0
+    for w in WIDTHS:
+        chunks.append((False, off, w))
+        off += w
+    chunks.append((False, off, sample_act.shape[2] - off))
     total = len(chunks)
     send = lambda x, pairs: lax.ppermute(x, "docs", pairs)
     tab, place, own, z, across = start_call(me, pair_doc, pair_sample, sample_grad, sample_act)
     z0 = send(z, OVER_Z)
     early_grad = send(across, ACROSS)
-    z, across = second_call(me, tab, own, sample_grad, sample_act, z)
-    z1 = send(z, OVER_Z)
-    early_act = send(across, ACROSS)
     tables = lax.all_to_all(
         jnp.broadcast_to(tab[None, :], (groups * 8, 8 * CAP)), ("groups", "docs"), 0, 0, tiled=True
     )
     codes = codes_call(me, tables, groups)
+    listed = list_call(me, tab, tables, early_grad)
 
     def send_extras(count):
         if count == 0:
-            return tuple(jnp.zeros((EXTRAS[-1],) + x.shape[1:], x.dtype) for x in (sample_grad, sample_act))
+            return blank_call([(EXTRAS[-1],) + x.shape[1:] for x in (sample_grad, sample_act)], own)
         sent = [send(x, ACROSS) for x in ahead_call(count, own, sample_grad, sample_act)]
         return tuple(jnp.pad(x, ((0, EXTRAS[-1] - count), (0, 0), (0, 0))) for x in sent)
 
     extras = lax.switch(codes[BRANCH], [functools.partial(send_extras, c) for c in EXTRAS])
 
-    ahead_of = [z0, z1]
+    ahead_of = [(z0, 0)]
     main, late, sides = {}, {}, {}
     state = dict(grads=None, score=None)
 
     def came(i):
-        return ahead_of[i] if i < LEAD else main[i - LEAD]
+        return ahead_of[i] if i < LEAD else (main[i - LEAD], 0)
+
+    def partner(i):
+        array, first = ahead_of[i // 2]
+        return array, first + i % 2 * 2 * CAP
 
     def sample(i):
         return sample_grad if chunks[i][0] else sample_act
@@ -517,14 +505,14 @@
     def over_arrays(i):
         is_grad, off, _ = chunks[i]
         extra = extras[0 if is_grad else 1]
-        if i >= LEAD:
+        if not is_grad:
             return [late[i], extra], (None, off)
-        return [early_grad if is_grad else early_act, late[i], extra], (off, off)
+        return [early_grad, late[i], extra], (off, off)
 
     def mix(i, token):
         _, off, w = chunks[i]
-        first = OWN if i < LEAD else 0
-        out = mix_call(me, codes, sample(i), came(i), MAIN - first, first, off, w, token)
+        first = OWN if chunks[i][0] else 0
+        out = mix_call(me, listed, sample(i), *came(i), MAIN - first, first, off, w, token)
         late[i] = send(out, ACROSS)
         return out
 
@@ -535,8 +523,8 @@
         return out
 
     def side(i, token):
-        out = side_call(me, codes, tab, sample(i), came(i), *over_arrays(i), ahead_of[i // 2], main[i],
-                        chunks[i][1], i % 2, token)
+        out = side_call(me, codes, tab, sample(i), *came(i), *over_arrays(i), *partner(i), main[i], chunks[i][1],
+                        token)
         sides[i] = send(out, OVER_Y)
         return out
 
@@ -549,8 +537,8 @@
         else:
             held, mode = [*state["grads"], state["score"]], "score"
         out = gram_call(
-            me, codes, sample(i), came(i), *over_arrays(i), ahead_of[i // 2], main[i],
-            sides[i], doc_grad if is_grad else doc_act, off, i % 2, token, mode, held, last, tensor,
+            me, codes, sample(i), *came(i), *over_arrays(i), *partner(i), main[i], sides[i],
+            doc_grad if is_grad else doc_act, off, token, mode, held, last, tensor,
         )
         if not is_grad:
             state["score"] = out
@@ -563,20 +551,27 @@
             state["score"] = jnp.zeros((8 * CAP, 256), jnp.float32)
         return out
 
-    token = mix(0, codes)
-    z2, z3 = third_call(me, tab, sample_act, token)
-    ahead_of.append(send(z2, OVER_Z))
-    ahead_of.append(send(z3, OVER_Z))
-    token = z2
+    token = mix(0, listed)
+    spans = [c[1:] for c in chunks[2:]]
+
+    def ahead_block(i, token):
+        out = ahead_block_call(me, tab, sample_act, sample(i), token, spans[2 * i - 2 : 2 * i], chunks[i][1:])
+        ahead_of.append((send(out, OVER_Z), 0))
+        return out
+
+    token = ahead_block(1, token)
+    token = ahead_block(2, token)
     for i in range(total + 2):
         if i + 1 < total:
             token = mix(i + 1, token)
         if i < total:
             token = forward(i, token)
+        if i == 0:
+            token = ahead_block(3, token)
+        if 1 <= i < total + 1:
+            token = side(i - 1, token)
         if i >= 2:
             token = gram(i - 2, token)
-        if 1 <= i < total + 1:
-            token = side(i - 1, token)
     back = lax.all_to_all(state["score"], ("docs", "tensor"), 0, 0, tiled=True)
     return pl.pallas_call(
         functools.partial(finish_kernel, tensor=tensor),
@@ -588,35 +583,17 @@
     )(back, place)
 
 
-def codes_kernel(me_ref, all_ref, out_ref, scratch, masks, *, groups):
-    group, me = me_ref[1], me_ref[0]
-    base = group * 8
-
-    def owner_mask(row, _):
-        first = jnp.where((row & 7) < 4, 8, 0)
-        mask = jnp.int32(0)
-        for j in range(8):
-            mask = mask | jnp.left_shift(1, all_ref[row, first + j])
-        masks[row] = mask
-        return 0
-
-    lax.fori_loop(0, groups * 8, owner_mask, 0)
-
-    def longest(k, best):
-        row = (k >> 2) * 8 + 2 + (k & 3)
-        return jnp.maximum(best, jnp.maximum(bits(masks[row]), OWN) + bits(masks[row ^ 2]))
-
-    best = lax.fori_loop(0, groups * 4, longest, jnp.int32(0))
-    branch = jnp.int32(0)
-    for c in EXTRAS[:-1]:
-        branch = branch + (best > MAIN + c).astype(jnp.int32)
-    for i in range(CODES):
-        out_ref[i] = 0
+def list_kernel(me_ref, mine_ref, all_ref, token_ref, out_ref, scratch):
+    me = me_ref[0]
+    first = jnp.where(me < 4, 8, 0)
+    mine, partner = jnp.int32(0), jnp.int32(0)
+    for j in range(8):
+        mine = mine | jnp.left_shift(1, mine_ref[first + j])
+        partner = partner | jnp.left_shift(1, all_ref[me_ref[1] * 8 + (me ^ 2), first + j])
     for i in range(32):
         scratch[i] = 0
-    out_ref[BRANCH] = branch
-    inner = is_inner(me)
-    mine, partner = masks[base + me], masks[base + (me ^ 2)]
+    for i in range(16):
+        out_ref[i] = 0
     count = jnp.int32(0)
     for s in range(8):
         hit = (mine >> s) & 1
@@ -630,6 +607,46 @@
     need = jnp.maximum(count - MAIN, 0)
     for k in range(MAIN):
         out_ref[LIST + k] = scratch[k if k < OWN else k + need]
+
+
+def list_call(me, mine, tables, token):
+    return pl.pallas_call(
+        list_kernel,
+        out_shape=jax.ShapeDtypeStruct((16,), jnp.int32),
+        in_specs=[SMEM, SMEM, SMEM, ANY],
+        out_specs=SMEM,
+        scratch_shapes=[pltpu.SMEM((32,), jnp.int32)],
+        compiler_params=SMALL,
+        cost_estimate=CHEAP,
+    )(me, mine, tables, token)
+
+
+def codes_kernel(me_ref, all_ref, out_ref, masks, *, groups):
+    group, me = me_ref[1], me_ref[0]
+    base = group * 8
+
+    def owner_mask(row, _):
+        first = jnp.where((row & 7) < 4, 8, 0)
+        mask = jnp.int32(0)
+        for j in range(8):
+            mask = mask | jnp.left_shift(1, all_ref[row, first + j])
+        masks[row] = mask
+        return 0
+
+    lax.fori_loop(0, groups * 8, owner_mask, 0)
+
+    def longest(k, best):
+        row = (k >> 2) * 8 + 2 + (k & 3)
+        return jnp.maximum(best, jnp.maximum(bits(masks[row]), OWN) + bits(masks[row ^ 2]))
+
+    best = lax.fori_loop(0, groups * 4, longest, jnp.int32(0))
+    branch = jnp.int32(0)
+    for c in EXTRAS[:-1]:
+        branch = branch + (best > MAIN + c).astype(jnp.int32)
+    for i in range(CODES):
+        out_ref[i] = 0
+    out_ref[BRANCH] = branch
+    inner = is_inner(me)
     far, far_outer = masks[base + (me ^ 6)], masks[base + (me ^ 4)]
     after = jnp.maximum(bits(far), OWN)
     extra = jnp.maximum(after + bits(far_outer) - MAIN, 0)
@@ -665,7 +682,7 @@
         out_shape=jax.ShapeDtypeStruct((CODES,), jnp.int32),
         in_specs=[SMEM, SMEM],
         out_specs=SMEM,
-        scratch_shapes=[pltpu.SMEM((32,), jnp.int32), pltpu.SMEM((groups * 8,), jnp.int32)],
+        scratch_shapes=[pltpu.SMEM((groups * 8,), jnp.int32)],
         compiler_params=SMALL,
         cost_estimate=CHEAP,
     )(me, tables)
@@ -720,7 +737,8 @@
             and pair_doc.shape[0] == 8 * CAP
             and sample_act.shape[0] == 8
             and sample_grad.shape[2] == 2 * CHUNK
-            and 5 * CHUNK < sample_act.shape[2] <= 6 * CHUNK
+            and 0 < sample_act.shape[2] - sum(WIDTHS) <= CHUNK
+            and sample_act.shape[2] % 128 == 0
         )
         run = chain if fits else direct
         return run(sample_act, sample_grad, doc_act, doc_grad, pair_doc, pair_sample)

time: 217 us -> 227 us (1.046)
  waiting for transfers between devices: 89.7 us -> 38.5 us
  starting transfers between devices: 48.6 us -> 91.5 us
  blocking collectives: 10.1 us -> 25 us
  Pallas kernels: 60.3 us -> 63.5 us
    ppermute x30 -> x31, waiting for transfers between devices: 88.1 us -> 38.5 us  [chain(): send = lambda x, pairs: lax.ppermute(x, 'docs', pairs)]
    ppermute x30 -> x31, starting transfers between devices: 42.7 us -> 91.5 us  [chain(): send = lambda x, pairs: lax.ppermute(x, 'docs', pairs)]
    all_to_all x0 -> x1, blocking collectives: none -> 14.7 us  [chain(): lax.all_to_all(jnp.broadcast_to(tab[None, :], (groups * 8, 8 * CAP)), ('g...]
    all_to_all x1 -> x0, starting transfers between devices: 5.85 us -> none  [chain(): lax.all_to_all(jnp.broadcast_to(tab[None, :], (groups * 8, 8 * CAP)), ('g...]
    pallas_call x26 -> x29, Pallas kernels: 47.9 us -> 50.1 us  [the longest x8 27.9 us: gram_call(): pl.pallas_call(functools.partial(gram_kernel, offs=offs, off=off, at=at,...]
  transfers between devices with their start and end apart: 32 -> 32, of which waited for: 13 -> 9; matrix products, arithmetic and copies ran while one was open for 2% -> 1% of each run, Pallas kernels for 22% -> 22%
where the time goes in v3:
time: 227 us; the launch traced here: 226 us
  starting transfers between devices  91.5 us (40%)
  Pallas kernels  63.5 us (28%)
  waiting for transfers between devices  38.5 us (17%)
  blocking collectives  25 us (11%)
  local copies, waits for them, and re-layouts  5.69 us (3%)
    ppermute x31, starting transfers between devices, chain(): send = lambda x, pairs: lax.ppermute(x, 'docs', pairs)  91.5 us
    ppermute x31, waiting for transfers between devices, chain(): send = lambda x, pairs: lax.ppermute(x, 'docs', pairs)  38.5 us
    pallas_call x8, Pallas kernels, gram_call(): pl.pallas_call(functools.partial(gram_kernel, offs=offs, off=off, at=at,...  27.9 us
    all_to_all x1, blocking collectives, chain(): lax.all_to_all(jnp.broadcast_to(tab[None, :], (groups * 8, 8 * CAP)), ('g...  14.7 us
    all_to_all x1, blocking collectives, chain(): back = lax.all_to_all(state['score'], ('docs', 'tensor'), 0, 0, tiled=True)  10.4 us
    pallas_call x8, Pallas kernels, side_call(): pl.pallas_call(functools.partial(side_kernel, offs=offs, off=off, at=at,...  9.13 us
    pallas_call x8, Pallas kernels, mix_call(): pl.pallas_call(functools.partial(mix_kernel, first=first, off=off, at=at)...  6.8 us
    pallas_call x8, Pallas kernels, forward_call(): pl.pallas_call(functools.partial(forward_kernel, offs=offs, ahead=ahead),...  6.76 us
  transfers between devices with their start and end apart: 32, of which 9 were waited for; matrix products, arithmetic and copies ran while one was open for 1% of the time, Pallas kernels for 22%

profile of v3, /device:TPU:0, one launch (start us, length us, event | category | flops | bytes accessed | tf_op | source)
XLA Modules:
  0.0 225.9 jit_solution(10312424576179395285)
XLA Ops:
  1.5 3.1 %shard_map.64 = (s32[16]{0:T(128)S(1)}, s32[16]{0:T(128)S(1)}, s32[16]{0:T(128)S(1)}, bf16[8,32,1024]{2,1,0:T(8,128)(2,1)S(1)}, bf16[4,32,2048]{2,1,0:T(8,128)(2,1)S(1)}) custom-call(s32[2]{0:T(128)S(1)} %pad_add_fusion.me_ref, s32[16,1]{1,0:T(8,128)S(1)} %copy.8.doc_ref, s32[16]{0:T(128)S(1)} %copy-done.1, bf16[8,32,2048]{2,1,0:T(8,128)(2,1)} %own_ref.22, ...), custom_call_target="tpu_custom_call" | custom-call | bytes 1024 | tf_op jit(solution)/shard_map/pallas_call | solution.py:141
  5.3 5.9 %collective-permute-start.7 = (bf16[8,32,1024]{2,1,0:T(8,128)(2,1)S(1)}, bf16[8,32,1024]{2,1,0:T(8,128)(2,1)S(1)}, u32[]{:S(2)}, u32[]{:S(2)}) collective-permute-start(bf16[8,32,1024]{2,1,0:T(8,128)(2,1)S(1)} %get-tuple-element.48), channel_id=1, source_target_pairs={{0,4},{2,6},{4,0},{6,2},{8,12},{10,14},{12,8},{14,10},{1,5},{3,7},... | collective-permute-start | bytes 1572872 | tf_op jit(solution)/shard_map/ppermute | solution.py:473
  11.2 14.7 %all_to_all.13 = s32[16,1,16]{2,1,0:T(1,128)S(1)} all-to-all(s32[16,1,16]{2,1,0:T(1,128)S(1)} %broadcast_in_dim.4), channel_id=1, replica_groups=mesh['groups'=2,'docs'=8,'tensor'=2] {'groups','docs'}, dimensions={0} | all-to-all | bytes 2048 | tf_op jit(solution)/shard_map/all_to_all | solution.py:477
  25.9 1.4 shard_map.66.codes_ref.token_ref
  27.2 1.4 shard_map.67.token_ref
  29.5 1.4 collective-permute-start.9
  31.5 1.6 shard_map.69.token_ref
  33.2 3.6 %collective-permute-start.13 = (bf16[8,32,1024]{2,1,0:T(8,128)(2,1)}, bf16[8,32,1024]{2,1,0:T(8,128)(2,1)S(1)}, u32[]{:S(2)}, u32[]{:S(2)}) collective-permute-start(bf16[8,32,1024]{2,1,0:T(8,128)(2,1)} %shard_map.69.token_ref), channel_id=1, source_target_pairs={{0,4},{2,6},{4,0},{6,2},{8,12},{10,14},{12,8},{14,10},{1,5},{3,7},... | collective-permute-start | bytes 1572872 | tf_op jit(solution)/shard_map/ppermute | solution.py:473
  36.8 7.6 %collective-permute-done.9.came_ref.rest_2_ = bf16[8,32,1024]{2,1,0:T(8,128)(2,1)S(1)} collective-permute-done((bf16[8,32,1024]{2,1,0:T(8,128)(2,1)S(1)}, bf16[8,32,1024]{2,1,0:T(8,128)(2,1)S(1)}, u32[]{:S(2)}, u32[]{:S(2)}) %collective-permute-start.9) | collective-permute-done | bytes 524320 | tf_op jit(solution)/shard_map/ppermute | solution.py:473
  44.4 1.4 shard_map.70.rest_4_
  46.5 2.1 shard_map.65.codes_ref
  49.8 6.7 %conditional.1 = ((bf16[4,32,2048]{2,1,0:T(8,128)(2,1)}, bf16[4,32,5504]{2,1,0:T(8,128)(2,1)})) conditional(s32[]{:T(128)} %bitcast.3, s32[16]{0:T(128)S(1)} %get-tuple-element.49, (s32[16]{0:T(128)S(1)}, bf16[8,32,2048]{2,1,0:T(8,128)(2,1)S(1)}, bf16[8,32,5504]{2,1,0:T(8,128)(2,1)S(1)}) %tuple.33, (s32[16]{0:T(128)S(1)}, ...), branch_computations={%region_0.0_spmd, %region_1.2_spmd, %region_2.3_spmd, %region_3.4_... | conditional | bytes 18039944 | solution.py:489
  49.9 1.5 copy-done.4
  51.4 1.7 branch_1_fun.1
  55.4 1.2 pad.13
  56.6 2.0 shard_map.71.token_ref
  59.4 14.6 %collective-permute-start.11 = (bf16[8,32,1024]{2,1,0:T(8,128)(2,1)S(1)}, bf16[8,32,1024]{2,1,0:T(8,128)(2,1)S(1)}, u32[]{:S(2)}, u32[]{:S(2)}) collective-permute-start(bf16[8,32,1024]{2,1,0:T(8,128)(2,1)S(1)} %shard_map.71.token_ref), channel_id=1, source_target_pairs={{0,4},{2,6},{4,0},{6,2},{8,12},{10,14},{12,8},{14,10},{1,5},{3,7},... | collective-permute-start | bytes 1572872 | tf_op jit(solution)/shard_map/ppermute | solution.py:473
  76.5 5.6 %collective-permute-start.16 = (bf16[8,32,1024]{2,1,0:T(8,128)(2,1)S(1)}, bf16[8,32,1024]{2,1,0:T(8,128)(2,1)S(1)}, u32[]{:S(2)}, u32[]{:S(2)}) collective-permute-start(bf16[8,32,1024]{2,1,0:T(8,128)(2,1)S(1)} %shard_map.74.rest_5_), channel_id=1, source_target_pairs={{0,4},{2,6},{4,0},{6,2},{8,12},{10,14},{12,8},{14,10},{1,5},{3,7},... | collective-permute-start | bytes 1572872 | tf_op jit(solution)/shard_map/ppermute | solution.py:473
  82.1 4.8 %collective-permute-done.11.rest_4_.came_ref = bf16[8,32,1024]{2,1,0:T(8,128)(2,1)S(1)} collective-permute-done((bf16[8,32,1024]{2,1,0:T(8,128)(2,1)S(1)}, bf16[8,32,1024]{2,1,0:T(8,128)(2,1)S(1)}, u32[]{:S(2)}, u32[]{:S(2)}) %collective-permute-start.11) | collective-permute-done | bytes 524320 | tf_op jit(solution)/shard_map/ppermute | solution.py:473
  86.9 1.2 shard_map.75.token_ref
  88.1 10.0 %collective-permute-done.10.came_ref.rest_2_ = bf16[8,32,1024]{2,1,0:T(8,128)(2,1)S(1)} collective-permute-done((bf16[8,32,1024]{2,1,0:T(8,128)(2,1)S(1)}, bf16[8,32,1024]{2,1,0:T(8,128)(2,1)S(1)}, u32[]{:S(2)}, u32[]{:S(2)}) %collective-permute-start.10) | collective-permute-done | bytes 524320 | tf_op jit(solution)/shard_map/ppermute | solution.py:473
  100.9 6.5 %collective-permute-start.21 = (bf16[8,32,1024]{2,1,0:T(8,128)(2,1)S(1)}, bf16[8,32,1024]{2,1,0:T(8,128)(2,1)S(1)}, u32[]{:S(2)}, u32[]{:S(2)}) collective-permute-start(bf16[8,32,1024]{2,1,0:T(8,128)(2,1)S(1)} %shard_map.77.rest_5_), channel_id=1, source_target_pairs={{0,4},{2,6},{4,0},{6,2},{8,12},{10,14},{12,8},{14,10},{1,5},{3,7},... | collective-permute-start | bytes 1572872 | tf_op jit(solution)/shard_map/ppermute | solution.py:473
  107.4 2.0 collective-permute-done.16.rest_4_.came_ref
  111.2 2.5 %collective-permute-done.15.rest_5_ = bf16[8,32,1024]{2,1,0:T(8,128)(2,1)S(1)} collective-permute-done((bf16[8,32,1024]{2,1,0:T(8,128)(2,1)S(1)}, bf16[8,32,1024]{2,1,0:T(8,128)(2,1)S(1)}, u32[]{:S(2)}, u32[]{:S(2)}) %collective-permute-start.15) | collective-permute-done | bytes 524320 | tf_op jit(solution)/shard_map/ppermute | solution.py:473
  113.7 3.7 %shard_map.79.token_ref.rest_8_ = f32[512,768]{1,0:T(8,128)S(1)} custom-call(s32[2]{0:T(128)S(1)} %pad_add_fusion.me_ref, s32[64]{0:T(128)S(1)} %shard_map.65.codes_ref, bf16[8,32,2048]{2,1,0:T(8,128)(2,1)S(1)} %copy-done.9, bf16[8,32,1024]{2,1,0:T(8,128)(2,1)S(1)} %collective-permute-done.7.came_ref.rest_3_, ...), custom_call_target="tpu_custom_call" | custom-call | bytes 1024 | tf_op jit(solution)/shard_map/pallas_call | solution.py:434
  118.8 1.2 shard_map.82.rest_7_
  120.1 3.7 %shard_map.83.token_ref.rest_7_ = f32[512,768]{1,0:T(8,128)S(1)} custom-call(s32[2]{0:T(128)S(1)} %pad_add_fusion.me_ref, s32[64]{0:T(128)S(1)} %shard_map.65.codes_ref, bf16[8,32,2048]{2,1,0:T(8,128)(2,1)S(1)} %copy-done.9, bf16[8,32,1024]{2,1,0:T(8,128)(2,1)S(1)} %collective-permute-done.9.came_ref.rest_2_, ...), custom_call_target="tpu_custom_call" | custom-call | bytes 1024 | tf_op jit(solution)/shard_map/pallas_call | solution.py:434
  124.6 8.3 %collective-permute-start.18 = (bf16[8,32,1024]{2,1,0:T(8,128)(2,1)S(1)}, bf16[8,32,1024]{2,1,0:T(8,128)(2,1)S(1)}, u32[]{:S(2)}, u32[]{:S(2)}) collective-permute-start(bf16[8,32,1024]{2,1,0:T(8,128)(2,1)S(1)} %shard_map.81.rest_4_), channel_id=1, source_target_pairs={{0,4},{2,6},{4,0},{6,2},{8,12},{10,14},{12,8},{14,10},{1,5},{3,7},... | collective-permute-start | bytes 1572872 | tf_op jit(solution)/shard_map/ppermute | solution.py:473
  135.7 16.9 %collective-permute-start.23 = (bf16[8,32,1024]{2,1,0:T(8,128)(2,1)S(1)}, bf16[8,32,1024]{2,1,0:T(8,128)(2,1)S(1)}, u32[]{:S(2)}, u32[]{:S(2)}) collective-permute-start(bf16[8,32,1024]{2,1,0:T(8,128)(2,1)S(1)} %shard_map.85.rest_4_), channel_id=1, source_target_pairs={{0,4},{2,6},{4,0},{6,2},{8,12},{10,14},{12,8},{14,10},{1,5},{3,7},... | collective-permute-start | bytes 1572872 | tf_op jit(solution)/shard_map/ppermute | solution.py:473
  152.7 1.2 shard_map.86.rest_6_
  154.6 3.7 %shard_map.87.token_ref.rest_9_ = f32[16,256]{1,0:T(8,128)S(1)} custom-call(s32[2]{0:T(128)S(1)} %pad_add_fusion.me_ref, s32[64]{0:T(128)S(1)} %shard_map.65.codes_ref, bf16[8,32,5504]{2,1,0:T(8,128)(2,1)S(1)} %copy-done.3, bf16[8,32,1024]{2,1,0:T(8,128)(2,1)S(1)} %collective-permute-done.13.came_ref.rest_2_, ...), custom_call_target="tpu_custom_call" | custom-call | bytes 1024 | tf_op jit(solution)/shard_map/pallas_call | solution.py:434
  160.3 9.2 %collective-permute-start.29 = (bf16[8,32,1024]{2,1,0:T(8,128)(2,1)S(1)}, bf16[8,32,1024]{2,1,0:T(8,128)(2,1)S(1)}, u32[]{:S(2)}, u32[]{:S(2)}) collective-permute-start(bf16[8,32,1024]{2,1,0:T(8,128)(2,1)S(1)} %shard_map.89.rest_4_), channel_id=1, source_target_pairs={{0,4},{2,6},{4,0},{6,2},{8,12},{10,14},{12,8},{14,10},{1,5},{3,7},... | collective-permute-start | bytes 1572872 | tf_op jit(solution)/shard_map/ppermute | solution.py:473
  169.5 1.2 shard_map.90.rest_6_
  171.4 3.8 %shard_map.91.token_ref.rest_9_ = f32[16,256]{1,0:T(8,128)S(1)} custom-call(s32[2]{0:T(128)S(1)} %pad_add_fusion.me_ref, s32[64]{0:T(128)S(1)} %shard_map.65.codes_ref, bf16[8,32,5504]{2,1,0:T(8,128)(2,1)S(1)} %copy-done.3, bf16[8,32,1024]{2,1,0:T(8,128)(2,1)S(1)} %collective-permute-done.10.came_ref.rest_2_, ...), custom_call_target="tpu_custom_call" | custom-call | bytes 1024 | tf_op jit(solution)/shard_map/pallas_call | solution.py:434
  177.2 4.1 %collective-permute-done.29.rest_3_ = bf16[8,32,1024]{2,1,0:T(8,128)(2,1)S(1)} collective-permute-done((bf16[8,32,1024]{2,1,0:T(8,128)(2,1)S(1)}, bf16[8,32,1024]{2,1,0:T(8,128)(2,1)S(1)}, u32[]{:S(2)}, u32[]{:S(2)}) %collective-permute-start.29) | collective-permute-done | bytes 524320 | tf_op jit(solution)/shard_map/ppermute | solution.py:473
  181.3 1.2 shard_map.94.rest_6_
  183.2 1.8 collective-permute-start.33
  185.0 3.6 %shard_map.95.rest_3_.rest_9_ = f32[16,256]{1,0:T(8,128)S(1)} custom-call(s32[2]{0:T(128)S(1)} %pad_add_fusion.me_ref, s32[64]{0:T(128)S(1)} %shard_map.65.codes_ref, bf16[8,32,5504]{2,1,0:T(8,128)(2,1)S(1)} %copy-done.3, bf16[8,32,1024]{2,1,0:T(8,128)(2,1)S(1)} %collective-permute-done.11.rest_4_.came_ref, ...), custom_call_target="tpu_custom_call" | custom-call | bytes 1024 | tf_op jit(solution)/shard_map/pallas_call | solution.py:434
  189.3 3.0 %collective-permute-start.31 = (bf16[8,32,640]{2,1,0:T(8,128)(2,1)S(1)}, bf16[8,32,640]{2,1,0:T(8,128)(2,1)S(1)}, u32[]{:S(2)}, u32[]{:S(2)}) collective-permute-start(bf16[8,32,640]{2,1,0:T(8,128)(2,1)S(1)} %shard_map.96.rest_4_), channel_id=1, source_target_pairs={{0,4},{2,6},{4,0},{6,2},{8,12},{10,14},{12,8},{14,10},{1,5},{3,7},... | collective-permute-start | bytes 983048 | tf_op jit(solution)/shard_map/ppermute | solution.py:473
  192.3 2.0 collective-permute-done.33.rest_3_
  195.2 2.0 collective-permute-start.35
  197.2 3.6 %shard_map.98.rest_4_.rest_9_ = f32[16,256]{1,0:T(8,128)S(1)} custom-call(s32[2]{0:T(128)S(1)} %pad_add_fusion.me_ref, s32[64]{0:T(128)S(1)} %shard_map.65.codes_ref, bf16[8,32,5504]{2,1,0:T(8,128)(2,1)S(1)} %copy-done.3, bf16[8,32,1024]{2,1,0:T(8,128)(2,1)S(1)} %collective-permute-done.16.rest_4_.came_ref, ...), custom_call_target="tpu_custom_call" | custom-call | bytes 1024 | tf_op jit(solution)/shard_map/pallas_call | solution.py:434
  202.5 2.8 %collective-permute-done.35.rest_4_ = bf16[8,32,768]{2,1,0:T(8,128)(2,1)S(1)} collective-permute-done((bf16[8,32,768]{2,1,0:T(8,128)(2,1)S(1)}, bf16[8,32,768]{2,1,0:T(8,128)(2,1)S(1)}, u32[]{:S(2)}, u32[]{:S(2)}) %collective-permute-start.35) | collective-permute-done | bytes 393248 | tf_op jit(solution)/shard_map/ppermute | solution.py:473
  205.3 2.9 %shard_map.100.rest_6_.rest_9_ = f32[16,256]{1,0:T(8,128)S(1)} custom-call(s32[2]{0:T(128)S(1)} %pad_add_fusion.me_ref, s32[64]{0:T(128)S(1)} %shard_map.65.codes_ref, bf16[8,32,5504]{2,1,0:T(8,128)(2,1)S(1)} %copy-done.3, bf16[8,32,1024]{2,1,0:T(8,128)(2,1)S(1)} %collective-permute-done.21.rest_3_.came_ref, ...), custom_call_target="tpu_custom_call" | custom-call | bytes 1024 | tf_op jit(solution)/shard_map/pallas_call | solution.py:434
  208.2 2.8 %collective-permute-done.34.rest_4_ = bf16[8,32,640]{2,1,0:T(8,128)(2,1)S(1)} collective-permute-done((bf16[8,32,640]{2,1,0:T(8,128)(2,1)S(1)}, bf16[8,32,640]{2,1,0:T(8,128)(2,1)S(1)}, u32[]{:S(2)}, u32[]{:S(2)}) %collective-permute-start.34) | collective-permute-done | bytes 327712 | tf_op jit(solution)/shard_map/ppermute | solution.py:473
  211.0 2.8 %shard_map.101 = f32[16,2,128]{2,1,0:T(2,128)S(1)} custom-call(s32[2]{0:T(128)S(1)} %pad_add_fusion.me_ref, s32[64]{0:T(128)S(1)} %shard_map.65.codes_ref, bf16[8,32,5504]{2,1,0:T(8,128)(2,1)S(1)} %copy-done.3, bf16[8,32,1024]{2,1,0:T(8,128)(2,1)S(1)} %collective-permute-done.18.rest_3_.came_ref, bf16[12,32,640]{2,1,0:T(8,128)(2,1)S(1)} %collective-permute-done.27.rest_0_, ...), custom_call_target="tpu_custom_call" | custom-call | bytes 1024 | tf_op jit(solution)/shard_map/pallas_call | solution.py:434
  213.9 10.4 %all_to_all.14.came_ref = f32[16,2,128]{2,1,0:T(2,128)S(1)} all-to-all(f32[16,2,128]{2,1,0:T(2,128)S(1)} %shard_map.101), channel_id=1, replica_groups=mesh['groups'=2,'docs'=8,'tensor'=2] {'docs','tensor'}, dimensions={0} | all-to-all | bytes 32768 | tf_op jit(solution)/shard_map/all_to_all | solution.py:575
  224.3 1.5 shard_map.102
  (91 shorter events, 29.2 us)
Async XLA Ops:
  0.8 0.7 copy-start.1
  1.5 25.8 %copy-start.8 = (bf16[8,32,2048]{2,1,0:T(8,128)(2,1)S(1)}, bf16[8,32,2048]{2,1,0:T(8,128)(2,1)}, u32[]{:S(2)}) copy-start(bf16[8,32,2048]{2,1,0:T(8,128)(2,1)} %own_ref.22) | copy-start | bytes 3145732
  1.5 27.2 %copy-start.2 = (bf16[8,32,5504]{2,1,0:T(8,128)(2,1)S(1)}, bf16[8,32,5504]{2,1,0:T(8,128)(2,1)}, u32[]{:S(2)}) copy-start(bf16[8,32,5504]{2,1,0:T(8,128)(2,1)} %own_ref.31) | copy-start | bytes 8454148
  4.6 21.3 %collective-permute-start.6 = (bf16[4,32,2048]{2,1,0:T(8,128)(2,1)S(1)}, bf16[4,32,2048]{2,1,0:T(8,128)(2,1)S(1)}, u32[]{:S(2)}, u32[]{:S(2)}) collective-permute-start(bf16[4,32,2048]{2,1,0:T(8,128)(2,1)S(1)} %get-tuple-element.47), channel_id=1, source_target_pairs={{4,8},{6,10},{8,4},{10,6},{5,9},{7,11},{9,5},{11,7},{20,24},{22,26... | collective-permute-start | bytes 1572872 | tf_op jit(solution)/shard_map/ppermute | solution.py:473
  5.3 21.9 %collective-permute-start.7 = (bf16[8,32,1024]{2,1,0:T(8,128)(2,1)S(1)}, bf16[8,32,1024]{2,1,0:T(8,128)(2,1)S(1)}, u32[]{:S(2)}, u32[]{:S(2)}) collective-permute-start(bf16[8,32,1024]{2,1,0:T(8,128)(2,1)S(1)} %get-tuple-element.48), channel_id=1, source_target_pairs={{0,4},{2,6},{4,0},{6,2},{8,12},{10,14},{12,8},{14,10},{1,5},{3,7},... | collective-permute-start | bytes 1572872 | tf_op jit(solution)/shard_map/ppermute | solution.py:473
  29.5 14.9 %collective-permute-start.9 = (bf16[8,32,1024]{2,1,0:T(8,128)(2,1)S(1)}, bf16[8,32,1024]{2,1,0:T(8,128)(2,1)S(1)}, u32[]{:S(2)}, u32[]{:S(2)}) collective-permute-start(bf16[8,32,1024]{2,1,0:T(8,128)(2,1)S(1)} %shard_map.68.token_ref), channel_id=1, source_target_pairs={{0,4},{2,6},{4,0},{6,2},{8,12},{10,14},{12,8},{14,10},{1,5},{3,7},... | collective-permute-start | bytes 1572872 | tf_op jit(solution)/shard_map/ppermute | solution.py:473
  30.9 25.7 %collective-permute-start.8 = (bf16[8,32,1024]{2,1,0:T(8,128)(2,1)}, bf16[8,32,1024]{2,1,0:T(8,128)(2,1)S(1)}, u32[]{:S(2)}, u32[]{:S(2)}) collective-permute-start(bf16[8,32,1024]{2,1,0:T(8,128)(2,1)} %shard_map.67.token_ref), channel_id=1, source_target_pairs={{4,8},{6,10},{8,4},{10,6},{5,9},{7,11},{9,5},{11,7},{20,24},{22,26... | collective-permute-start | bytes 1572872 | tf_op jit(solution)/shard_map/ppermute | solution.py:473
  33.2 41.0 %collective-permute-start.13 = (bf16[8,32,1024]{2,1,0:T(8,128)(2,1)}, bf16[8,32,1024]{2,1,0:T(8,128)(2,1)S(1)}, u32[]{:S(2)}, u32[]{:S(2)}) collective-permute-start(bf16[8,32,1024]{2,1,0:T(8,128)(2,1)} %shard_map.69.token_ref), channel_id=1, source_target_pairs={{0,4},{2,6},{4,0},{6,2},{8,12},{10,14},{12,8},{14,10},{1,5},{3,7},... | collective-permute-start | bytes 1572872 | tf_op jit(solution)/shard_map/ppermute | solution.py:473
  45.8 29.9 %collective-permute-start.12 = (bf16[8,32,1024]{2,1,0:T(8,128)(2,1)}, bf16[8,32,1024]{2,1,0:T(8,128)(2,1)S(1)}, u32[]{:S(2)}, u32[]{:S(2)}) collective-permute-start(bf16[8,32,1024]{2,1,0:T(8,128)(2,1)} %shard_map.70.rest_4_), channel_id=1, source_target_pairs={{4,8},{6,10},{8,4},{10,6},{5,9},{7,11},{9,5},{11,7},{20,24},{22,26... | collective-permute-start | bytes 1572872 | tf_op jit(solution)/shard_map/ppermute | solution.py:473
  49.9 1.5 copy-start.4
  53.1 2.2 collective-permute-start.1
  53.8 0.7 collective-permute-start
  56.6 2.0 copy-start.3
  59.4 16.3 %copy-start.11 = (bf16[4,32,2048]{2,1,0:T(8,128)(2,1)S(1)}, bf16[4,32,2048]{2,1,0:T(8,128)(2,1)}, u32[]{:S(2)}) copy-start(bf16[4,32,2048]{2,1,0:T(8,128)(2,1)} %get-tuple-element.50.rest_2_) | copy-start | bytes 1572868
  59.4 27.5 %collective-permute-start.11 = (bf16[8,32,1024]{2,1,0:T(8,128)(2,1)S(1)}, bf16[8,32,1024]{2,1,0:T(8,128)(2,1)S(1)}, u32[]{:S(2)}, u32[]{:S(2)}) collective-permute-start(bf16[8,32,1024]{2,1,0:T(8,128)(2,1)S(1)} %shard_map.71.token_ref), channel_id=1, source_target_pairs={{0,4},{2,6},{4,0},{6,2},{8,12},{10,14},{12,8},{14,10},{1,5},{3,7},... | collective-permute-start | bytes 1572872 | tf_op jit(solution)/shard_map/ppermute | solution.py:473
  74.1 24.1 %collective-permute-start.10 = (bf16[8,32,1024]{2,1,0:T(8,128)(2,1)S(1)}, bf16[8,32,1024]{2,1,0:T(8,128)(2,1)S(1)}, u32[]{:S(2)}, u32[]{:S(2)}) collective-permute-start(bf16[8,32,1024]{2,1,0:T(8,128)(2,1)S(1)} %shard_map.72.token_ref), channel_id=1, source_target_pairs={{0,4},{2,6},{4,0},{6,2},{8,12},{10,14},{12,8},{14,10},{1,5},{3,7},... | collective-permute-start | bytes 1572872 | tf_op jit(solution)/shard_map/ppermute | solution.py:473
  74.8 12.1 %copy-start.9 = (bf16[8,32,2048]{2,1,0:T(8,128)(2,1)S(1)}, bf16[8,32,2048]{2,1,0:T(8,128)(2,1)}, u32[]{:S(2)}) copy-start(bf16[8,32,2048]{2,1,0:T(8,128)(2,1)} %own_ref.22) | copy-start | bytes 3145732
  74.8 25.3 %collective-permute-start.17 = (bf16[12,32,1024]{2,1,0:T(8,128)(2,1)S(1)}, bf16[12,32,1024]{2,1,0:T(8,128)(2,1)S(1)}, u32[]{:S(2)}, u32[]{:S(2)}) collective-permute-start(bf16[12,32,1024]{2,1,0:T(8,128)(2,1)S(1)} %shard_map.73.rest_4_), channel_id=1, source_target_pairs={{4,8},{6,10},{8,4},{10,6},{5,9},{7,11},{9,5},{11,7},{20,24},{22,26... | collective-permute-start | bytes 2359304 | tf_op jit(solution)/shard_map/ppermute | solution.py:473
  76.5 32.9 %collective-permute-start.16 = (bf16[8,32,1024]{2,1,0:T(8,128)(2,1)S(1)}, bf16[8,32,1024]{2,1,0:T(8,128)(2,1)S(1)}, u32[]{:S(2)}, u32[]{:S(2)}) collective-permute-start(bf16[8,32,1024]{2,1,0:T(8,128)(2,1)S(1)} %shard_map.74.rest_5_), channel_id=1, source_target_pairs={{0,4},{2,6},{4,0},{6,2},{8,12},{10,14},{12,8},{14,10},{1,5},{3,7},... | collective-permute-start | bytes 1572872 | tf_op jit(solution)/shard_map/ppermute | solution.py:473
  88.1 12.0 %copy-start.7 = (bf16[4,32,5504]{2,1,0:T(8,128)(2,1)S(1)}, bf16[4,32,5504]{2,1,0:T(8,128)(2,1)}, u32[]{:S(2)}) copy-start(bf16[4,32,5504]{2,1,0:T(8,128)(2,1)} %get-tuple-element.51.rest_1_) | copy-start | bytes 4227076
  98.8 19.2 %collective-permute-start.14 = (bf16[12,32,1024]{2,1,0:T(8,128)(2,1)S(1)}, bf16[12,32,1024]{2,1,0:T(8,128)(2,1)S(1)}, u32[]{:S(2)}, u32[]{:S(2)}) collective-permute-start(bf16[12,32,1024]{2,1,0:T(8,128)(2,1)S(1)} %shard_map.76.rest_3_), channel_id=1, source_target_pairs={{4,8},{6,10},{8,4},{10,6},{5,9},{7,11},{9,5},{11,7},{20,24},{22,26... | collective-permute-start | bytes 2359304 | tf_op jit(solution)/shard_map/ppermute | solution.py:473
  99.5 14.1 %collective-permute-start.15 = (bf16[8,32,1024]{2,1,0:T(8,128)(2,1)S(1)}, bf16[8,32,1024]{2,1,0:T(8,128)(2,1)S(1)}, u32[]{:S(2)}, u32[]{:S(2)}) collective-permute-start(bf16[8,32,1024]{2,1,0:T(8,128)(2,1)S(1)} %shard_map.75.token_ref), channel_id=1, source_target_pairs={{0,2},{2,0},{4,6},{6,4},{8,10},{10,8},{12,14},{14,12},{1,3},{3,1},... | collective-permute-start | bytes 1572872 | tf_op jit(solution)/shard_map/ppermute | solution.py:473
  100.9 12.8 %copy-start = (bf16[1,768,2048]{2,1,0:T(8,128)(2,1)S(1)}, bf16[1,768,2048]{2,1,0:T(8,128)(2,1)}, u32[]{:S(2)}) copy-start(bf16[1,768,2048]{2,1,0:T(8,128)(2,1)} %rest_6_.3) | copy-start | bytes 9437188
  100.9 17.9 %collective-permute-start.21 = (bf16[8,32,1024]{2,1,0:T(8,128)(2,1)S(1)}, bf16[8,32,1024]{2,1,0:T(8,128)(2,1)S(1)}, u32[]{:S(2)}, u32[]{:S(2)}) collective-permute-start(bf16[8,32,1024]{2,1,0:T(8,128)(2,1)S(1)} %shard_map.77.rest_5_), channel_id=1, source_target_pairs={{0,4},{2,6},{4,0},{6,2},{8,12},{10,14},{12,8},{14,10},{1,5},{3,7},... | collective-permute-start | bytes 1572872 | tf_op jit(solution)/shard_map/ppermute | solution.py:473
  110.6 9.4 %collective-permute-start.20 = (bf16[8,32,1024]{2,1,0:T(8,128)(2,1)S(1)}, bf16[8,32,1024]{2,1,0:T(8,128)(2,1)S(1)}, u32[]{:S(2)}, u32[]{:S(2)}) collective-permute-start(bf16[8,32,1024]{2,1,0:T(8,128)(2,1)S(1)} %shard_map.78.rest_7_), channel_id=1, source_target_pairs={{0,2},{2,0},{4,6},{6,4},{8,10},{10,8},{12,14},{14,12},{1,3},{3,1},... | collective-permute-start | bytes 1572872 | tf_op jit(solution)/shard_map/ppermute | solution.py:473
  120.0 34.5 %slice-start = ((s8[8454144]{0:T(1024)(128)(4,1)}), s8[4194304]{0:T(1024)(128)(4,1)S(1)}, s32[]{:S(2)}) async-start(s8[8454144]{0:T(1024)(128)(4,1)} %bitcast.4), calls=%async_computation.2 | async-start | bytes 8388608
  120.1 34.5 %slice-start.1 = ((s8[8454144]{0:T(1024)(128)(4,1)}), s8[4194304]{0:T(1024)(128)(4,1)S(1)}, s32[]{:S(2)}) async-start(s8[8454144]{0:T(1024)(128)(4,1)} %bitcast.4), calls=%async_computation.3 | async-start | bytes 8388608
  123.8 30.8 %collective-permute-start.26 = (f32[512,768]{1,0:T(8,128)S(1)}, f32[512,768]{1,0:T(8,128)S(1)}, u32[]{:S(2)}, u32[]{:S(2)}) collective-permute-start(f32[512,768]{1,0:T(8,128)S(1)} %shard_map.83.token_ref.rest_7_), channel_id=1, source_target_pairs={{0,1},{1,0},{2,3},{3,2},{4,5},{5,4},{6,7},{7,6},{8,9},{9,8},{10,11... | collective-permute-start | bytes 4718600 | tf_op jit(solution)/shard_map/ppermute | solution.py:548
  123.9 11.3 %collective-permute-start.19 = (bf16[12,32,1024]{2,1,0:T(8,128)(2,1)S(1)}, bf16[12,32,1024]{2,1,0:T(8,128)(2,1)S(1)}, u32[]{:S(2)}, u32[]{:S(2)}) collective-permute-start(bf16[12,32,1024]{2,1,0:T(8,128)(2,1)S(1)} %shard_map.80.rest_3_), channel_id=1, source_target_pairs={{4,8},{6,10},{8,4},{10,6},{5,9},{7,11},{9,5},{11,7},{20,24},{22,26... | collective-permute-start | bytes 2359304 | tf_op jit(solution)/shard_map/ppermute | solution.py:473
  124.6 28.1 %collective-permute-start.18 = (bf16[8,32,1024]{2,1,0:T(8,128)(2,1)S(1)}, bf16[8,32,1024]{2,1,0:T(8,128)(2,1)S(1)}, u32[]{:S(2)}, u32[]{:S(2)}) collective-permute-start(bf16[8,32,1024]{2,1,0:T(8,128)(2,1)S(1)} %shard_map.81.rest_4_), channel_id=1, source_target_pairs={{0,4},{2,6},{4,0},{6,2},{8,12},{10,14},{12,8},{14,10},{1,5},{3,7},... | collective-permute-start | bytes 1572872 | tf_op jit(solution)/shard_map/ppermute | solution.py:473
  133.5 21.0 %slice-start.2 = ((s8[8454144]{0:T(1024)(128)(4,1)}), s8[65536]{0:T(1024)(128)(4,1)S(1)}, s32[]{:S(2)}) async-start(s8[8454144]{0:T(1024)(128)(4,1)} %bitcast.4), calls=%async_computation.4 | async-start | bytes 131072
  133.6 26.1 %collective-permute-start.24 = (bf16[12,32,1024]{2,1,0:T(8,128)(2,1)S(1)}, bf16[12,32,1024]{2,1,0:T(8,128)(2,1)S(1)}, u32[]{:S(2)}, u32[]{:S(2)}) collective-permute-start(bf16[12,32,1024]{2,1,0:T(8,128)(2,1)S(1)} %shard_map.84.rest_3_), channel_id=1, source_target_pairs={{4,8},{6,10},{8,4},{10,6},{5,9},{7,11},{9,5},{11,7},{20,24},{22,26... | collective-permute-start | bytes 2359304 | tf_op jit(solution)/shard_map/ppermute | solution.py:473
  134.4 20.1 %collective-permute-start.25 = (bf16[8,32,1024]{2,1,0:T(8,128)(2,1)S(1)}, bf16[8,32,1024]{2,1,0:T(8,128)(2,1)S(1)}, u32[]{:S(2)}, u32[]{:S(2)}) collective-permute-start(bf16[8,32,1024]{2,1,0:T(8,128)(2,1)S(1)} %shard_map.82.rest_7_), channel_id=1, source_target_pairs={{0,2},{2,0},{4,6},{6,4},{8,10},{10,8},{12,14},{14,12},{1,3},{3,1},... | collective-permute-start | bytes 1572872 | tf_op jit(solution)/shard_map/ppermute | solution.py:473
  135.7 33.8 %collective-permute-start.23 = (bf16[8,32,1024]{2,1,0:T(8,128)(2,1)S(1)}, bf16[8,32,1024]{2,1,0:T(8,128)(2,1)S(1)}, u32[]{:S(2)}, u32[]{:S(2)}) collective-permute-start(bf16[8,32,1024]{2,1,0:T(8,128)(2,1)S(1)} %shard_map.85.rest_4_), channel_id=1, source_target_pairs={{0,4},{2,6},{4,0},{6,2},{8,12},{10,14},{12,8},{14,10},{1,5},{3,7},... | collective-permute-start | bytes 1572872 | tf_op jit(solution)/shard_map/ppermute | solution.py:473
  153.9 17.5 %collective-permute-start.22 = (bf16[8,32,1024]{2,1,0:T(8,128)(2,1)S(1)}, bf16[8,32,1024]{2,1,0:T(8,128)(2,1)S(1)}, u32[]{:S(2)}, u32[]{:S(2)}) collective-permute-start(bf16[8,32,1024]{2,1,0:T(8,128)(2,1)S(1)} %shard_map.86.rest_6_), channel_id=1, source_target_pairs={{0,2},{2,0},{4,6},{6,4},{8,10},{10,8},{12,14},{14,12},{1,3},{3,1},... | collective-permute-start | bytes 1572872 | tf_op jit(solution)/shard_map/ppermute | solution.py:473
  158.9 17.7 %collective-permute-start.30 = (bf16[12,32,768]{2,1,0:T(8,128)(2,1)S(1)}, bf16[12,32,768]{2,1,0:T(8,128)(2,1)S(1)}, u32[]{:S(2)}, u32[]{:S(2)}) collective-permute-start(bf16[12,32,768]{2,1,0:T(8,128)(2,1)S(1)} %shard_map.88.rest_3_), channel_id=1, source_target_pairs={{4,8},{6,10},{8,4},{10,6},{5,9},{7,11},{9,5},{11,7},{20,24},{22,26... | collective-permute-start | bytes 1769480 | tf_op jit(solution)/shard_map/ppermute | solution.py:473
  160.3 21.0 %collective-permute-start.29 = (bf16[8,32,1024]{2,1,0:T(8,128)(2,1)S(1)}, bf16[8,32,1024]{2,1,0:T(8,128)(2,1)S(1)}, u32[]{:S(2)}, u32[]{:S(2)}) collective-permute-start(bf16[8,32,1024]{2,1,0:T(8,128)(2,1)S(1)} %shard_map.89.rest_4_), channel_id=1, source_target_pairs={{0,4},{2,6},{4,0},{6,2},{8,12},{10,14},{12,8},{14,10},{1,5},{3,7},... | collective-permute-start | bytes 1572872 | tf_op jit(solution)/shard_map/ppermute | solution.py:473
  170.8 14.2 %collective-permute-start.28 = (bf16[8,32,1024]{2,1,0:T(8,128)(2,1)S(1)}, bf16[8,32,1024]{2,1,0:T(8,128)(2,1)S(1)}, u32[]{:S(2)}, u32[]{:S(2)}) collective-permute-start(bf16[8,32,1024]{2,1,0:T(8,128)(2,1)S(1)} %shard_map.90.rest_6_), channel_id=1, source_target_pairs={{0,2},{2,0},{4,6},{6,4},{8,10},{10,8},{12,14},{14,12},{1,3},{3,1},... | collective-permute-start | bytes 1572872 | tf_op jit(solution)/shard_map/ppermute | solution.py:473
  175.9 12.7 %collective-permute-start.27 = (bf16[12,32,640]{2,1,0:T(8,128)(2,1)S(1)}, bf16[12,32,640]{2,1,0:T(8,128)(2,1)S(1)}, u32[]{:S(2)}, u32[]{:S(2)}) collective-permute-start(bf16[12,32,640]{2,1,0:T(8,128)(2,1)S(1)} %shard_map.92.rest_3_), channel_id=1, source_target_pairs={{4,8},{6,10},{8,4},{10,6},{5,9},{7,11},{9,5},{11,7},{20,24},{22,26... | collective-permute-start | bytes 1474568 | tf_op jit(solution)/shard_map/ppermute | solution.py:473
  182.5 14.7 %collective-permute-start.32 = (bf16[8,32,1024]{2,1,0:T(8,128)(2,1)S(1)}, bf16[8,32,1024]{2,1,0:T(8,128)(2,1)S(1)}, u32[]{:S(2)}, u32[]{:S(2)}) collective-permute-start(bf16[8,32,1024]{2,1,0:T(8,128)(2,1)S(1)} %shard_map.94.rest_6_), channel_id=1, source_target_pairs={{0,2},{2,0},{4,6},{6,4},{8,10},{10,8},{12,14},{14,12},{1,3},{3,1},... | collective-permute-start | bytes 1572872 | tf_op jit(solution)/shard_map/ppermute | solution.py:473
  183.2 11.0 %collective-permute-start.33 = (bf16[8,32,768]{2,1,0:T(8,128)(2,1)S(1)}, bf16[8,32,768]{2,1,0:T(8,128)(2,1)S(1)}, u32[]{:S(2)}, u32[]{:S(2)}) collective-permute-start(bf16[8,32,768]{2,1,0:T(8,128)(2,1)S(1)} %shard_map.93.rest_4_), channel_id=1, source_target_pairs={{0,4},{2,6},{4,0},{6,2},{8,12},{10,14},{12,8},{14,10},{1,5},{3,7},... | collective-permute-start | bytes 1179656 | tf_op jit(solution)/shard_map/ppermute | solution.py:473
  189.3 11.6 %collective-permute-start.31 = (bf16[8,32,640]{2,1,0:T(8,128)(2,1)S(1)}, bf16[8,32,640]{2,1,0:T(8,128)(2,1)S(1)}, u32[]{:S(2)}, u32[]{:S(2)}) collective-permute-start(bf16[8,32,640]{2,1,0:T(8,128)(2,1)S(1)} %shard_map.96.rest_4_), channel_id=1, source_target_pairs={{0,4},{2,6},{4,0},{6,2},{8,12},{10,14},{12,8},{14,10},{1,5},{3,7},... | collective-permute-start | bytes 983048 | tf_op jit(solution)/shard_map/ppermute | solution.py:473
  195.2 10.1 %collective-permute-start.35 = (bf16[8,32,768]{2,1,0:T(8,128)(2,1)S(1)}, bf16[8,32,768]{2,1,0:T(8,128)(2,1)S(1)}, u32[]{:S(2)}, u32[]{:S(2)}) collective-permute-start(bf16[8,32,768]{2,1,0:T(8,128)(2,1)S(1)} %shard_map.97.rest_6_), channel_id=1, source_target_pairs={{0,2},{2,0},{4,6},{6,4},{8,10},{10,8},{12,14},{14,12},{1,3},{3,1},... | collective-permute-start | bytes 1179656 | tf_op jit(solution)/shard_map/ppermute | solution.py:473
  201.8 9.2 %collective-permute-start.34 = (bf16[8,32,640]{2,1,0:T(8,128)(2,1)S(1)}, bf16[8,32,640]{2,1,0:T(8,128)(2,1)S(1)}, u32[]{:S(2)}, u32[]{:S(2)}) collective-permute-start(bf16[8,32,640]{2,1,0:T(8,128)(2,1)S(1)} %shard_map.99.rest_6_), channel_id=1, source_target_pairs={{0,2},{2,0},{4,6},{6,4},{8,10},{10,8},{12,14},{14,12},{1,3},{3,1},... | collective-permute-start | bytes 983048 | tf_op jit(solution)/shard_map/ppermute | solution.py:473

commit v4 on v3

--- a/solution.py
+++ b/solution.py
@@ -560,7 +560,8 @@
         return out
 
     token = ahead_block(1, token)
-    token = ahead_block(2, token)
+    ahead_block(2, token)
+    token = extras[0]
     for i in range(total + 2):
         if i + 1 < total:
             token = mix(i + 1, token)

time: 227 us -> 206 us (0.907)
  starting transfers between devices: 91.5 us -> 82 us
  waiting for transfers between devices: 38.5 us -> 34.5 us
  local copies, waits for them, and re-layouts: 5.69 us -> 2.02 us
    ppermute x31 -> x29, starting transfers between devices: 91.5 us -> 81.9 us  [chain(): send = lambda x, pairs: lax.ppermute(x, 'docs', pairs)]
    ppermute x31 -> x29, waiting for transfers between devices: 38.5 us -> 34.5 us  [chain(): send = lambda x, pairs: lax.ppermute(x, 'docs', pairs)]
  transfers between devices with their start and end apart: 32 -> 30, of which waited for: 9 -> 11; matrix products, arithmetic and copies ran while one was open for 1% -> 0% of each run, Pallas kernels for 22% -> 23%
where the time goes in v4:
time: 206 us
  starting transfers between devices  82 us (40%)
  Pallas kernels  61.3 us (30%)
  waiting for transfers between devices  34.5 us (17%)
  blocking collectives  24.4 us (12%)
    ppermute x29, starting transfers between devices, chain(): send = lambda x, pairs: lax.ppermute(x, 'docs', pairs)  81.9 us
    ppermute x29, waiting for transfers between devices, chain(): send = lambda x, pairs: lax.ppermute(x, 'docs', pairs)  34.5 us
    pallas_call x8, Pallas kernels, gram_call(): pl.pallas_call(functools.partial(gram_kernel, offs=offs, off=off, at=at,...  27.9 us
    all_to_all x1, blocking collectives, chain(): lax.all_to_all(jnp.broadcast_to(tab[None, :], (groups * 8, 8 * CAP)), ('g...  14.7 us
    all_to_all x1, blocking collectives, chain(): back = lax.all_to_all(state['score'], ('docs', 'tensor'), 0, 0, tiled=True)  9.74 us
    pallas_call x8, Pallas kernels, side_call(): pl.pallas_call(functools.partial(side_kernel, offs=offs, off=off, at=at,...  9.13 us
    pallas_call x8, Pallas kernels, forward_call(): pl.pallas_call(functools.partial(forward_kernel, offs=offs, ahead=ahead),...  6.5 us
    pallas_call x8, Pallas kernels, mix_call(): pl.pallas_call(functools.partial(mix_kernel, first=first, off=off, at=at)...  5.22 us
  transfers between devices with their start and end apart: 30, of which 11 were waited for; matrix products, arithmetic and copies ran while one was open for 0% of the time, Pallas kernels for 23%

profile of v4, /device:TPU:0, one launch (start us, length us, event | category | flops | bytes accessed | tf_op | source)
XLA Modules:
  0.0 205.7 jit_solution(3620850396420193145)
XLA Ops:
  1.5 3.1 %shard_map.64 = (s32[16]{0:T(128)S(1)}, s32[16]{0:T(128)S(1)}, s32[16]{0:T(128)S(1)}, bf16[8,32,1024]{2,1,0:T(8,128)(2,1)S(1)}, bf16[4,32,2048]{2,1,0:T(8,128)(2,1)S(1)}) custom-call(s32[2]{0:T(128)S(1)} %pad_add_fusion.me_ref, s32[16,1]{1,0:T(8,128)S(1)} %copy.8.doc_ref, s32[16]{0:T(128)S(1)} %copy-done.1, bf16[8,32,2048]{2,1,0:T(8,128)(2,1)} %own_ref.22, ...), custom_call_target="tpu_custom_call" | custom-call | bytes 1024 | tf_op jit(solution)/shard_map/pallas_call | solution.py:141
  5.3 5.9 %collective-permute-start.7 = (bf16[8,32,1024]{2,1,0:T(8,128)(2,1)S(1)}, bf16[8,32,1024]{2,1,0:T(8,128)(2,1)S(1)}, u32[]{:S(2)}, u32[]{:S(2)}) collective-permute-start(bf16[8,32,1024]{2,1,0:T(8,128)(2,1)S(1)} %get-tuple-element.48), channel_id=1, source_target_pairs={{0,4},{2,6},{4,0},{6,2},{8,12},{10,14},{12,8},{14,10},{1,5},{3,7},... | collective-permute-start | bytes 1572872 | tf_op jit(solution)/shard_map/ppermute | solution.py:473
  11.2 14.7 %all_to_all.13 = s32[16,1,16]{2,1,0:T(1,128)S(1)} all-to-all(s32[16,1,16]{2,1,0:T(1,128)S(1)} %broadcast_in_dim.4), channel_id=1, replica_groups=mesh['groups'=2,'docs'=8,'tensor'=2] {'groups','docs'}, dimensions={0} | all-to-all | bytes 2048 | tf_op jit(solution)/shard_map/all_to_all | solution.py:477
  25.9 1.4 shard_map.66.codes_ref.token_ref
  27.9 1.6 shard_map.68.token_ref
  29.5 1.4 collective-permute-start.9
  31.6 1.6 shard_map.72
  33.2 3.6 %collective-permute-start.13 = (bf16[8,32,1024]{2,1,0:T(8,128)(2,1)}, bf16[8,32,1024]{2,1,0:T(8,128)(2,1)S(1)}, u32[]{:S(2)}, u32[]{:S(2)}) collective-permute-start(bf16[8,32,1024]{2,1,0:T(8,128)(2,1)} %shard_map.72), channel_id=1, source_target_pairs={{0,4},{2,6},{4,0},{6,2},{8,12},{10,14},{12,8},{14,10},{1,5},{3,7},... | collective-permute-start | bytes 1572872 | tf_op jit(solution)/shard_map/ppermute | solution.py:473
  36.8 2.0 shard_map.65.codes_ref
  40.7 4.0 %collective-permute-done.9.came_ref.rest_2_ = bf16[8,32,1024]{2,1,0:T(8,128)(2,1)S(1)} collective-permute-done((bf16[8,32,1024]{2,1,0:T(8,128)(2,1)}, bf16[8,32,1024]{2,1,0:T(8,128)(2,1)S(1)}, u32[]{:S(2)}, u32[]{:S(2)}) %collective-permute-start.9) | collective-permute-done | bytes 524320 | tf_op jit(solution)/shard_map/ppermute | solution.py:473
  46.1 1.7 shard_map.70.token_ref
  48.7 5.3 %collective-permute-start.11 = (bf16[8,32,1024]{2,1,0:T(8,128)(2,1)S(1)}, bf16[8,32,1024]{2,1,0:T(8,128)(2,1)S(1)}, u32[]{:S(2)}, u32[]{:S(2)}) collective-permute-start(bf16[8,32,1024]{2,1,0:T(8,128)(2,1)S(1)} %shard_map.70.token_ref), channel_id=1, source_target_pairs={{0,4},{2,6},{4,0},{6,2},{8,12},{10,14},{12,8},{14,10},{1,5},{3,7},... | collective-permute-start | bytes 1572872 | tf_op jit(solution)/shard_map/ppermute | solution.py:473
  54.0 1.9 collective-permute-done.13.came_ref.rest_2_
  56.6 0.8 collective-permute-start.17
  58.2 5.4 %collective-permute-start.16 = (bf16[8,32,1024]{2,1,0:T(8,128)(2,1)S(1)}, bf16[8,32,1024]{2,1,0:T(8,128)(2,1)S(1)}, u32[]{:S(2)}, u32[]{:S(2)}) collective-permute-start(bf16[8,32,1024]{2,1,0:T(8,128)(2,1)S(1)} %shard_map.74.rest_5_), channel_id=1, source_target_pairs={{0,4},{2,6},{4,0},{6,2},{8,12},{10,14},{12,8},{14,10},{1,5},{3,7},... | collective-permute-start | bytes 1572872 | tf_op jit(solution)/shard_map/ppermute | solution.py:473
  63.6 3.5 %collective-permute-done.11.rest_4_.came_ref = bf16[8,32,1024]{2,1,0:T(8,128)(2,1)S(1)} collective-permute-done((bf16[8,32,1024]{2,1,0:T(8,128)(2,1)S(1)}, bf16[8,32,1024]{2,1,0:T(8,128)(2,1)S(1)}, u32[]{:S(2)}, u32[]{:S(2)}) %collective-permute-start.11) | collective-permute-done | bytes 524320 | tf_op jit(solution)/shard_map/ppermute | solution.py:473
  67.1 1.2 shard_map.75.token_ref
  68.3 10.0 %collective-permute-done.10.came_ref.rest_2_ = bf16[8,32,1024]{2,1,0:T(8,128)(2,1)S(1)} collective-permute-done((bf16[8,32,1024]{2,1,0:T(8,128)(2,1)S(1)}, bf16[8,32,1024]{2,1,0:T(8,128)(2,1)S(1)}, u32[]{:S(2)}, u32[]{:S(2)}) %collective-permute-start.10) | collective-permute-done | bytes 524320 | tf_op jit(solution)/shard_map/ppermute | solution.py:473
  81.2 5.5 %collective-permute-start.21 = (bf16[8,32,1024]{2,1,0:T(8,128)(2,1)S(1)}, bf16[8,32,1024]{2,1,0:T(8,128)(2,1)S(1)}, u32[]{:S(2)}, u32[]{:S(2)}) collective-permute-start(bf16[8,32,1024]{2,1,0:T(8,128)(2,1)S(1)} %shard_map.77.rest_5_), channel_id=1, source_target_pairs={{0,4},{2,6},{4,0},{6,2},{8,12},{10,14},{12,8},{14,10},{1,5},{3,7},... | collective-permute-start | bytes 1572872 | tf_op jit(solution)/shard_map/ppermute | solution.py:473
  86.7 2.9 %collective-permute-done.16.rest_4_.came_ref = bf16[8,32,1024]{2,1,0:T(8,128)(2,1)S(1)} collective-permute-done((bf16[8,32,1024]{2,1,0:T(8,128)(2,1)S(1)}, bf16[8,32,1024]{2,1,0:T(8,128)(2,1)S(1)}, u32[]{:S(2)}, u32[]{:S(2)}) %collective-permute-start.16) | collective-permute-done | bytes 524320 | tf_op jit(solution)/shard_map/ppermute | solution.py:473
  89.6 1.2 shard_map.78.rest_7_
  91.5 3.7 %shard_map.79.token_ref.rest_8_ = f32[512,768]{1,0:T(8,128)S(1)} custom-call(s32[2]{0:T(128)S(1)} %pad_add_fusion.me_ref, s32[64]{0:T(128)S(1)} %shard_map.65.codes_ref, bf16[8,32,2048]{2,1,0:T(8,128)(2,1)S(1)} %copy-done.9, bf16[8,32,1024]{2,1,0:T(8,128)(2,1)S(1)} %collective-permute-done.7.came_ref.rest_3_, ...), custom_call_target="tpu_custom_call" | custom-call | bytes 1024 | tf_op jit(solution)/shard_map/pallas_call | solution.py:434
  96.6 1.5 collective-permute-done.21.rest_3_.came_ref
  98.1 1.2 shard_map.82.rest_7_
  99.3 0.9 collective-permute-done.20.rest_5_
  100.2 3.7 %shard_map.83.token_ref.rest_7_ = f32[512,768]{1,0:T(8,128)S(1)} custom-call(s32[2]{0:T(128)S(1)} %pad_add_fusion.me_ref, s32[64]{0:T(128)S(1)} %shard_map.65.codes_ref, bf16[8,32,2048]{2,1,0:T(8,128)(2,1)S(1)} %copy-done.9, bf16[8,32,1024]{2,1,0:T(8,128)(2,1)S(1)} %collective-permute-done.9.came_ref.rest_2_, ...), custom_call_target="tpu_custom_call" | custom-call | bytes 1024 | tf_op jit(solution)/shard_map/pallas_call | solution.py:434
  104.7 7.4 %collective-permute-start.18 = (bf16[8,32,1024]{2,1,0:T(8,128)(2,1)S(1)}, bf16[8,32,1024]{2,1,0:T(8,128)(2,1)S(1)}, u32[]{:S(2)}, u32[]{:S(2)}) collective-permute-start(bf16[8,32,1024]{2,1,0:T(8,128)(2,1)S(1)} %shard_map.81.rest_4_), channel_id=1, source_target_pairs={{0,4},{2,6},{4,0},{6,2},{8,12},{10,14},{12,8},{14,10},{1,5},{3,7},... | collective-permute-start | bytes 1572872 | tf_op jit(solution)/shard_map/ppermute | solution.py:473
  114.7 19.2 %collective-permute-start.23 = (bf16[8,32,1024]{2,1,0:T(8,128)(2,1)S(1)}, bf16[8,32,1024]{2,1,0:T(8,128)(2,1)S(1)}, u32[]{:S(2)}, u32[]{:S(2)}) collective-permute-start(bf16[8,32,1024]{2,1,0:T(8,128)(2,1)S(1)} %shard_map.85.rest_4_), channel_id=1, source_target_pairs={{0,4},{2,6},{4,0},{6,2},{8,12},{10,14},{12,8},{14,10},{1,5},{3,7},... | collective-permute-start | bytes 1572872 | tf_op jit(solution)/shard_map/ppermute | solution.py:473
  133.9 1.2 shard_map.86.rest_6_
  135.5 3.6 %shard_map.87.token_ref.rest_9_ = f32[16,256]{1,0:T(8,128)S(1)} custom-call(s32[2]{0:T(128)S(1)} %pad_add_fusion.me_ref, s32[64]{0:T(128)S(1)} %shard_map.65.codes_ref, bf16[8,32,5504]{2,1,0:T(8,128)(2,1)S(1)} %copy-done.3, bf16[8,32,1024]{2,1,0:T(8,128)(2,1)S(1)} %collective-permute-done.13.came_ref.rest_2_, ...), custom_call_target="tpu_custom_call" | custom-call | bytes 1024 | tf_op jit(solution)/shard_map/pallas_call | solution.py:434
  141.2 9.5 %collective-permute-start.29 = (bf16[8,32,1024]{2,1,0:T(8,128)(2,1)S(1)}, bf16[8,32,1024]{2,1,0:T(8,128)(2,1)S(1)}, u32[]{:S(2)}, u32[]{:S(2)}) collective-permute-start(bf16[8,32,1024]{2,1,0:T(8,128)(2,1)S(1)} %shard_map.89.rest_4_), channel_id=1, source_target_pairs={{0,4},{2,6},{4,0},{6,2},{8,12},{10,14},{12,8},{14,10},{1,5},{3,7},... | collective-permute-start | bytes 1572872 | tf_op jit(solution)/shard_map/ppermute | solution.py:473
  150.7 1.2 shard_map.90.rest_6_
  152.3 3.8 %shard_map.91.token_ref.rest_9_ = f32[16,256]{1,0:T(8,128)S(1)} custom-call(s32[2]{0:T(128)S(1)} %pad_add_fusion.me_ref, s32[64]{0:T(128)S(1)} %shard_map.65.codes_ref, bf16[8,32,5504]{2,1,0:T(8,128)(2,1)S(1)} %copy-done.3, bf16[8,32,1024]{2,1,0:T(8,128)(2,1)S(1)} %collective-permute-done.10.came_ref.rest_2_, ...), custom_call_target="tpu_custom_call" | custom-call | bytes 1024 | tf_op jit(solution)/shard_map/pallas_call | solution.py:434
  158.2 3.9 %collective-permute-done.29.rest_3_ = bf16[8,32,1024]{2,1,0:T(8,128)(2,1)S(1)} collective-permute-done((bf16[8,32,1024]{2,1,0:T(8,128)(2,1)S(1)}, bf16[8,32,1024]{2,1,0:T(8,128)(2,1)S(1)}, u32[]{:S(2)}, u32[]{:S(2)}) %collective-permute-start.29) | collective-permute-done | bytes 524320 | tf_op jit(solution)/shard_map/ppermute | solution.py:473
  162.1 1.2 shard_map.94.rest_6_
  163.7 1.8 collective-permute-start.33
  165.5 3.6 %shard_map.95.rest_3_.rest_9_ = f32[16,256]{1,0:T(8,128)S(1)} custom-call(s32[2]{0:T(128)S(1)} %pad_add_fusion.me_ref, s32[64]{0:T(128)S(1)} %shard_map.65.codes_ref, bf16[8,32,5504]{2,1,0:T(8,128)(2,1)S(1)} %copy-done.3, bf16[8,32,1024]{2,1,0:T(8,128)(2,1)S(1)} %collective-permute-done.11.rest_4_.came_ref, ...), custom_call_target="tpu_custom_call" | custom-call | bytes 1024 | tf_op jit(solution)/shard_map/pallas_call | solution.py:434
  169.8 3.4 %collective-permute-start.31 = (bf16[8,32,640]{2,1,0:T(8,128)(2,1)S(1)}, bf16[8,32,640]{2,1,0:T(8,128)(2,1)S(1)}, u32[]{:S(2)}, u32[]{:S(2)}) collective-permute-start(bf16[8,32,640]{2,1,0:T(8,128)(2,1)S(1)} %shard_map.96.rest_4_), channel_id=1, source_target_pairs={{0,4},{2,6},{4,0},{6,2},{8,12},{10,14},{12,8},{14,10},{1,5},{3,7},... | collective-permute-start | bytes 983048 | tf_op jit(solution)/shard_map/ppermute | solution.py:473
  173.3 1.0 shard_map.97.rest_6_
  174.3 3.1 %collective-permute-start.35 = (bf16[8,32,768]{2,1,0:T(8,128)(2,1)S(1)}, bf16[8,32,768]{2,1,0:T(8,128)(2,1)S(1)}, u32[]{:S(2)}, u32[]{:S(2)}) collective-permute-start(bf16[8,32,768]{2,1,0:T(8,128)(2,1)S(1)} %shard_map.97.rest_6_), channel_id=1, source_target_pairs={{0,2},{2,0},{4,6},{6,4},{8,10},{10,8},{12,14},{14,12},{1,3},{3,1},... | collective-permute-start | bytes 1179656 | tf_op jit(solution)/shard_map/ppermute | solution.py:473
  177.4 3.6 %shard_map.98.rest_4_.rest_9_ = f32[16,256]{1,0:T(8,128)S(1)} custom-call(s32[2]{0:T(128)S(1)} %pad_add_fusion.me_ref, s32[64]{0:T(128)S(1)} %shard_map.65.codes_ref, bf16[8,32,5504]{2,1,0:T(8,128)(2,1)S(1)} %copy-done.3, bf16[8,32,1024]{2,1,0:T(8,128)(2,1)S(1)} %collective-permute-done.16.rest_4_.came_ref, ...), custom_call_target="tpu_custom_call" | custom-call | bytes 1024 | tf_op jit(solution)/shard_map/pallas_call | solution.py:434
  181.1 0.9 shard_map.99.rest_6_
  182.8 3.9 %collective-permute-done.35.rest_4_ = bf16[8,32,768]{2,1,0:T(8,128)(2,1)S(1)} collective-permute-done((bf16[8,32,768]{2,1,0:T(8,128)(2,1)S(1)}, bf16[8,32,768]{2,1,0:T(8,128)(2,1)S(1)}, u32[]{:S(2)}, u32[]{:S(2)}) %collective-permute-start.35) | collective-permute-done | bytes 393248 | tf_op jit(solution)/shard_map/ppermute | solution.py:473
  186.7 2.9 %shard_map.100.rest_6_.rest_9_ = f32[16,256]{1,0:T(8,128)S(1)} custom-call(s32[2]{0:T(128)S(1)} %pad_add_fusion.me_ref, s32[64]{0:T(128)S(1)} %shard_map.65.codes_ref, bf16[8,32,5504]{2,1,0:T(8,128)(2,1)S(1)} %copy-done.3, bf16[8,32,1024]{2,1,0:T(8,128)(2,1)S(1)} %collective-permute-done.21.rest_3_.came_ref, ...), custom_call_target="tpu_custom_call" | custom-call | bytes 1024 | tf_op jit(solution)/shard_map/pallas_call | solution.py:434
  189.6 1.9 collective-permute-done.34.rest_4_
  191.5 2.8 %shard_map.101 = f32[16,2,128]{2,1,0:T(2,128)S(1)} custom-call(s32[2]{0:T(128)S(1)} %pad_add_fusion.me_ref, s32[64]{0:T(128)S(1)} %shard_map.65.codes_ref, bf16[8,32,5504]{2,1,0:T(8,128)(2,1)S(1)} %copy-done.3, bf16[8,32,1024]{2,1,0:T(8,128)(2,1)S(1)} %collective-permute-done.18.rest_3_.came_ref, bf16[12,32,640]{2,1,0:T(8,128)(2,1)S(1)} %collective-permute-done.27.rest_0_, ...), custom_call_target="tpu_custom_call" | custom-call | bytes 1024 | tf_op jit(solution)/shard_map/pallas_call | solution.py:434
  194.4 9.7 %all_to_all.14.came_ref = f32[16,2,128]{2,1,0:T(2,128)S(1)} all-to-all(f32[16,2,128]{2,1,0:T(2,128)S(1)} %shard_map.101), channel_id=1, replica_groups=mesh['groups'=2,'docs'=8,'tensor'=2] {'docs','tensor'}, dimensions={0} | all-to-all | bytes 32768 | tf_op jit(solution)/shard_map/all_to_all | solution.py:576
  204.1 1.5 shard_map.102
  (83 shorter events, 23.9 us)
Async XLA Ops:
  0.8 0.7 copy-start.1
  1.5 25.8 %copy-start.8 = (bf16[8,32,2048]{2,1,0:T(8,128)(2,1)S(1)}, bf16[8,32,2048]{2,1,0:T(8,128)(2,1)}, u32[]{:S(2)}) copy-start(bf16[8,32,2048]{2,1,0:T(8,128)(2,1)} %own_ref.22) | copy-start | bytes 3145732
  1.5 26.4 %copy-start.2 = (bf16[8,32,5504]{2,1,0:T(8,128)(2,1)S(1)}, bf16[8,32,5504]{2,1,0:T(8,128)(2,1)}, u32[]{:S(2)}) copy-start(bf16[8,32,5504]{2,1,0:T(8,128)(2,1)} %own_ref.31) | copy-start | bytes 8454148
  4.6 21.3 %collective-permute-start.6 = (bf16[4,32,2048]{2,1,0:T(8,128)(2,1)S(1)}, bf16[4,32,2048]{2,1,0:T(8,128)(2,1)S(1)}, u32[]{:S(2)}, u32[]{:S(2)}) collective-permute-start(bf16[4,32,2048]{2,1,0:T(8,128)(2,1)S(1)} %get-tuple-element.47), channel_id=1, source_target_pairs={{4,8},{6,10},{8,4},{10,6},{5,9},{7,11},{9,5},{11,7},{20,24},{22,26... | collective-permute-start | bytes 1572872 | tf_op jit(solution)/shard_map/ppermute | solution.py:473
  5.3 21.9 %collective-permute-start.7 = (bf16[8,32,1024]{2,1,0:T(8,128)(2,1)S(1)}, bf16[8,32,1024]{2,1,0:T(8,128)(2,1)S(1)}, u32[]{:S(2)}, u32[]{:S(2)}) collective-permute-start(bf16[8,32,1024]{2,1,0:T(8,128)(2,1)S(1)} %get-tuple-element.48), channel_id=1, source_target_pairs={{0,4},{2,6},{4,0},{6,2},{8,12},{10,14},{12,8},{14,10},{1,5},{3,7},... | collective-permute-start | bytes 1572872 | tf_op jit(solution)/shard_map/ppermute | solution.py:473
  29.5 15.1 %collective-permute-start.9 = (bf16[8,32,1024]{2,1,0:T(8,128)(2,1)}, bf16[8,32,1024]{2,1,0:T(8,128)(2,1)S(1)}, u32[]{:S(2)}, u32[]{:S(2)}) collective-permute-start(bf16[8,32,1024]{2,1,0:T(8,128)(2,1)} %shard_map.68.token_ref), channel_id=1, source_target_pairs={{0,4},{2,6},{4,0},{6,2},{8,12},{10,14},{12,8},{14,10},{1,5},{3,7},... | collective-permute-start | bytes 1572872 | tf_op jit(solution)/shard_map/ppermute | solution.py:473
  30.9 15.2 %collective-permute-start.8 = (bf16[8,32,1024]{2,1,0:T(8,128)(2,1)S(1)}, bf16[8,32,1024]{2,1,0:T(8,128)(2,1)S(1)}, u32[]{:S(2)}, u32[]{:S(2)}) collective-permute-start(bf16[8,32,1024]{2,1,0:T(8,128)(2,1)S(1)} %shard_map.67.token_ref), channel_id=1, source_target_pairs={{4,8},{6,10},{8,4},{10,6},{5,9},{7,11},{9,5},{11,7},{20,24},{22,26... | collective-permute-start | bytes 1572872 | tf_op jit(solution)/shard_map/ppermute | solution.py:473
  33.2 22.6 %collective-permute-start.13 = (bf16[8,32,1024]{2,1,0:T(8,128)(2,1)}, bf16[8,32,1024]{2,1,0:T(8,128)(2,1)S(1)}, u32[]{:S(2)}, u32[]{:S(2)}) collective-permute-start(bf16[8,32,1024]{2,1,0:T(8,128)(2,1)} %shard_map.72), channel_id=1, source_target_pairs={{0,4},{2,6},{4,0},{6,2},{8,12},{10,14},{12,8},{14,10},{1,5},{3,7},... | collective-permute-start | bytes 1572872 | tf_op jit(solution)/shard_map/ppermute | solution.py:473
  40.7 5.5 %copy-start.11 = (bf16[4,32,2048]{2,1,0:T(8,128)(2,1)S(1)}, bf16[4,32,2048]{2,1,0:T(8,128)(2,1)}, u32[]{:S(2)}) copy-start(bf16[4,32,2048]{2,1,0:T(8,128)(2,1)} %get-tuple-element.50.token_ref.rest_2_) | copy-start | bytes 1572868
  45.3 2.6 %copy-start.3 = (bf16[8,32,5504]{2,1,0:T(8,128)(2,1)S(1)}, bf16[8,32,5504]{2,1,0:T(8,128)(2,1)}, u32[]{:S(2)}) copy-start(bf16[8,32,5504]{2,1,0:T(8,128)(2,1)} %own_ref.31) | copy-start | bytes 8454148
  45.3 12.1 %collective-permute-start.12 = (bf16[8,32,1024]{2,1,0:T(8,128)(2,1)S(1)}, bf16[8,32,1024]{2,1,0:T(8,128)(2,1)S(1)}, u32[]{:S(2)}, u32[]{:S(2)}) collective-permute-start(bf16[8,32,1024]{2,1,0:T(8,128)(2,1)S(1)} %shard_map.69.rest_4_), channel_id=1, source_target_pairs={{4,8},{6,10},{8,4},{10,6},{5,9},{7,11},{9,5},{11,7},{20,24},{22,26... | collective-permute-start | bytes 1572872 | tf_op jit(solution)/shard_map/ppermute | solution.py:473
  48.7 18.4 %collective-permute-start.11 = (bf16[8,32,1024]{2,1,0:T(8,128)(2,1)S(1)}, bf16[8,32,1024]{2,1,0:T(8,128)(2,1)S(1)}, u32[]{:S(2)}, u32[]{:S(2)}) collective-permute-start(bf16[8,32,1024]{2,1,0:T(8,128)(2,1)S(1)} %shard_map.70.token_ref), channel_id=1, source_target_pairs={{0,4},{2,6},{4,0},{6,2},{8,12},{10,14},{12,8},{14,10},{1,5},{3,7},... | collective-permute-start | bytes 1572872 | tf_op jit(solution)/shard_map/ppermute | solution.py:473
  53.9 24.4 %collective-permute-start.10 = (bf16[8,32,1024]{2,1,0:T(8,128)(2,1)S(1)}, bf16[8,32,1024]{2,1,0:T(8,128)(2,1)S(1)}, u32[]{:S(2)}, u32[]{:S(2)}) collective-permute-start(bf16[8,32,1024]{2,1,0:T(8,128)(2,1)S(1)} %shard_map.71.token_ref), channel_id=1, source_target_pairs={{0,4},{2,6},{4,0},{6,2},{8,12},{10,14},{12,8},{14,10},{1,5},{3,7},... | collective-permute-start | bytes 1572872 | tf_op jit(solution)/shard_map/ppermute | solution.py:473
  56.5 10.6 %copy-start.9 = (bf16[8,32,2048]{2,1,0:T(8,128)(2,1)S(1)}, bf16[8,32,2048]{2,1,0:T(8,128)(2,1)}, u32[]{:S(2)}) copy-start(bf16[8,32,2048]{2,1,0:T(8,128)(2,1)} %own_ref.22) | copy-start | bytes 3145732
  56.6 23.8 %collective-permute-start.17 = (bf16[12,32,1024]{2,1,0:T(8,128)(2,1)S(1)}, bf16[12,32,1024]{2,1,0:T(8,128)(2,1)S(1)}, u32[]{:S(2)}, u32[]{:S(2)}) collective-permute-start(bf16[12,32,1024]{2,1,0:T(8,128)(2,1)S(1)} %shard_map.73.rest_4_), channel_id=1, source_target_pairs={{4,8},{6,10},{8,4},{10,6},{5,9},{7,11},{9,5},{11,7},{20,24},{22,26... | collective-permute-start | bytes 2359304 | tf_op jit(solution)/shard_map/ppermute | solution.py:473
  58.2 31.3 %collective-permute-start.16 = (bf16[8,32,1024]{2,1,0:T(8,128)(2,1)S(1)}, bf16[8,32,1024]{2,1,0:T(8,128)(2,1)S(1)}, u32[]{:S(2)}, u32[]{:S(2)}) collective-permute-start(bf16[8,32,1024]{2,1,0:T(8,128)(2,1)S(1)} %shard_map.74.rest_5_), channel_id=1, source_target_pairs={{0,4},{2,6},{4,0},{6,2},{8,12},{10,14},{12,8},{14,10},{1,5},{3,7},... | collective-permute-start | bytes 1572872 | tf_op jit(solution)/shard_map/ppermute | solution.py:473
  68.3 12.1 %copy-start.7 = (bf16[4,32,5504]{2,1,0:T(8,128)(2,1)S(1)}, bf16[4,32,5504]{2,1,0:T(8,128)(2,1)}, u32[]{:S(2)}) copy-start(bf16[4,32,5504]{2,1,0:T(8,128)(2,1)} %get-tuple-element.51.rest_1_) | copy-start | bytes 4227076
  79.0 16.8 %collective-permute-start.14 = (bf16[12,32,1024]{2,1,0:T(8,128)(2,1)S(1)}, bf16[12,32,1024]{2,1,0:T(8,128)(2,1)S(1)}, u32[]{:S(2)}, u32[]{:S(2)}) collective-permute-start(bf16[12,32,1024]{2,1,0:T(8,128)(2,1)S(1)} %shard_map.76.rest_3_), channel_id=1, source_target_pairs={{4,8},{6,10},{8,4},{10,6},{5,9},{7,11},{9,5},{11,7},{20,24},{22,26... | collective-permute-start | bytes 2359304 | tf_op jit(solution)/shard_map/ppermute | solution.py:473
  79.7 11.7 %collective-permute-start.15 = (bf16[8,32,1024]{2,1,0:T(8,128)(2,1)S(1)}, bf16[8,32,1024]{2,1,0:T(8,128)(2,1)S(1)}, u32[]{:S(2)}, u32[]{:S(2)}) collective-permute-start(bf16[8,32,1024]{2,1,0:T(8,128)(2,1)S(1)} %shard_map.75.token_ref), channel_id=1, source_target_pairs={{0,2},{2,0},{4,6},{6,4},{8,10},{10,8},{12,14},{14,12},{1,3},{3,1},... | collective-permute-start | bytes 1572872 | tf_op jit(solution)/shard_map/ppermute | solution.py:473
  81.2 10.3 %copy-start = (bf16[1,768,2048]{2,1,0:T(8,128)(2,1)S(1)}, bf16[1,768,2048]{2,1,0:T(8,128)(2,1)}, u32[]{:S(2)}) copy-start(bf16[1,768,2048]{2,1,0:T(8,128)(2,1)} %rest_6_.3) | copy-start | bytes 9437188
  81.2 16.9 %collective-permute-start.21 = (bf16[8,32,1024]{2,1,0:T(8,128)(2,1)S(1)}, bf16[8,32,1024]{2,1,0:T(8,128)(2,1)S(1)}, u32[]{:S(2)}, u32[]{:S(2)}) collective-permute-start(bf16[8,32,1024]{2,1,0:T(8,128)(2,1)S(1)} %shard_map.77.rest_5_), channel_id=1, source_target_pairs={{0,4},{2,6},{4,0},{6,2},{8,12},{10,14},{12,8},{14,10},{1,5},{3,7},... | collective-permute-start | bytes 1572872 | tf_op jit(solution)/shard_map/ppermute | solution.py:473
  90.8 9.4 %collective-permute-start.20 = (bf16[8,32,1024]{2,1,0:T(8,128)(2,1)S(1)}, bf16[8,32,1024]{2,1,0:T(8,128)(2,1)S(1)}, u32[]{:S(2)}, u32[]{:S(2)}) collective-permute-start(bf16[8,32,1024]{2,1,0:T(8,128)(2,1)S(1)} %shard_map.78.rest_7_), channel_id=1, source_target_pairs={{0,2},{2,0},{4,6},{6,4},{8,10},{10,8},{12,14},{14,12},{1,3},{3,1},... | collective-permute-start | bytes 1572872 | tf_op jit(solution)/shard_map/ppermute | solution.py:473
  100.2 35.3 %slice-start = ((s8[8454144]{0:T(1024)(128)(4,1)}), s8[4194304]{0:T(1024)(128)(4,1)S(1)}, s32[]{:S(2)}) async-start(s8[8454144]{0:T(1024)(128)(4,1)} %bitcast.4), calls=%async_computation.2 | async-start | bytes 8388608
  100.2 35.3 %slice-start.1 = ((s8[8454144]{0:T(1024)(128)(4,1)}), s8[4194304]{0:T(1024)(128)(4,1)S(1)}, s32[]{:S(2)}) async-start(s8[8454144]{0:T(1024)(128)(4,1)} %bitcast.4), calls=%async_computation.3 | async-start | bytes 8388608
  103.9 31.5 %collective-permute-start.26 = (f32[512,768]{1,0:T(8,128)S(1)}, f32[512,768]{1,0:T(8,128)S(1)}, u32[]{:S(2)}, u32[]{:S(2)}) collective-permute-start(f32[512,768]{1,0:T(8,128)S(1)} %shard_map.83.token_ref.rest_7_), channel_id=1, source_target_pairs={{0,1},{1,0},{2,3},{3,2},{4,5},{5,4},{6,7},{7,6},{8,9},{9,8},{10,11... | collective-permute-start | bytes 4718600 | tf_op jit(solution)/shard_map/ppermute | solution.py:548
  104.0 10.1 %collective-permute-start.19 = (bf16[12,32,1024]{2,1,0:T(8,128)(2,1)S(1)}, bf16[12,32,1024]{2,1,0:T(8,128)(2,1)S(1)}, u32[]{:S(2)}, u32[]{:S(2)}) collective-permute-start(bf16[12,32,1024]{2,1,0:T(8,128)(2,1)S(1)} %shard_map.80.rest_3_), channel_id=1, source_target_pairs={{4,8},{6,10},{8,4},{10,6},{5,9},{7,11},{9,5},{11,7},{20,24},{22,26... | collective-permute-start | bytes 2359304 | tf_op jit(solution)/shard_map/ppermute | solution.py:473
  104.7 29.1 %collective-permute-start.18 = (bf16[8,32,1024]{2,1,0:T(8,128)(2,1)S(1)}, bf16[8,32,1024]{2,1,0:T(8,128)(2,1)S(1)}, u32[]{:S(2)}, u32[]{:S(2)}) collective-permute-start(bf16[8,32,1024]{2,1,0:T(8,128)(2,1)S(1)} %shard_map.81.rest_4_), channel_id=1, source_target_pairs={{0,4},{2,6},{4,0},{6,2},{8,12},{10,14},{12,8},{14,10},{1,5},{3,7},... | collective-permute-start | bytes 1572872 | tf_op jit(solution)/shard_map/ppermute | solution.py:473
  112.8 22.7 %slice-start.2 = ((s8[8454144]{0:T(1024)(128)(4,1)}), s8[65536]{0:T(1024)(128)(4,1)S(1)}, s32[]{:S(2)}) async-start(s8[8454144]{0:T(1024)(128)(4,1)} %bitcast.4), calls=%async_computation.4 | async-start | bytes 131072
  112.8 27.7 %collective-permute-start.24 = (bf16[12,32,1024]{2,1,0:T(8,128)(2,1)S(1)}, bf16[12,32,1024]{2,1,0:T(8,128)(2,1)S(1)}, u32[]{:S(2)}, u32[]{:S(2)}) collective-permute-start(bf16[12,32,1024]{2,1,0:T(8,128)(2,1)S(1)} %shard_map.84.rest_3_), channel_id=1, source_target_pairs={{4,8},{6,10},{8,4},{10,6},{5,9},{7,11},{9,5},{11,7},{20,24},{22,26... | collective-permute-start | bytes 2359304 | tf_op jit(solution)/shard_map/ppermute | solution.py:473
  113.7 21.8 %collective-permute-start.25 = (bf16[8,32,1024]{2,1,0:T(8,128)(2,1)S(1)}, bf16[8,32,1024]{2,1,0:T(8,128)(2,1)S(1)}, u32[]{:S(2)}, u32[]{:S(2)}) collective-permute-start(bf16[8,32,1024]{2,1,0:T(8,128)(2,1)S(1)} %shard_map.82.rest_7_), channel_id=1, source_target_pairs={{0,2},{2,0},{4,6},{6,4},{8,10},{10,8},{12,14},{14,12},{1,3},{3,1},... | collective-permute-start | bytes 1572872 | tf_op jit(solution)/shard_map/ppermute | solution.py:473
  114.7 36.0 %collective-permute-start.23 = (bf16[8,32,1024]{2,1,0:T(8,128)(2,1)S(1)}, bf16[8,32,1024]{2,1,0:T(8,128)(2,1)S(1)}, u32[]{:S(2)}, u32[]{:S(2)}) collective-permute-start(bf16[8,32,1024]{2,1,0:T(8,128)(2,1)S(1)} %shard_map.85.rest_4_), channel_id=1, source_target_pairs={{0,4},{2,6},{4,0},{6,2},{8,12},{10,14},{12,8},{14,10},{1,5},{3,7},... | collective-permute-start | bytes 1572872 | tf_op jit(solution)/shard_map/ppermute | solution.py:473
  135.1 17.2 %collective-permute-start.22 = (bf16[8,32,1024]{2,1,0:T(8,128)(2,1)S(1)}, bf16[8,32,1024]{2,1,0:T(8,128)(2,1)S(1)}, u32[]{:S(2)}, u32[]{:S(2)}) collective-permute-start(bf16[8,32,1024]{2,1,0:T(8,128)(2,1)S(1)} %shard_map.86.rest_6_), channel_id=1, source_target_pairs={{0,2},{2,0},{4,6},{6,4},{8,10},{10,8},{12,14},{14,12},{1,3},{3,1},... | collective-permute-start | bytes 1572872 | tf_op jit(solution)/shard_map/ppermute | solution.py:473
  139.8 17.7 %collective-permute-start.30 = (bf16[12,32,768]{2,1,0:T(8,128)(2,1)S(1)}, bf16[12,32,768]{2,1,0:T(8,128)(2,1)S(1)}, u32[]{:S(2)}, u32[]{:S(2)}) collective-permute-start(bf16[12,32,768]{2,1,0:T(8,128)(2,1)S(1)} %shard_map.88.rest_3_), channel_id=1, source_target_pairs={{4,8},{6,10},{8,4},{10,6},{5,9},{7,11},{9,5},{11,7},{20,24},{22,26... | collective-permute-start | bytes 1769480 | tf_op jit(solution)/shard_map/ppermute | solution.py:473
  141.2 20.9 %collective-permute-start.29 = (bf16[8,32,1024]{2,1,0:T(8,128)(2,1)S(1)}, bf16[8,32,1024]{2,1,0:T(8,128)(2,1)S(1)}, u32[]{:S(2)}, u32[]{:S(2)}) collective-permute-start(bf16[8,32,1024]{2,1,0:T(8,128)(2,1)S(1)} %shard_map.89.rest_4_), channel_id=1, source_target_pairs={{0,4},{2,6},{4,0},{6,2},{8,12},{10,14},{12,8},{14,10},{1,5},{3,7},... | collective-permute-start | bytes 1572872 | tf_op jit(solution)/shard_map/ppermute | solution.py:473
  151.9 13.6 %collective-permute-start.28 = (bf16[8,32,1024]{2,1,0:T(8,128)(2,1)S(1)}, bf16[8,32,1024]{2,1,0:T(8,128)(2,1)S(1)}, u32[]{:S(2)}, u32[]{:S(2)}) collective-permute-start(bf16[8,32,1024]{2,1,0:T(8,128)(2,1)S(1)} %shard_map.90.rest_6_), channel_id=1, source_target_pairs={{0,2},{2,0},{4,6},{6,4},{8,10},{10,8},{12,14},{14,12},{1,3},{3,1},... | collective-permute-start | bytes 1572872 | tf_op jit(solution)/shard_map/ppermute | solution.py:473
  156.8 12.3 %collective-permute-start.27 = (bf16[12,32,640]{2,1,0:T(8,128)(2,1)S(1)}, bf16[12,32,640]{2,1,0:T(8,128)(2,1)S(1)}, u32[]{:S(2)}, u32[]{:S(2)}) collective-permute-start(bf16[12,32,640]{2,1,0:T(8,128)(2,1)S(1)} %shard_map.92.rest_3_), channel_id=1, source_target_pairs={{4,8},{6,10},{8,4},{10,6},{5,9},{7,11},{9,5},{11,7},{20,24},{22,26... | collective-permute-start | bytes 1474568 | tf_op jit(solution)/shard_map/ppermute | solution.py:473
  163.3 14.1 %collective-permute-start.32 = (bf16[8,32,1024]{2,1,0:T(8,128)(2,1)S(1)}, bf16[8,32,1024]{2,1,0:T(8,128)(2,1)S(1)}, u32[]{:S(2)}, u32[]{:S(2)}) collective-permute-start(bf16[8,32,1024]{2,1,0:T(8,128)(2,1)S(1)} %shard_map.94.rest_6_), channel_id=1, source_target_pairs={{0,2},{2,0},{4,6},{6,4},{8,10},{10,8},{12,14},{14,12},{1,3},{3,1},... | collective-permute-start | bytes 1572872 | tf_op jit(solution)/shard_map/ppermute | solution.py:473
  163.7 9.6 %collective-permute-start.33 = (bf16[8,32,768]{2,1,0:T(8,128)(2,1)S(1)}, bf16[8,32,768]{2,1,0:T(8,128)(2,1)S(1)}, u32[]{:S(2)}, u32[]{:S(2)}) collective-permute-start(bf16[8,32,768]{2,1,0:T(8,128)(2,1)S(1)} %shard_map.93.rest_4_), channel_id=1, source_target_pairs={{0,4},{2,6},{4,0},{6,2},{8,12},{10,14},{12,8},{14,10},{1,5},{3,7},... | collective-permute-start | bytes 1179656 | tf_op jit(solution)/shard_map/ppermute | solution.py:473
  169.8 11.3 %collective-permute-start.31 = (bf16[8,32,640]{2,1,0:T(8,128)(2,1)S(1)}, bf16[8,32,640]{2,1,0:T(8,128)(2,1)S(1)}, u32[]{:S(2)}, u32[]{:S(2)}) collective-permute-start(bf16[8,32,640]{2,1,0:T(8,128)(2,1)S(1)} %shard_map.96.rest_4_), channel_id=1, source_target_pairs={{0,4},{2,6},{4,0},{6,2},{8,12},{10,14},{12,8},{14,10},{1,5},{3,7},... | collective-permute-start | bytes 983048 | tf_op jit(solution)/shard_map/ppermute | solution.py:473
  174.3 12.4 %collective-permute-start.35 = (bf16[8,32,768]{2,1,0:T(8,128)(2,1)S(1)}, bf16[8,32,768]{2,1,0:T(8,128)(2,1)S(1)}, u32[]{:S(2)}, u32[]{:S(2)}) collective-permute-start(bf16[8,32,768]{2,1,0:T(8,128)(2,1)S(1)} %shard_map.97.rest_6_), channel_id=1, source_target_pairs={{0,2},{2,0},{4,6},{6,4},{8,10},{10,8},{12,14},{14,12},{1,3},{3,1},... | collective-permute-start | bytes 1179656 | tf_op jit(solution)/shard_map/ppermute | solution.py:473
  182.0 9.5 %collective-permute-start.34 = (bf16[8,32,640]{2,1,0:T(8,128)(2,1)S(1)}, bf16[8,32,640]{2,1,0:T(8,128)(2,1)S(1)}, u32[]{:S(2)}, u32[]{:S(2)}) collective-permute-start(bf16[8,32,640]{2,1,0:T(8,128)(2,1)S(1)} %shard_map.99.rest_6_), channel_id=1, source_target_pairs={{0,2},{2,0},{4,6},{6,4},{8,10},{10,8},{12,14},{14,12},{1,3},{3,1},... | collective-permute-start | bytes 983048 | tf_op jit(solution)/shard_map/ppermute | solution.py:473

commit v5 on v4

--- a/solution.py
+++ b/solution.py
@@ -567,11 +567,13 @@
             token = mix(i + 1, token)
         if i < total:
             token = forward(i, token)
+        if i == 4:
+            token = gram(1, token)
         if i == 0:
             token = ahead_block(3, token)
         if 1 <= i < total + 1:
             token = side(i - 1, token)
-        if i >= 2:
+        if i >= 2 and i != 3:
             token = gram(i - 2, token)
     back = lax.all_to_all(state["score"], ("docs", "tensor"), 0, 0, tiled=True)
     return pl.pallas_call(

time: 206 us -> 202 us (0.981)
  starting transfers between devices: 82 us -> 60.1 us
  waiting for transfers between devices: 34.5 us -> 51.7 us
    ppermute x29, starting transfers between devices: 81.9 us -> 60.1 us  [chain(): send = lambda x, pairs: lax.ppermute(x, 'docs', pairs)]
    ppermute x29, waiting for transfers between devices: 34.5 us -> 51.7 us  [chain(): send = lambda x, pairs: lax.ppermute(x, 'docs', pairs)]
  transfers between devices with their start and end apart: 30 -> 30, of which waited for: 11 -> 12; matrix products, arithmetic and copies ran while one was open for 0% -> 0% of each run, Pallas kernels for 23% -> 24%
where the time goes in v5:
time: 202 us
  Pallas kernels  61.3 us (30%)
  starting transfers between devices  60.1 us (30%)
  waiting for transfers between devices  51.7 us (26%)
  blocking collectives  24.9 us (12%)
  local copies, waits for them, and re-layouts  2.03 us (1%)
    ppermute x29, starting transfers between devices, chain(): send = lambda x, pairs: lax.ppermute(x, 'docs', pairs)  60.1 us
    ppermute x29, waiting for transfers between devices, chain(): send = lambda x, pairs: lax.ppermute(x, 'docs', pairs)  51.7 us
    pallas_call x8, Pallas kernels, gram_call(): pl.pallas_call(functools.partial(gram_kernel, offs=offs, off=off, at=at,...  27.9 us
    all_to_all x1, blocking collectives, chain(): lax.all_to_all(jnp.broadcast_to(tab[None, :], (groups * 8, 8 * CAP)), ('g...  14.7 us
    all_to_all x1, blocking collectives, chain(): back = lax.all_to_all(state['score'], ('docs', 'tensor'), 0, 0, tiled=True)  10.3 us
    pallas_call x8, Pallas kernels, side_call(): pl.pallas_call(functools.partial(side_kernel, offs=offs, off=off, at=at,...  9.13 us
    pallas_call x8, Pallas kernels, forward_call(): pl.pallas_call(functools.partial(forward_kernel, offs=offs, ahead=ahead),...  6.5 us
    pallas_call x8, Pallas kernels, mix_call(): pl.pallas_call(functools.partial(mix_kernel, first=first, off=off, at=at)...  5.22 us
  transfers between devices with their start and end apart: 30, of which 12 were waited for; matrix products, arithmetic and copies ran while one was open for 0% of the time, Pallas kernels for 24%

profile of v5, /device:TPU:0, one launch (start us, length us, event | category | flops | bytes accessed | tf_op | source)
XLA Modules:
  0.0 201.7 jit_solution(13640567937638680898)
XLA Ops:
  1.5 3.1 %shard_map.64 = (s32[16]{0:T(128)S(1)}, s32[16]{0:T(128)S(1)}, s32[16]{0:T(128)S(1)}, bf16[8,32,1024]{2,1,0:T(8,128)(2,1)S(1)}, bf16[4,32,2048]{2,1,0:T(8,128)(2,1)S(1)}) custom-call(s32[2]{0:T(128)S(1)} %pad_add_fusion.me_ref, s32[16,1]{1,0:T(8,128)S(1)} %copy.8.doc_ref, s32[16]{0:T(128)S(1)} %copy-done.1, bf16[8,32,2048]{2,1,0:T(8,128)(2,1)} %own_ref.23, ...), custom_call_target="tpu_custom_call" | custom-call | bytes 1024 | tf_op jit(solution)/shard_map/pallas_call | solution.py:141
  5.3 5.9 %collective-permute-start.7 = (bf16[8,32,1024]{2,1,0:T(8,128)(2,1)S(1)}, bf16[8,32,1024]{2,1,0:T(8,128)(2,1)S(1)}, u32[]{:S(2)}, u32[]{:S(2)}) collective-permute-start(bf16[8,32,1024]{2,1,0:T(8,128)(2,1)S(1)} %get-tuple-element.48), channel_id=1, source_target_pairs={{0,4},{2,6},{4,0},{6,2},{8,12},{10,14},{12,8},{14,10},{1,5},{3,7},... | collective-permute-start | bytes 1572872 | tf_op jit(solution)/shard_map/ppermute | solution.py:473
  11.2 14.7 %all_to_all.13 = s32[16,1,16]{2,1,0:T(1,128)S(1)} all-to-all(s32[16,1,16]{2,1,0:T(1,128)S(1)} %broadcast_in_dim.4), channel_id=1, replica_groups=mesh['groups'=2,'docs'=8,'tensor'=2] {'groups','docs'}, dimensions={0} | all-to-all | bytes 2048 | tf_op jit(solution)/shard_map/all_to_all | solution.py:477
  25.9 1.4 shard_map.66.codes_ref.token_ref
  27.9 1.6 shard_map.68.token_ref
  29.5 1.4 collective-permute-start.9
  31.6 1.6 shard_map.72
  33.2 3.6 %collective-permute-start.13 = (bf16[8,32,1024]{2,1,0:T(8,128)(2,1)}, bf16[8,32,1024]{2,1,0:T(8,128)(2,1)S(1)}, u32[]{:S(2)}, u32[]{:S(2)}) collective-permute-start(bf16[8,32,1024]{2,1,0:T(8,128)(2,1)} %shard_map.72), channel_id=1, source_target_pairs={{0,4},{2,6},{4,0},{6,2},{8,12},{10,14},{12,8},{14,10},{1,5},{3,7},... | collective-permute-start | bytes 1572872 | tf_op jit(solution)/shard_map/ppermute | solution.py:473
  36.8 2.0 %shard_map.65.codes_ref = s32[64]{0:T(128)S(1)} custom-call(s32[2]{0:T(128)S(1)} %pad_add_fusion.me_ref, s32[16,16]{1,0:T(8,128)S(1)} %bitcast.7), custom_call_target="tpu_custom_call" | custom-call | bytes 1024 | tf_op jit(solution)/shard_map/pallas_call | solution.py:683
  40.7 4.0 %collective-permute-done.9.came_ref.rest_2_ = bf16[8,32,1024]{2,1,0:T(8,128)(2,1)S(1)} collective-permute-done((bf16[8,32,1024]{2,1,0:T(8,128)(2,1)}, bf16[8,32,1024]{2,1,0:T(8,128)(2,1)S(1)}, u32[]{:S(2)}, u32[]{:S(2)}) %collective-permute-start.9) | collective-permute-done | bytes 524320 | tf_op jit(solution)/shard_map/ppermute | solution.py:473
  46.1 1.7 shard_map.70.token_ref
  47.8 5.1 %collective-permute-start.11 = (bf16[8,32,1024]{2,1,0:T(8,128)(2,1)S(1)}, bf16[8,32,1024]{2,1,0:T(8,128)(2,1)S(1)}, u32[]{:S(2)}, u32[]{:S(2)}) collective-permute-start(bf16[8,32,1024]{2,1,0:T(8,128)(2,1)S(1)} %shard_map.70.token_ref), channel_id=1, source_target_pairs={{0,4},{2,6},{4,0},{6,2},{8,12},{10,14},{12,8},{14,10},{1,5},{3,7},... | collective-permute-start | bytes 1572872 | tf_op jit(solution)/shard_map/ppermute | solution.py:473
  53.8 2.1 %collective-permute-done.13.came_ref.rest_2_ = bf16[8,32,1024]{2,1,0:T(8,128)(2,1)S(1)} collective-permute-done((bf16[8,32,1024]{2,1,0:T(8,128)(2,1)}, bf16[8,32,1024]{2,1,0:T(8,128)(2,1)S(1)}, u32[]{:S(2)}, u32[]{:S(2)}) %collective-permute-start.13) | collective-permute-done | bytes 524320 | tf_op jit(solution)/shard_map/ppermute | solution.py:473
  57.4 4.7 %collective-permute-start.10 = (bf16[8,32,1024]{2,1,0:T(8,128)(2,1)S(1)}, bf16[8,32,1024]{2,1,0:T(8,128)(2,1)S(1)}, u32[]{:S(2)}, u32[]{:S(2)}) collective-permute-start(bf16[8,32,1024]{2,1,0:T(8,128)(2,1)S(1)} %shard_map.71.token_ref), channel_id=1, source_target_pairs={{0,4},{2,6},{4,0},{6,2},{8,12},{10,14},{12,8},{14,10},{1,5},{3,7},... | collective-permute-start | bytes 1572872 | tf_op jit(solution)/shard_map/ppermute | solution.py:473
  63.5 3.7 %collective-permute-done.11.rest_4_.came_ref = bf16[8,32,1024]{2,1,0:T(8,128)(2,1)S(1)} collective-permute-done((bf16[8,32,1024]{2,1,0:T(8,128)(2,1)S(1)}, bf16[8,32,1024]{2,1,0:T(8,128)(2,1)S(1)}, u32[]{:S(2)}, u32[]{:S(2)}) %collective-permute-start.11) | collective-permute-done | bytes 524320 | tf_op jit(solution)/shard_map/ppermute | solution.py:473
  67.1 1.2 shard_map.75.token_ref
  69.0 9.3 %collective-permute-done.10.came_ref.rest_2_ = bf16[8,32,1024]{2,1,0:T(8,128)(2,1)S(1)} collective-permute-done((bf16[8,32,1024]{2,1,0:T(8,128)(2,1)S(1)}, bf16[8,32,1024]{2,1,0:T(8,128)(2,1)S(1)}, u32[]{:S(2)}, u32[]{:S(2)}) %collective-permute-start.10) | collective-permute-done | bytes 524320 | tf_op jit(solution)/shard_map/ppermute | solution.py:473
  80.5 6.3 %collective-permute-done.16.rest_4_.came_ref = bf16[8,32,1024]{2,1,0:T(8,128)(2,1)S(1)} collective-permute-done((bf16[8,32,1024]{2,1,0:T(8,128)(2,1)S(1)}, bf16[8,32,1024]{2,1,0:T(8,128)(2,1)S(1)}, u32[]{:S(2)}, u32[]{:S(2)}) %collective-permute-start.16) | collective-permute-done | bytes 524320 | tf_op jit(solution)/shard_map/ppermute | solution.py:473
  86.9 1.2 shard_map.78.rest_7_
  88.1 3.7 %shard_map.79.token_ref.rest_8_ = f32[512,768]{1,0:T(8,128)S(1)} custom-call(s32[2]{0:T(128)S(1)} %pad_add_fusion.me_ref, s32[64]{0:T(128)S(1)} %shard_map.65.codes_ref, bf16[8,32,2048]{2,1,0:T(8,128)(2,1)S(1)} %copy-done.9, bf16[8,32,1024]{2,1,0:T(8,128)(2,1)S(1)} %collective-permute-done.7.came_ref.rest_3_, ...), custom_call_target="tpu_custom_call" | custom-call | bytes 1024 | tf_op jit(solution)/shard_map/pallas_call | solution.py:434
  93.2 4.7 %collective-permute-start.21 = (bf16[8,32,1024]{2,1,0:T(8,128)(2,1)S(1)}, bf16[8,32,1024]{2,1,0:T(8,128)(2,1)S(1)}, u32[]{:S(2)}, u32[]{:S(2)}) collective-permute-start(bf16[8,32,1024]{2,1,0:T(8,128)(2,1)S(1)} %shard_map.77.rest_5_), channel_id=1, source_target_pairs={{0,4},{2,6},{4,0},{6,2},{8,12},{10,14},{12,8},{14,10},{1,5},{3,7},... | collective-permute-start | bytes 1572872 | tf_op jit(solution)/shard_map/ppermute | solution.py:473
  99.1 8.0 %collective-permute-done.21.rest_3_.came_ref = bf16[8,32,1024]{2,1,0:T(8,128)(2,1)S(1)} collective-permute-done((bf16[8,32,1024]{2,1,0:T(8,128)(2,1)S(1)}, bf16[8,32,1024]{2,1,0:T(8,128)(2,1)S(1)}, u32[]{:S(2)}, u32[]{:S(2)}) %collective-permute-start.21) | collective-permute-done | bytes 524320 | tf_op jit(solution)/shard_map/ppermute | solution.py:473
  107.1 1.2 shard_map.82.token_ref
  109.7 3.7 %shard_map.85.rest_4_.rest_7_ = f32[512,768]{1,0:T(8,128)S(1)} custom-call(s32[2]{0:T(128)S(1)} %pad_add_fusion.me_ref, s32[64]{0:T(128)S(1)} %shard_map.65.codes_ref, bf16[8,32,2048]{2,1,0:T(8,128)(2,1)S(1)} %copy-done.9, bf16[8,32,1024]{2,1,0:T(8,128)(2,1)S(1)} %collective-permute-done.9.came_ref.rest_2_, ...), custom_call_target="tpu_custom_call" | custom-call | bytes 1024 | tf_op jit(solution)/shard_map/pallas_call | solution.py:434
  113.5 5.7 %collective-permute-start.18 = (bf16[8,32,1024]{2,1,0:T(8,128)(2,1)S(1)}, bf16[8,32,1024]{2,1,0:T(8,128)(2,1)S(1)}, u32[]{:S(2)}, u32[]{:S(2)}) collective-permute-start(bf16[8,32,1024]{2,1,0:T(8,128)(2,1)S(1)} %shard_map.81.rest_4_), channel_id=1, source_target_pairs={{0,4},{2,6},{4,0},{6,2},{8,12},{10,14},{12,8},{14,10},{1,5},{3,7},... | collective-permute-start | bytes 1572872 | tf_op jit(solution)/shard_map/ppermute | solution.py:473
  120.4 2.7 %collective-permute-start.23 = (bf16[8,32,1024]{2,1,0:T(8,128)(2,1)S(1)}, bf16[8,32,1024]{2,1,0:T(8,128)(2,1)S(1)}, u32[]{:S(2)}, u32[]{:S(2)}) collective-permute-start(bf16[8,32,1024]{2,1,0:T(8,128)(2,1)S(1)} %shard_map.84.rest_7_), channel_id=1, source_target_pairs={{0,4},{2,6},{4,0},{6,2},{8,12},{10,14},{12,8},{14,10},{1,5},{3,7},... | collective-permute-start | bytes 1572872 | tf_op jit(solution)/shard_map/ppermute | solution.py:473
  123.2 8.8 %collective-permute-done.18.rest_3_.came_ref = bf16[8,32,1024]{2,1,0:T(8,128)(2,1)S(1)} collective-permute-done((bf16[8,32,1024]{2,1,0:T(8,128)(2,1)S(1)}, bf16[8,32,1024]{2,1,0:T(8,128)(2,1)S(1)}, u32[]{:S(2)}, u32[]{:S(2)}) %collective-permute-start.18) | collective-permute-done | bytes 524320 | tf_op jit(solution)/shard_map/ppermute | solution.py:473
  132.0 1.2 shard_map.86.rest_6_
  134.0 3.7 %shard_map.87.token_ref.rest_9_ = f32[16,256]{1,0:T(8,128)S(1)} custom-call(s32[2]{0:T(128)S(1)} %pad_add_fusion.me_ref, s32[64]{0:T(128)S(1)} %shard_map.65.codes_ref, bf16[8,32,5504]{2,1,0:T(8,128)(2,1)S(1)} %copy-done.3, bf16[8,32,1024]{2,1,0:T(8,128)(2,1)S(1)} %collective-permute-done.13.came_ref.rest_2_, ...), custom_call_target="tpu_custom_call" | custom-call | bytes 1024 | tf_op jit(solution)/shard_map/pallas_call | solution.py:434
  139.7 5.7 %collective-permute-start.29 = (bf16[8,32,1024]{2,1,0:T(8,128)(2,1)S(1)}, bf16[8,32,1024]{2,1,0:T(8,128)(2,1)S(1)}, u32[]{:S(2)}, u32[]{:S(2)}) collective-permute-start(bf16[8,32,1024]{2,1,0:T(8,128)(2,1)S(1)} %shard_map.89.rest_4_), channel_id=1, source_target_pairs={{0,4},{2,6},{4,0},{6,2},{8,12},{10,14},{12,8},{14,10},{1,5},{3,7},... | collective-permute-start | bytes 1572872 | tf_op jit(solution)/shard_map/ppermute | solution.py:473
  145.4 1.2 shard_map.90.rest_6_
  146.7 1.7 collective-permute-start.28
  148.3 3.8 %shard_map.91.token_ref.rest_9_ = f32[16,256]{1,0:T(8,128)S(1)} custom-call(s32[2]{0:T(128)S(1)} %pad_add_fusion.me_ref, s32[64]{0:T(128)S(1)} %shard_map.65.codes_ref, bf16[8,32,5504]{2,1,0:T(8,128)(2,1)S(1)} %copy-done.3, bf16[8,32,1024]{2,1,0:T(8,128)(2,1)S(1)} %collective-permute-done.10.came_ref.rest_2_, ...), custom_call_target="tpu_custom_call" | custom-call | bytes 1024 | tf_op jit(solution)/shard_map/pallas_call | solution.py:434
  154.2 2.4 %collective-permute-done.29.rest_3_ = bf16[8,32,1024]{2,1,0:T(8,128)(2,1)S(1)} collective-permute-done((bf16[8,32,1024]{2,1,0:T(8,128)(2,1)S(1)}, bf16[8,32,1024]{2,1,0:T(8,128)(2,1)S(1)}, u32[]{:S(2)}, u32[]{:S(2)}) %collective-permute-start.29) | collective-permute-done | bytes 524320 | tf_op jit(solution)/shard_map/ppermute | solution.py:473
  156.5 1.2 shard_map.94.rest_6_
  157.7 1.3 collective-permute-start.32
  159.1 3.3 %collective-permute-start.33 = (bf16[8,32,768]{2,1,0:T(8,128)(2,1)S(1)}, bf16[8,32,768]{2,1,0:T(8,128)(2,1)S(1)}, u32[]{:S(2)}, u32[]{:S(2)}) collective-permute-start(bf16[8,32,768]{2,1,0:T(8,128)(2,1)S(1)} %shard_map.93.rest_4_), channel_id=1, source_target_pairs={{0,4},{2,6},{4,0},{6,2},{8,12},{10,14},{12,8},{14,10},{1,5},{3,7},... | collective-permute-start | bytes 1179656 | tf_op jit(solution)/shard_map/ppermute | solution.py:473
  162.4 3.7 %shard_map.95.rest_3_.rest_9_ = f32[16,256]{1,0:T(8,128)S(1)} custom-call(s32[2]{0:T(128)S(1)} %pad_add_fusion.me_ref, s32[64]{0:T(128)S(1)} %shard_map.65.codes_ref, bf16[8,32,5504]{2,1,0:T(8,128)(2,1)S(1)} %copy-done.3, bf16[8,32,1024]{2,1,0:T(8,128)(2,1)S(1)} %collective-permute-done.11.rest_4_.came_ref, ...), custom_call_target="tpu_custom_call" | custom-call | bytes 1024 | tf_op jit(solution)/shard_map/pallas_call | solution.py:434
  166.7 3.0 %collective-permute-start.31 = (bf16[8,32,640]{2,1,0:T(8,128)(2,1)S(1)}, bf16[8,32,640]{2,1,0:T(8,128)(2,1)S(1)}, u32[]{:S(2)}, u32[]{:S(2)}) collective-permute-start(bf16[8,32,640]{2,1,0:T(8,128)(2,1)S(1)} %shard_map.96.rest_4_), channel_id=1, source_target_pairs={{0,4},{2,6},{4,0},{6,2},{8,12},{10,14},{12,8},{14,10},{1,5},{3,7},... | collective-permute-start | bytes 983048 | tf_op jit(solution)/shard_map/ppermute | solution.py:473
  169.7 1.0 shard_map.97.rest_6_
  171.4 3.6 %shard_map.98.rest_4_.rest_9_ = f32[16,256]{1,0:T(8,128)S(1)} custom-call(s32[2]{0:T(128)S(1)} %pad_add_fusion.me_ref, s32[64]{0:T(128)S(1)} %shard_map.65.codes_ref, bf16[8,32,5504]{2,1,0:T(8,128)(2,1)S(1)} %copy-done.3, bf16[8,32,1024]{2,1,0:T(8,128)(2,1)S(1)} %collective-permute-done.16.rest_4_.came_ref, ...), custom_call_target="tpu_custom_call" | custom-call | bytes 1024 | tf_op jit(solution)/shard_map/pallas_call | solution.py:434
  176.9 1.2 collective-permute-start.34
  178.1 4.4 %collective-permute-done.35.rest_4_ = bf16[8,32,768]{2,1,0:T(8,128)(2,1)S(1)} collective-permute-done((bf16[8,32,768]{2,1,0:T(8,128)(2,1)S(1)}, bf16[8,32,768]{2,1,0:T(8,128)(2,1)S(1)}, u32[]{:S(2)}, u32[]{:S(2)}) %collective-permute-start.35) | collective-permute-done | bytes 393248 | tf_op jit(solution)/shard_map/ppermute | solution.py:473
  182.4 2.9 %shard_map.100.rest_6_.rest_9_ = f32[16,256]{1,0:T(8,128)S(1)} custom-call(s32[2]{0:T(128)S(1)} %pad_add_fusion.me_ref, s32[64]{0:T(128)S(1)} %shard_map.65.codes_ref, bf16[8,32,5504]{2,1,0:T(8,128)(2,1)S(1)} %copy-done.3, bf16[8,32,1024]{2,1,0:T(8,128)(2,1)S(1)} %collective-permute-done.21.rest_3_.came_ref, ...), custom_call_target="tpu_custom_call" | custom-call | bytes 1024 | tf_op jit(solution)/shard_map/pallas_call | solution.py:434
  185.3 1.6 collective-permute-done.34.rest_4_
  186.9 2.9 %shard_map.101 = f32[16,2,128]{2,1,0:T(2,128)S(1)} custom-call(s32[2]{0:T(128)S(1)} %pad_add_fusion.me_ref, s32[64]{0:T(128)S(1)} %shard_map.65.codes_ref, bf16[8,32,5504]{2,1,0:T(8,128)(2,1)S(1)} %copy-done.3, bf16[8,32,1024]{2,1,0:T(8,128)(2,1)S(1)} %collective-permute-done.18.rest_3_.came_ref, bf16[12,32,640]{2,1,0:T(8,128)(2,1)S(1)} %collective-permute-done.27.rest_0_, ...), custom_call_target="tpu_custom_call" | custom-call | bytes 1024 | tf_op jit(solution)/shard_map/pallas_call | solution.py:434
  189.8 10.3 %all_to_all.14.came_ref = f32[16,2,128]{2,1,0:T(2,128)S(1)} all-to-all(f32[16,2,128]{2,1,0:T(2,128)S(1)} %shard_map.101), channel_id=1, replica_groups=mesh['groups'=2,'docs'=8,'tensor'=2] {'docs','tensor'}, dimensions={0} | all-to-all | bytes 32768 | tf_op jit(solution)/shard_map/all_to_all | solution.py:578
  200.1 1.5 shard_map.102
  (83 shorter events, 26.1 us)
Async XLA Ops:
  0.8 0.7 copy-start.1
  1.5 25.8 %copy-start.8 = (bf16[8,32,2048]{2,1,0:T(8,128)(2,1)S(1)}, bf16[8,32,2048]{2,1,0:T(8,128)(2,1)}, u32[]{:S(2)}) copy-start(bf16[8,32,2048]{2,1,0:T(8,128)(2,1)} %own_ref.23) | copy-start | bytes 3145732
  1.5 26.4 %copy-start.2 = (bf16[8,32,5504]{2,1,0:T(8,128)(2,1)S(1)}, bf16[8,32,5504]{2,1,0:T(8,128)(2,1)}, u32[]{:S(2)}) copy-start(bf16[8,32,5504]{2,1,0:T(8,128)(2,1)} %own_ref.31) | copy-start | bytes 8454148
  4.6 21.3 %collective-permute-start.6 = (bf16[4,32,2048]{2,1,0:T(8,128)(2,1)S(1)}, bf16[4,32,2048]{2,1,0:T(8,128)(2,1)S(1)}, u32[]{:S(2)}, u32[]{:S(2)}) collective-permute-start(bf16[4,32,2048]{2,1,0:T(8,128)(2,1)S(1)} %get-tuple-element.47), channel_id=1, source_target_pairs={{4,8},{6,10},{8,4},{10,6},{5,9},{7,11},{9,5},{11,7},{20,24},{22,26... | collective-permute-start | bytes 1572872 | tf_op jit(solution)/shard_map/ppermute | solution.py:473
  5.3 21.9 %collective-permute-start.7 = (bf16[8,32,1024]{2,1,0:T(8,128)(2,1)S(1)}, bf16[8,32,1024]{2,1,0:T(8,128)(2,1)S(1)}, u32[]{:S(2)}, u32[]{:S(2)}) collective-permute-start(bf16[8,32,1024]{2,1,0:T(8,128)(2,1)S(1)} %get-tuple-element.48), channel_id=1, source_target_pairs={{0,4},{2,6},{4,0},{6,2},{8,12},{10,14},{12,8},{14,10},{1,5},{3,7},... | collective-permute-start | bytes 1572872 | tf_op jit(solution)/shard_map/ppermute | solution.py:473
  29.5 15.1 %collective-permute-start.9 = (bf16[8,32,1024]{2,1,0:T(8,128)(2,1)}, bf16[8,32,1024]{2,1,0:T(8,128)(2,1)S(1)}, u32[]{:S(2)}, u32[]{:S(2)}) collective-permute-start(bf16[8,32,1024]{2,1,0:T(8,128)(2,1)} %shard_map.68.token_ref), channel_id=1, source_target_pairs={{0,4},{2,6},{4,0},{6,2},{8,12},{10,14},{12,8},{14,10},{1,5},{3,7},... | collective-permute-start | bytes 1572872 | tf_op jit(solution)/shard_map/ppermute | solution.py:473
  30.9 15.3 %collective-permute-start.8 = (bf16[8,32,1024]{2,1,0:T(8,128)(2,1)S(1)}, bf16[8,32,1024]{2,1,0:T(8,128)(2,1)S(1)}, u32[]{:S(2)}, u32[]{:S(2)}) collective-permute-start(bf16[8,32,1024]{2,1,0:T(8,128)(2,1)S(1)} %shard_map.67.token_ref), channel_id=1, source_target_pairs={{4,8},{6,10},{8,4},{10,6},{5,9},{7,11},{9,5},{11,7},{20,24},{22,26... | collective-permute-start | bytes 1572872 | tf_op jit(solution)/shard_map/ppermute | solution.py:473
  33.2 22.7 %collective-permute-start.13 = (bf16[8,32,1024]{2,1,0:T(8,128)(2,1)}, bf16[8,32,1024]{2,1,0:T(8,128)(2,1)S(1)}, u32[]{:S(2)}, u32[]{:S(2)}) collective-permute-start(bf16[8,32,1024]{2,1,0:T(8,128)(2,1)} %shard_map.72), channel_id=1, source_target_pairs={{0,4},{2,6},{4,0},{6,2},{8,12},{10,14},{12,8},{14,10},{1,5},{3,7},... | collective-permute-start | bytes 1572872 | tf_op jit(solution)/shard_map/ppermute | solution.py:473
  40.7 5.5 %copy-start.11 = (bf16[4,32,2048]{2,1,0:T(8,128)(2,1)S(1)}, bf16[4,32,2048]{2,1,0:T(8,128)(2,1)}, u32[]{:S(2)}) copy-start(bf16[4,32,2048]{2,1,0:T(8,128)(2,1)} %get-tuple-element.50.token_ref.rest_2_) | copy-start | bytes 1572868
  45.3 7.7 %copy-start.3 = (bf16[8,32,5504]{2,1,0:T(8,128)(2,1)S(1)}, bf16[8,32,5504]{2,1,0:T(8,128)(2,1)}, u32[]{:S(2)}) copy-start(bf16[8,32,5504]{2,1,0:T(8,128)(2,1)} %own_ref.31) | copy-start | bytes 8454148
  45.3 16.9 %collective-permute-start.12 = (bf16[8,32,1024]{2,1,0:T(8,128)(2,1)S(1)}, bf16[8,32,1024]{2,1,0:T(8,128)(2,1)S(1)}, u32[]{:S(2)}, u32[]{:S(2)}) collective-permute-start(bf16[8,32,1024]{2,1,0:T(8,128)(2,1)S(1)} %shard_map.69.rest_4_), channel_id=1, source_target_pairs={{4,8},{6,10},{8,4},{10,6},{5,9},{7,11},{9,5},{11,7},{20,24},{22,26... | collective-permute-start | bytes 1572872 | tf_op jit(solution)/shard_map/ppermute | solution.py:473
  47.8 19.3 %collective-permute-start.11 = (bf16[8,32,1024]{2,1,0:T(8,128)(2,1)S(1)}, bf16[8,32,1024]{2,1,0:T(8,128)(2,1)S(1)}, u32[]{:S(2)}, u32[]{:S(2)}) collective-permute-start(bf16[8,32,1024]{2,1,0:T(8,128)(2,1)S(1)} %shard_map.70.token_ref), channel_id=1, source_target_pairs={{0,4},{2,6},{4,0},{6,2},{8,12},{10,14},{12,8},{14,10},{1,5},{3,7},... | collective-permute-start | bytes 1572872 | tf_op jit(solution)/shard_map/ppermute | solution.py:473
  56.5 10.6 %copy-start.9 = (bf16[8,32,2048]{2,1,0:T(8,128)(2,1)S(1)}, bf16[8,32,2048]{2,1,0:T(8,128)(2,1)}, u32[]{:S(2)}) copy-start(bf16[8,32,2048]{2,1,0:T(8,128)(2,1)} %own_ref.23) | copy-start | bytes 3145732
  56.6 23.2 %collective-permute-start.17 = (bf16[12,32,1024]{2,1,0:T(8,128)(2,1)S(1)}, bf16[12,32,1024]{2,1,0:T(8,128)(2,1)S(1)}, u32[]{:S(2)}, u32[]{:S(2)}) collective-permute-start(bf16[12,32,1024]{2,1,0:T(8,128)(2,1)S(1)} %shard_map.73.rest_4_), channel_id=1, source_target_pairs={{4,8},{6,10},{8,4},{10,6},{5,9},{7,11},{9,5},{11,7},{20,24},{22,26... | collective-permute-start | bytes 2359304 | tf_op jit(solution)/shard_map/ppermute | solution.py:473
  57.4 20.9 %collective-permute-start.10 = (bf16[8,32,1024]{2,1,0:T(8,128)(2,1)S(1)}, bf16[8,32,1024]{2,1,0:T(8,128)(2,1)S(1)}, u32[]{:S(2)}, u32[]{:S(2)}) collective-permute-start(bf16[8,32,1024]{2,1,0:T(8,128)(2,1)S(1)} %shard_map.71.token_ref), channel_id=1, source_target_pairs={{0,4},{2,6},{4,0},{6,2},{8,12},{10,14},{12,8},{14,10},{1,5},{3,7},... | collective-permute-start | bytes 1572872 | tf_op jit(solution)/shard_map/ppermute | solution.py:473
  63.0 23.9 %collective-permute-start.16 = (bf16[8,32,1024]{2,1,0:T(8,128)(2,1)S(1)}, bf16[8,32,1024]{2,1,0:T(8,128)(2,1)S(1)}, u32[]{:S(2)}, u32[]{:S(2)}) collective-permute-start(bf16[8,32,1024]{2,1,0:T(8,128)(2,1)S(1)} %shard_map.74.rest_5_), channel_id=1, source_target_pairs={{0,4},{2,6},{4,0},{6,2},{8,12},{10,14},{12,8},{14,10},{1,5},{3,7},... | collective-permute-start | bytes 1572872 | tf_op jit(solution)/shard_map/ppermute | solution.py:473
  68.3 11.4 %copy-start.7 = (bf16[4,32,5504]{2,1,0:T(8,128)(2,1)S(1)}, bf16[4,32,5504]{2,1,0:T(8,128)(2,1)}, u32[]{:S(2)}) copy-start(bf16[4,32,5504]{2,1,0:T(8,128)(2,1)} %get-tuple-element.51.rest_1_) | copy-start | bytes 4227076
  68.3 19.8 %collective-permute-start.15 = (bf16[8,32,1024]{2,1,0:T(8,128)(2,1)S(1)}, bf16[8,32,1024]{2,1,0:T(8,128)(2,1)S(1)}, u32[]{:S(2)}, u32[]{:S(2)}) collective-permute-start(bf16[8,32,1024]{2,1,0:T(8,128)(2,1)S(1)} %shard_map.75.token_ref), channel_id=1, source_target_pairs={{0,2},{2,0},{4,6},{6,4},{8,10},{10,8},{12,14},{14,12},{1,3},{3,1},... | collective-permute-start | bytes 1572872 | tf_op jit(solution)/shard_map/ppermute | solution.py:473
  79.0 19.4 %collective-permute-start.14 = (bf16[12,32,1024]{2,1,0:T(8,128)(2,1)S(1)}, bf16[12,32,1024]{2,1,0:T(8,128)(2,1)S(1)}, u32[]{:S(2)}, u32[]{:S(2)}) collective-permute-start(bf16[12,32,1024]{2,1,0:T(8,128)(2,1)S(1)} %shard_map.76.rest_3_), channel_id=1, source_target_pairs={{4,8},{6,10},{8,4},{10,6},{5,9},{7,11},{9,5},{11,7},{20,24},{22,26... | collective-permute-start | bytes 2359304 | tf_op jit(solution)/shard_map/ppermute | solution.py:473
  80.5 7.6 %copy-start = (bf16[1,768,2048]{2,1,0:T(8,128)(2,1)S(1)}, bf16[1,768,2048]{2,1,0:T(8,128)(2,1)}, u32[]{:S(2)}) copy-start(bf16[1,768,2048]{2,1,0:T(8,128)(2,1)} %rest_6_.3) | copy-start | bytes 9437188
  92.5 16.6 %collective-permute-start.20 = (bf16[12,32,1024]{2,1,0:T(8,128)(2,1)S(1)}, bf16[12,32,1024]{2,1,0:T(8,128)(2,1)S(1)}, u32[]{:S(2)}, u32[]{:S(2)}) collective-permute-start(bf16[12,32,1024]{2,1,0:T(8,128)(2,1)S(1)} %shard_map.80.rest_3_), channel_id=1, source_target_pairs={{4,8},{6,10},{8,4},{10,6},{5,9},{7,11},{9,5},{11,7},{20,24},{22,26... | collective-permute-start | bytes 2359304 | tf_op jit(solution)/shard_map/ppermute | solution.py:473
  93.2 14.0 %collective-permute-start.21 = (bf16[8,32,1024]{2,1,0:T(8,128)(2,1)S(1)}, bf16[8,32,1024]{2,1,0:T(8,128)(2,1)S(1)}, u32[]{:S(2)}, u32[]{:S(2)}) collective-permute-start(bf16[8,32,1024]{2,1,0:T(8,128)(2,1)S(1)} %shard_map.77.rest_5_), channel_id=1, source_target_pairs={{0,4},{2,6},{4,0},{6,2},{8,12},{10,14},{12,8},{14,10},{1,5},{3,7},... | collective-permute-start | bytes 1572872 | tf_op jit(solution)/shard_map/ppermute | solution.py:473
  97.9 11.8 %collective-permute-start.19 = (bf16[8,32,1024]{2,1,0:T(8,128)(2,1)S(1)}, bf16[8,32,1024]{2,1,0:T(8,128)(2,1)S(1)}, u32[]{:S(2)}, u32[]{:S(2)}) collective-permute-start(bf16[8,32,1024]{2,1,0:T(8,128)(2,1)S(1)} %shard_map.78.rest_7_), channel_id=1, source_target_pairs={{0,2},{2,0},{4,6},{6,4},{8,10},{10,8},{12,14},{14,12},{1,3},{3,1},... | collective-permute-start | bytes 1572872 | tf_op jit(solution)/shard_map/ppermute | solution.py:473
  109.7 24.3 %slice-start = ((s8[8454144]{0:T(1024)(128)(4,1)}), s8[4194304]{0:T(1024)(128)(4,1)S(1)}, s32[]{:S(2)}) async-start(s8[8454144]{0:T(1024)(128)(4,1)} %bitcast.4), calls=%async_computation.2 | async-start | bytes 8388608
  109.7 24.3 %slice-start.1 = ((s8[8454144]{0:T(1024)(128)(4,1)}), s8[4194304]{0:T(1024)(128)(4,1)S(1)}, s32[]{:S(2)}) async-start(s8[8454144]{0:T(1024)(128)(4,1)} %bitcast.4), calls=%async_computation.3 | async-start | bytes 8388608
  113.4 20.6 %slice-start.2 = ((s8[8454144]{0:T(1024)(128)(4,1)}), s8[65536]{0:T(1024)(128)(4,1)S(1)}, s32[]{:S(2)}) async-start(s8[8454144]{0:T(1024)(128)(4,1)} %bitcast.4), calls=%async_computation.4 | async-start | bytes 131072
  113.4 20.6 %collective-permute-start.26 = (f32[512,768]{1,0:T(8,128)S(1)}, f32[512,768]{1,0:T(8,128)S(1)}, u32[]{:S(2)}, u32[]{:S(2)}) collective-permute-start(f32[512,768]{1,0:T(8,128)S(1)} %shard_map.85.rest_4_.rest_7_), channel_id=1, source_target_pairs={{0,1},{1,0},{2,3},{3,2},{4,5},{5,4},{6,7},{7,6},{8,9},{9,8},{10,11... | collective-permute-start | bytes 4718600 | tf_op jit(solution)/shard_map/ppermute | solution.py:548
  113.5 18.5 %collective-permute-start.18 = (bf16[8,32,1024]{2,1,0:T(8,128)(2,1)S(1)}, bf16[8,32,1024]{2,1,0:T(8,128)(2,1)S(1)}, u32[]{:S(2)}, u32[]{:S(2)}) collective-permute-start(bf16[8,32,1024]{2,1,0:T(8,128)(2,1)S(1)} %shard_map.81.rest_4_), channel_id=1, source_target_pairs={{0,4},{2,6},{4,0},{6,2},{8,12},{10,14},{12,8},{14,10},{1,5},{3,7},... | collective-permute-start | bytes 1572872 | tf_op jit(solution)/shard_map/ppermute | solution.py:473
  119.2 19.9 %collective-permute-start.24 = (bf16[12,32,1024]{2,1,0:T(8,128)(2,1)S(1)}, bf16[12,32,1024]{2,1,0:T(8,128)(2,1)S(1)}, u32[]{:S(2)}, u32[]{:S(2)}) collective-permute-start(bf16[12,32,1024]{2,1,0:T(8,128)(2,1)S(1)} %shard_map.83.rest_3_), channel_id=1, source_target_pairs={{4,8},{6,10},{8,4},{10,6},{5,9},{7,11},{9,5},{11,7},{20,24},{22,26... | collective-permute-start | bytes 2359304 | tf_op jit(solution)/shard_map/ppermute | solution.py:473
  119.9 14.1 %collective-permute-start.25 = (bf16[8,32,1024]{2,1,0:T(8,128)(2,1)S(1)}, bf16[8,32,1024]{2,1,0:T(8,128)(2,1)S(1)}, u32[]{:S(2)}, u32[]{:S(2)}) collective-permute-start(bf16[8,32,1024]{2,1,0:T(8,128)(2,1)S(1)} %shard_map.82.token_ref), channel_id=1, source_target_pairs={{0,2},{2,0},{4,6},{6,4},{8,10},{10,8},{12,14},{14,12},{1,3},{3,1},... | collective-permute-start | bytes 1572872 | tf_op jit(solution)/shard_map/ppermute | solution.py:473
  120.4 25.0 %collective-permute-start.23 = (bf16[8,32,1024]{2,1,0:T(8,128)(2,1)S(1)}, bf16[8,32,1024]{2,1,0:T(8,128)(2,1)S(1)}, u32[]{:S(2)}, u32[]{:S(2)}) collective-permute-start(bf16[8,32,1024]{2,1,0:T(8,128)(2,1)S(1)} %shard_map.84.rest_7_), channel_id=1, source_target_pairs={{0,4},{2,6},{4,0},{6,2},{8,12},{10,14},{12,8},{14,10},{1,5},{3,7},... | collective-permute-start | bytes 1572872 | tf_op jit(solution)/shard_map/ppermute | solution.py:473
  133.2 15.1 %collective-permute-start.22 = (bf16[8,32,1024]{2,1,0:T(8,128)(2,1)S(1)}, bf16[8,32,1024]{2,1,0:T(8,128)(2,1)S(1)}, u32[]{:S(2)}, u32[]{:S(2)}) collective-permute-start(bf16[8,32,1024]{2,1,0:T(8,128)(2,1)S(1)} %shard_map.86.rest_6_), channel_id=1, source_target_pairs={{0,2},{2,0},{4,6},{6,4},{8,10},{10,8},{12,14},{14,12},{1,3},{3,1},... | collective-permute-start | bytes 1572872 | tf_op jit(solution)/shard_map/ppermute | solution.py:473
  138.4 15.2 %collective-permute-start.30 = (bf16[12,32,768]{2,1,0:T(8,128)(2,1)S(1)}, bf16[12,32,768]{2,1,0:T(8,128)(2,1)S(1)}, u32[]{:S(2)}, u32[]{:S(2)}) collective-permute-start(bf16[12,32,768]{2,1,0:T(8,128)(2,1)S(1)} %shard_map.88.rest_3_), channel_id=1, source_target_pairs={{4,8},{6,10},{8,4},{10,6},{5,9},{7,11},{9,5},{11,7},{20,24},{22,26... | collective-permute-start | bytes 1769480 | tf_op jit(solution)/shard_map/ppermute | solution.py:473
  139.7 16.8 %collective-permute-start.29 = (bf16[8,32,1024]{2,1,0:T(8,128)(2,1)S(1)}, bf16[8,32,1024]{2,1,0:T(8,128)(2,1)S(1)}, u32[]{:S(2)}, u32[]{:S(2)}) collective-permute-start(bf16[8,32,1024]{2,1,0:T(8,128)(2,1)S(1)} %shard_map.89.rest_4_), channel_id=1, source_target_pairs={{0,4},{2,6},{4,0},{6,2},{8,12},{10,14},{12,8},{14,10},{1,5},{3,7},... | collective-permute-start | bytes 1572872 | tf_op jit(solution)/shard_map/ppermute | solution.py:473
  146.7 15.7 %collective-permute-start.28 = (bf16[8,32,1024]{2,1,0:T(8,128)(2,1)S(1)}, bf16[8,32,1024]{2,1,0:T(8,128)(2,1)S(1)}, u32[]{:S(2)}, u32[]{:S(2)}) collective-permute-start(bf16[8,32,1024]{2,1,0:T(8,128)(2,1)S(1)} %shard_map.90.rest_6_), channel_id=1, source_target_pairs={{0,2},{2,0},{4,6},{6,4},{8,10},{10,8},{12,14},{14,12},{1,3},{3,1},... | collective-permute-start | bytes 1572872 | tf_op jit(solution)/shard_map/ppermute | solution.py:473
  152.8 13.2 %collective-permute-start.27 = (bf16[12,32,640]{2,1,0:T(8,128)(2,1)S(1)}, bf16[12,32,640]{2,1,0:T(8,128)(2,1)S(1)}, u32[]{:S(2)}, u32[]{:S(2)}) collective-permute-start(bf16[12,32,640]{2,1,0:T(8,128)(2,1)S(1)} %shard_map.92.rest_3_), channel_id=1, source_target_pairs={{4,8},{6,10},{8,4},{10,6},{5,9},{7,11},{9,5},{11,7},{20,24},{22,26... | collective-permute-start | bytes 1474568 | tf_op jit(solution)/shard_map/ppermute | solution.py:473
  157.7 13.7 %collective-permute-start.32 = (bf16[8,32,1024]{2,1,0:T(8,128)(2,1)S(1)}, bf16[8,32,1024]{2,1,0:T(8,128)(2,1)S(1)}, u32[]{:S(2)}, u32[]{:S(2)}) collective-permute-start(bf16[8,32,1024]{2,1,0:T(8,128)(2,1)S(1)} %shard_map.94.rest_6_), channel_id=1, source_target_pairs={{0,2},{2,0},{4,6},{6,4},{8,10},{10,8},{12,14},{14,12},{1,3},{3,1},... | collective-permute-start | bytes 1572872 | tf_op jit(solution)/shard_map/ppermute | solution.py:473
  159.1 10.7 %collective-permute-start.33 = (bf16[8,32,768]{2,1,0:T(8,128)(2,1)S(1)}, bf16[8,32,768]{2,1,0:T(8,128)(2,1)S(1)}, u32[]{:S(2)}, u32[]{:S(2)}) collective-permute-start(bf16[8,32,768]{2,1,0:T(8,128)(2,1)S(1)} %shard_map.93.rest_4_), channel_id=1, source_target_pairs={{0,4},{2,6},{4,0},{6,2},{8,12},{10,14},{12,8},{14,10},{1,5},{3,7},... | collective-permute-start | bytes 1179656 | tf_op jit(solution)/shard_map/ppermute | solution.py:473
  166.7 9.3 %collective-permute-start.31 = (bf16[8,32,640]{2,1,0:T(8,128)(2,1)S(1)}, bf16[8,32,640]{2,1,0:T(8,128)(2,1)S(1)}, u32[]{:S(2)}, u32[]{:S(2)}) collective-permute-start(bf16[8,32,640]{2,1,0:T(8,128)(2,1)S(1)} %shard_map.96.rest_4_), channel_id=1, source_target_pairs={{0,4},{2,6},{4,0},{6,2},{8,12},{10,14},{12,8},{14,10},{1,5},{3,7},... | collective-permute-start | bytes 983048 | tf_op jit(solution)/shard_map/ppermute | solution.py:473
  170.7 11.7 %collective-permute-start.35 = (bf16[8,32,768]{2,1,0:T(8,128)(2,1)S(1)}, bf16[8,32,768]{2,1,0:T(8,128)(2,1)S(1)}, u32[]{:S(2)}, u32[]{:S(2)}) collective-permute-start(bf16[8,32,768]{2,1,0:T(8,128)(2,1)S(1)} %shard_map.97.rest_6_), channel_id=1, source_target_pairs={{0,2},{2,0},{4,6},{6,4},{8,10},{10,8},{12,14},{14,12},{1,3},{3,1},... | collective-permute-start | bytes 1179656 | tf_op jit(solution)/shard_map/ppermute | solution.py:473
  176.9 10.0 %collective-permute-start.34 = (bf16[8,32,640]{2,1,0:T(8,128)(2,1)S(1)}, bf16[8,32,640]{2,1,0:T(8,128)(2,1)S(1)}, u32[]{:S(2)}, u32[]{:S(2)}) collective-permute-start(bf16[8,32,640]{2,1,0:T(8,128)(2,1)S(1)} %shard_map.99.rest_6_), channel_id=1, source_target_pairs={{0,2},{2,0},{4,6},{6,4},{8,10},{10,8},{12,14},{14,12},{1,3},{3,1},... | collective-permute-start | bytes 983048 | tf_op jit(solution)/shard_map/ppermute | solution.py:473
